TPU v7x, 32 devices: a whole 2x2x4 slice. The times are simulated.
32 devices in a mesh: section: 4 (over z), tensor: 8 (over y, x, core).
Axes of the slice: x: 2, y: 2, z: 4, core: 2. Of those that a mesh axis runs over, the one named last changes fastest.
Arguments:
- acts_prev: bfloat16 [2048, 8192], P('section', 'tensor'), may hold values from -6 to 6
- embedded: bfloat16 [512, 8192], P(None, 'tensor'), may hold values from -6 to 6
- grads_next: bfloat16 [2048, 8192], P('section', 'tensor'), may hold values from -1.5 to 1.5
- loss_grad: bfloat16 [512, 8192], P(None, 'tensor'), may hold values from -1.5 to 1.5
- up_weight: bfloat16 [4, 2, 256, 32768], P('section', None, None, 'tensor'), may hold values from -0.25 to 0.25
- down_weight: bfloat16 [4, 2, 32768, 256], P('section', None, 'tensor'), may hold values from -0.125 to 0.125
Outputs:
- mixed: bfloat16 [2048, 8192], P('section', 'tensor')
- input_grads: bfloat16 [2048, 8192], P('section', 'tensor')
- up_grad: bfloat16 [4, 2, 256, 32768], P('section', None, None, 'tensor')
- down_grad: bfloat16 [4, 2, 32768, 256], P('section', None, 'tensor')
All inputs are finite; a program needn't handle non-finite values.
Results may differ from a plain program's by a relative error of at most 0.005.
Values may be sent and summed in bfloat16 or wider, within the bound.
No kernel may reach another device: no remote copies, remote signals or barrier semaphores. Data moves between devices by JAX's collectives and lax.ppermute only.
A program may use at most 64 MiB of HBM per device.

v0:
```python
import jax
import jax.numpy as jnp
from jax import lax
from jax.sharding import PartitionSpec as P


def from_behind(value, axis, by):
    length = lax.axis_size(axis)
    pairs = [(i, i + by) for i in range(length) if 0 <= i + by < length]
    return lax.ppermute(value, axis, pairs)


def swapped(value, axis, distance):
    mask = 2**distance
    pairs = [(source, source ^ mask) for source in range(lax.axis_size(axis))]
    return lax.ppermute(value, axis, pairs)


def gelu_tanh(values):
    return jax.nn.gelu(values, approximate=True)


def on_device(acts_prev, embedded, grads_next, loss_grad, up_weight, down_weight):
    sections = lax.axis_size("section")
    section_idx = lax.axis_index("section")
    received = from_behind(acts_prev, "section", 1)
    inputs = jnp.where(section_idx == 0, embedded, received)
    returned = from_behind(grads_next, "section", -1)
    cotangent = jnp.where(section_idx == sections - 1, loss_grad, returned)
    up_local = up_weight[0]
    down_local = down_weight[0]
    factors = up_local.shape[0]
    levels = factors - 1
    block_width = up_local.shape[1]
    tokens = inputs.shape[0]
    model_local = inputs.shape[1] // block_width
    hidden_local = up_local.shape[2] // block_width
    expand = hidden_local // model_local
    top_bit = lax.axis_size("tensor").bit_length() - 1
    first_bit = top_bit - levels
    position = 0
    got_inputs, got_grads = swapped((inputs, cotangent), "tensor", first_bit + position)
    their_inputs = [got_inputs]
    their_grads = [got_grads]
    up_shaped = up_local.reshape(factors, block_width, model_local, expand, block_width)
    down_shaped = down_local.reshape(factors, model_local, expand, block_width, block_width)
    stacked_inputs = jnp.stack([inputs] + their_inputs).reshape(
        factors, tokens, model_local, block_width
    )
    pre_act = jnp.einsum(
        "ktmp,kpmeq->tmeq", stacked_inputs, up_shaped, preferred_element_type=jnp.float32
    )
    hidden = gelu_tanh(pre_act).astype(jnp.bfloat16)
    partial_out = jnp.einsum(
        "tmep,kmepq->ktmq", hidden, down_shaped, preferred_element_type=jnp.float32
    )
    out_sum = partial_out[0]
    position = 0
    arrived = swapped(
        partial_out[1 + position].astype(jnp.bfloat16), "tensor", first_bit + position
    )
    out_sum = out_sum + arrived.astype(jnp.float32)
    stacked_grads = jnp.stack([cotangent] + their_grads).reshape(
        factors, tokens, model_local, block_width
    )
    grad_hidden = jnp.einsum(
        "ktmq,kmepq->tmep", stacked_grads, down_shaped, preferred_element_type=jnp.float32
    )
    down_grad_bits = jnp.einsum(
        "tmep,ktmq->kmepq", hidden, stacked_grads, preferred_element_type=jnp.float32
    )
    pullback = jax.vjp(gelu_tanh, pre_act)[1]
    grad_pre = pullback(grad_hidden)[0].astype(jnp.bfloat16)
    up_grad_bits = jnp.einsum(
        "ktmp,tmeq->kpmeq", stacked_inputs, grad_pre, preferred_element_type=jnp.float32
    )
    partial_back = jnp.einsum(
        "tmeq,kpmeq->ktmp", grad_pre, up_shaped, preferred_element_type=jnp.float32
    )
    back_sum = partial_back[0]
    position = 0
    arrived = swapped(
        partial_back[1 + position].astype(jnp.bfloat16), "tensor", first_bit + position
    )
    back_sum = back_sum + arrived.astype(jnp.float32)
    mixed = (
        inputs.astype(jnp.float32) + out_sum.reshape(tokens, model_local * block_width)
    ).astype(jnp.bfloat16)
    input_grads = (
        cotangent.astype(jnp.float32) + back_sum.reshape(tokens, model_local * block_width)
    ).astype(jnp.bfloat16)
    up_grad = up_grad_bits.reshape(factors, block_width, hidden_local * block_width).astype(
        jnp.bfloat16
    )[None]
    down_grad = down_grad_bits.reshape(factors, hidden_local * block_width, block_width).astype(
        jnp.bfloat16
    )[None]
    return (mixed, input_grads, up_grad, down_grad)


def solution(mesh):
    in_specs = (
        P("section", "tensor"),
        P(None, "tensor"),
        P("section", "tensor"),
        P(None, "tensor"),
        P("section", None, None, "tensor"),
        P("section", None, "tensor", None),
    )
    out_specs = (
        P("section", "tensor"),
        P("section", "tensor"),
        P("section", None, None, "tensor"),
        P("section", None, "tensor", None),
    )
    return jax.shard_map(
        on_device, mesh=mesh, in_specs=in_specs, out_specs=out_specs, check_vma=False
    )
```

profile of v0, /device:TPU:0, one launch (start us, length us, event | category | flops | bytes accessed | tf_op | source)
XLA Modules:
  0.0 161.9 jit_solution(3389482266775919508)
XLA Ops:
  0.6 0.0 copy-start.4
  0.6 2.4 %copy.27 = bf16[512,1024]{0,1:T(8,128)(2,1)} copy(bf16[512,1024]{1,0:T(8,128)(2,1)} %param.8) | data formatting | bytes 2097152 | tf_op args[2]
  3.0 1.3 collective-permute-start.3
  4.3 2.3 %copy.20 = bf16[512,1024]{0,1:T(8,128)(2,1)} copy(bf16[512,1024]{1,0:T(8,128)(2,1)} %param.6) | data formatting | bytes 2097152 | tf_op args[0]
  6.6 6.5 %collective-permute-start = (bf16[512,1024]{0,1:T(8,128)(2,1)}, bf16[512,1024]{0,1:T(8,128)(2,1)}, u32[]{:S(2)}, u32[]{:S(2)}) collective-permute-start(bf16[512,1024]{0,1:T(8,128)(2,1)} %copy.20), channel_id=1, source_target_pairs={{0,8},{8,16},{16,24},{1,9},{9,17},{17,25},{2,10},{10,18},{18,26},{... | collective-permute-start | bytes 3145736 | tf_op jit(solution)/shard_map/ppermute | solution.py:10
  13.1 0.0 copy-done.4
  13.1 0.5 copy.21
  13.6 1.5 copy.28
  15.2 16.2 %collective-permute-done.3 = bf16[512,1024]{0,1:T(8,128)(2,1)} collective-permute-done((bf16[512,1024]{0,1:T(8,128)(2,1)}, bf16[512,1024]{0,1:T(8,128)(2,1)}, u32[]{:S(2)}, u32[]{:S(2)}) %collective-permute-start.3) | collective-permute-done | bytes 1048608 | tf_op jit(solution)/shard_map/ppermute | solution.py:10
  31.4 1.3 broadcast_select_fusion
  32.7 1.7 %collective-permute-start.4 = (bf16[512,1024]{0,1:T(8,128)(2,1)S(1)}, bf16[512,1024]{0,1:T(8,128)(2,1)}, u32[]{:S(2)}, u32[]{:S(2)}) collective-permute-start(bf16[512,1024]{0,1:T(8,128)(2,1)S(1)} %broadcast_select_fusion), channel_id=1, source_target_pairs={{0,4},{1,5},{2,6},{3,7},{4,0},{5,1},{6,2},{7,3},{8,12},{9,13},{10,... | collective-permute-start | bytes 3145736 | tf_op jit(solution)/shard_map/ppermute | solution.py:16
  34.5 0.4 collective-permute-done
  34.8 0.1 broadcast_select_fusion.1
  35.0 1.7 %collective-permute-start.1 = (bf16[512,1024]{0,1:T(8,128)(2,1)S(1)}, bf16[512,1024]{0,1:T(8,128)(2,1)}, u32[]{:S(2)}, u32[]{:S(2)}) collective-permute-start(bf16[512,1024]{0,1:T(8,128)(2,1)S(1)} %broadcast_select_fusion.1), channel_id=1, source_target_pairs={{0,4},{1,5},{2,6},{3,7},{4,0},{5,1},{6,2},{7,3},{8,12},{9,13},{10,... | collective-permute-start | bytes 3145736 | tf_op jit(solution)/shard_map/ppermute | solution.py:16
  36.7 7.8 %reshape_squeeze.6 = bf16[2,256,4,4,256]{4,3,2,1,0:T(4,128)(2,1)} reshape(bf16[1,2,256,4096]{3,2,1,0:T(8,128)(2,1)} %param.10) | data formatting | bytes 8388608 | tf_op jit(solution)/shard_map/reshape;squeeze | solution.py:45
  44.5 1.3 copy.29
  45.8 0.5 copy.22
  46.3 12.7 %collective-permute-done.4 = bf16[512,1024]{0,1:T(8,128)(2,1)} collective-permute-done((bf16[512,1024]{0,1:T(8,128)(2,1)S(1)}, bf16[512,1024]{0,1:T(8,128)(2,1)}, u32[]{:S(2)}, u32[]{:S(2)}) %collective-permute-start.4) | collective-permute-done | bytes 1048608 | tf_op jit(solution)/shard_map/ppermute | solution.py:16
  59.0 2.3 %copy.30 = bf16[1,512,4,256]{3,1,0,2:T(8,128)(2,1)} copy(bf16[1,512,4,256]{1,3,2,0:T(8,128)(2,1)} %bitcast.19) | data formatting | bytes 2097152 | tf_op jit(solution)/shard_map/stack | solution.py:63
  61.3 18.5 %collective-permute-done.1 = bf16[512,1024]{0,1:T(8,128)(2,1)} collective-permute-done((bf16[512,1024]{0,1:T(8,128)(2,1)S(1)}, bf16[512,1024]{0,1:T(8,128)(2,1)}, u32[]{:S(2)}, u32[]{:S(2)}) %collective-permute-start.1) | collective-permute-done | bytes 1048608 | tf_op jit(solution)/shard_map/ppermute | solution.py:16
  79.7 2.3 %copy.23 = bf16[1,512,4,256]{3,1,0,2:T(8,128)(2,1)} copy(bf16[1,512,4,256]{1,3,2,0:T(8,128)(2,1)} %bitcast.1) | data formatting | bytes 2097152 | tf_op jit(solution)/shard_map/stack | solution.py:47
  82.0 5.0 %fusion.23 = f32[4,512,4,256,1]{3,1,4,2,0:T(8,128)S(1)} fusion(bf16[2,256,4,4,256]{4,3,2,1,0:T(4,128)(2,1)} %reshape_squeeze.6, bf16[1,512,4,256]{3,1,0,2:T(8,128)(2,1)} %copy.23, bf16[1,512,4,256]{3,1,0,2:T(8,128)(2,1)S(1)} %copy.22), kind=kOutput, calls=%fused_computation.28 | convolution fusion | flops 2151677952 | bytes 14680064 | tf_op jit(solution)/shard_map/ktmp,kpmeq->tmeq/dot_general | solution.py:50
  87.0 0.0 copy-start.5
  87.0 0.0 copy-start.6
  87.0 7.9 %fusion.31 = f32[2,512,4,256]{1,3,0,2:T(8,128)} fusion(bf16[2,4,4,256,256]{4,3,2,1,0:T(8,128)(2,1)} %bitcast.132, f32[4,512,4,256,1]{3,1,4,2,0:T(8,128)S(1)} %fusion.23), kind=kOutput, calls=%fused_computation.32 | convolution fusion | flops 2166358016 | bytes 16777216 | tf_op jit(solution)/shard_map/tmep,kmepq->ktmq/dot_general | solution.py:54
  94.9 0.0 copy-done.5
  94.9 0.0 copy-done.6
  94.9 9.4 %fusion.6 = bf16[512,4,4,256]{3,0,2,1:T(8,128)(2,1)} fusion(f32[4,512,4,256,1]{3,1,4,2,0:T(8,128)S(1)} %fusion.23, bf16[2,4,4,256,256]{4,3,2,1,0:T(8,128)(2,1)} %bitcast.133, bf16[1,512,4,256]{3,1,0,2:T(8,128)(2,1)S(1)} %copy-done.6, bf16[1,512,4,256]{3,1,0,2:T(8,128)(2,1)S(1)} %copy-done.5), kind=kOutput, calls=%fused_computation.8 | convolution fusion | flops 2193620992 | bytes 18874368 | tf_op jit(solution)/shard_map/ktmq,kmepq->tmep/dot_general | solution.py:66
  104.3 4.8 %convert_bitcast_fusion = bf16[2,4,4,256,256]{4,3,2,0,1:T(8,128)(2,1)} fusion(bf16[1,512,4,256]{3,1,0,2:T(8,128)(2,1)S(1)} %copy-done.6, bf16[1,512,4,256]{3,1,0,2:T(8,128)(2,1)S(1)} %copy-done.5, f32[4,512,4,256,1]{3,1,4,2,0:T(8,128)S(1)} %fusion.23), kind=kOutput, calls=%fused_computation.30 | convolution fusion | flops 2172649472 | bytes 14680064 | tf_op jit(solution)/shard_map/tmep,ktmq->kmepq/dot_general | solution.py:69
  109.1 2.7 %fusion.47 = bf16[512,4,256]{0,2,1:T(8,128)(2,1)} fusion(f32[2,512,4,256]{1,3,0,2:T(8,128)} %fusion.31), kind=kLoop, calls=%fused_computation.48 | loop fusion | bytes 2097152 | tf_op jit(solution)/shard_map/convert_element_type | solution.py:60
  111.8 1.4 collective-permute-start.2
  113.2 0.0 copy-done
  113.2 5.1 %fusion.36 = f32[2,512,4,256]{1,3,0,2:T(8,128)S(1)} fusion(bf16[2,256,4,4,256]{4,3,2,1,0:T(4,128)(2,1)S(1)} %copy-done, bf16[512,4,4,256]{3,0,2,1:T(8,128)(2,1)} %fusion.6), kind=kOutput, calls=%fused_computation.33 | convolution fusion | flops 2147483648 | bytes 12582912 | tf_op jit(solution)/shard_map/tmeq,kpmeq->ktmp/dot_general | solution.py:77
  118.3 1.2 fusion.48
  119.5 0.8 collective-permute-start.5
  120.3 0.0 copy-done.1
  120.3 2.4 %convert_bitcast_fusion.1 = bf16[2,256,4,4,256]{1,4,0,3,2:T(8,128)(2,1)S(1)} fusion(bf16[512,4,4,256]{3,0,2,1:T(8,128)(2,1)S(1)} %copy-done.7, bf16[1,512,4,256]{3,1,0,2:T(8,128)(2,1)S(1)} %copy-done.1, bf16[1,512,4,256]{3,1,0,2:T(8,128)(2,1)S(1)} %copy.22), kind=kOutput, calls=%fused_computation.31 | convolution fusion | flops 2153775104 | bytes 10485760 | tf_op jit(solution)/shard_map/ktmp,tmeq->kpmeq/dot_general | solution.py:74
  122.7 2.3 %copy.35 = bf16[2,256,4,4,256]{1,4,3,2,0:T(8,128)(2,1)} copy(bf16[2,256,4,4,256]{1,4,0,3,2:T(8,128)(2,1)S(1)} %convert_bitcast_fusion.1) | data formatting | bytes 8388608 | tf_op jit(solution)/shard_map/convert_element_type | solution.py:92
  125.0 6.3 %copy.40 = bf16[1,2,256,4096]{3,2,1,0:T(8,128)(2,1)} copy(bf16[1,2,256,4096]{2,3,1,0:T(8,128)(2,1)} %bitcast.128) | data formatting | bytes 8388608
  131.3 4.8 %copy.37 = bf16[2,4,4,256,256]{4,3,2,1,0:T(8,128)(2,1)} copy(bf16[2,4,4,256,256]{4,3,2,0,1:T(8,128)(2,1)} %convert_bitcast_fusion) | data formatting | bytes 8388608 | tf_op jit(solution)/shard_map/convert_element_type | solution.py:95
  136.1 2.1 %collective-permute-done.2 = bf16[512,4,256]{0,2,1:T(8,128)(2,1)} collective-permute-done((bf16[512,4,256]{0,2,1:T(8,128)(2,1)}, bf16[512,4,256]{0,2,1:T(8,128)(2,1)}, u32[]{:S(2)}, u32[]{:S(2)}) %collective-permute-start.2) | collective-permute-done | bytes 1048608 | tf_op jit(solution)/shard_map/ppermute | solution.py:16
  138.2 1.6 fusion.42
  139.8 0.4 fusion.46
  140.2 1.3 copy.38
  141.5 16.5 %collective-permute-done.5 = bf16[512,4,256]{0,2,1:T(8,128)(2,1)} collective-permute-done((bf16[512,4,256]{0,2,1:T(8,128)(2,1)}, bf16[512,4,256]{0,2,1:T(8,128)(2,1)}, u32[]{:S(2)}, u32[]{:S(2)}) %collective-permute-start.5) | collective-permute-done | bytes 1048608 | tf_op jit(solution)/shard_map/ppermute | solution.py:16
  158.0 2.2 %fusion.41 = f32[512,4,256]{0,2,1:T(8,128)S(1)} fusion(f32[2,512,4,256]{1,3,0,2:T(8,128)} %copy-done.2, bf16[512,4,256]{0,2,1:T(8,128)(2,1)} %collective-permute-done.5), kind=kLoop, calls=%fused_computation.36 | loop fusion | flops 1048576 | bytes 5242880 | tf_op jit(solution)/shard_map/add | solution.py:85
  160.2 0.4 fusion.45
  160.6 1.3 copy.39
  (8 shorter events, 0.0 us)
Async XLA Ops:
  0.6 12.5 %copy-start.4 = (bf16[512,1024]{1,0:T(8,128)(2,1)S(1)}, bf16[512,1024]{1,0:T(8,128)(2,1)}, u32[]{:S(2)}) copy-start(bf16[512,1024]{1,0:T(8,128)(2,1)} %param.7) | copy-start | bytes 3145732
  3.0 28.4 %collective-permute-start.3 = (bf16[512,1024]{0,1:T(8,128)(2,1)}, bf16[512,1024]{0,1:T(8,128)(2,1)}, u32[]{:S(2)}, u32[]{:S(2)}) collective-permute-start(bf16[512,1024]{0,1:T(8,128)(2,1)} %copy.27), channel_id=1, source_target_pairs={{8,0},{16,8},{24,16},{9,1},{17,9},{25,17},{10,2},{18,10},{26,18},{... | collective-permute-start | bytes 3145736 | tf_op jit(solution)/shard_map/ppermute | solution.py:10
  6.6 28.3 %collective-permute-start = (bf16[512,1024]{0,1:T(8,128)(2,1)}, bf16[512,1024]{0,1:T(8,128)(2,1)}, u32[]{:S(2)}, u32[]{:S(2)}) collective-permute-start(bf16[512,1024]{0,1:T(8,128)(2,1)} %copy.20), channel_id=1, source_target_pairs={{0,8},{8,16},{16,24},{1,9},{9,17},{17,25},{2,10},{10,18},{18,26},{... | collective-permute-start | bytes 3145736 | tf_op jit(solution)/shard_map/ppermute | solution.py:10
  32.7 26.3 %collective-permute-start.4 = (bf16[512,1024]{0,1:T(8,128)(2,1)S(1)}, bf16[512,1024]{0,1:T(8,128)(2,1)}, u32[]{:S(2)}, u32[]{:S(2)}) collective-permute-start(bf16[512,1024]{0,1:T(8,128)(2,1)S(1)} %broadcast_select_fusion), channel_id=1, source_target_pairs={{0,4},{1,5},{2,6},{3,7},{4,0},{5,1},{6,2},{7,3},{8,12},{9,13},{10,... | collective-permute-start | bytes 3145736 | tf_op jit(solution)/shard_map/ppermute | solution.py:16
  35.0 44.8 %collective-permute-start.1 = (bf16[512,1024]{0,1:T(8,128)(2,1)S(1)}, bf16[512,1024]{0,1:T(8,128)(2,1)}, u32[]{:S(2)}, u32[]{:S(2)}) collective-permute-start(bf16[512,1024]{0,1:T(8,128)(2,1)S(1)} %broadcast_select_fusion.1), channel_id=1, source_target_pairs={{0,4},{1,5},{2,6},{3,7},{4,0},{5,1},{6,2},{7,3},{8,12},{9,13},{10,... | collective-permute-start | bytes 3145736 | tf_op jit(solution)/shard_map/ppermute | solution.py:16
  87.0 7.9 %copy-start.5 = (bf16[1,512,4,256]{3,1,0,2:T(8,128)(2,1)S(1)}, bf16[1,512,4,256]{3,1,0,2:T(8,128)(2,1)}, u32[]{:S(2)}) copy-start(bf16[1,512,4,256]{3,1,0,2:T(8,128)(2,1)} %copy.29) | copy-start | bytes 3145732
  87.0 7.9 %copy-start.6 = (bf16[1,512,4,256]{3,1,0,2:T(8,128)(2,1)S(1)}, bf16[1,512,4,256]{3,1,0,2:T(8,128)(2,1)}, u32[]{:S(2)}) copy-start(bf16[1,512,4,256]{3,1,0,2:T(8,128)(2,1)} %copy.30) | copy-start | bytes 3145732
  104.3 8.9 %copy-start = (bf16[2,256,4,4,256]{4,3,2,1,0:T(4,128)(2,1)S(1)}, bf16[2,256,4,4,256]{4,3,2,1,0:T(4,128)(2,1)}, u32[]{:S(2)}) copy-start(bf16[2,256,4,4,256]{4,3,2,1,0:T(4,128)(2,1)} %reshape_squeeze.6) | copy-start | bytes 12582916
  111.8 8.5 %copy-start.1 = (bf16[1,512,4,256]{3,1,0,2:T(8,128)(2,1)S(1)}, bf16[1,512,4,256]{3,1,0,2:T(8,128)(2,1)}, u32[]{:S(2)}) copy-start(bf16[1,512,4,256]{3,1,0,2:T(8,128)(2,1)} %copy.23) | copy-start | bytes 3145732
  111.8 8.5 %copy-start.7 = (bf16[512,4,4,256]{3,0,2,1:T(8,128)(2,1)S(1)}, bf16[512,4,4,256]{3,0,2,1:T(8,128)(2,1)}, u32[]{:S(2)}) copy-start(bf16[512,4,4,256]{3,0,2,1:T(8,128)(2,1)} %fusion.6) | copy-start | bytes 12582916
  111.8 26.4 %collective-permute-start.2 = (bf16[512,4,256]{0,2,1:T(8,128)(2,1)}, bf16[512,4,256]{0,2,1:T(8,128)(2,1)}, u32[]{:S(2)}, u32[]{:S(2)}) collective-permute-start(bf16[512,4,256]{0,2,1:T(8,128)(2,1)} %fusion.47), channel_id=1, source_target_pairs={{0,4},{1,5},{2,6},{3,7},{4,0},{5,1},{6,2},{7,3},{8,12},{9,13},{10,... | collective-permute-start | bytes 3145736 | tf_op jit(solution)/shard_map/ppermute | solution.py:16
  118.3 4.4 %copy-start.2 = (f32[2,512,4,256]{1,3,0,2:T(8,128)}, f32[2,512,4,256]{1,3,0,2:T(8,128)S(1)}, u32[]{:S(2)}) copy-start(f32[2,512,4,256]{1,3,0,2:T(8,128)S(1)} %fusion.36) | copy-start | bytes 12582916
  119.5 38.5 %collective-permute-start.5 = (bf16[512,4,256]{0,2,1:T(8,128)(2,1)}, bf16[512,4,256]{0,2,1:T(8,128)(2,1)}, u32[]{:S(2)}, u32[]{:S(2)}) collective-permute-start(bf16[512,4,256]{0,2,1:T(8,128)(2,1)} %fusion.48), channel_id=1, source_target_pairs={{0,4},{1,5},{2,6},{3,7},{4,0},{5,1},{6,2},{7,3},{8,12},{9,13},{10,... | collective-permute-start | bytes 3145736 | tf_op jit(solution)/shard_map/ppermute | solution.py:16
  131.3 6.9 %copy-start.3 = (f32[2,512,4,256]{1,3,0,2:T(8,128)S(1)}, f32[2,512,4,256]{1,3,0,2:T(8,128)}, u32[]{:S(2)}) copy-start(f32[2,512,4,256]{1,3,0,2:T(8,128)} %fusion.31) | copy-start | bytes 12582916
where the time goes:
time: 163 us; the launch traced here: 162 us
  waiting for transfers between devices  66.4 us (41%)
  local copies, waits for them, and re-layouts  40.8 us (25%)
  matrix products  34.6 us (21%)
  starting transfers between devices  13.4 us (8%)
  other arithmetic  5.94 us (4%)
    ppermute x4, waiting for transfers between devices, swapped(): return lax.ppermute(value, axis, pairs)  49.8 us
    ppermute x2, waiting for transfers between devices, from_behind(): return lax.ppermute(value, axis, pairs)  16.6 us
    unnamed x23, local copies, waits for them, and re-layouts  15.7 us
    dot_general x1, matrix products, on_device(): jnp.einsum('ktmq,kmepq->tmep', stacked_grads, down_shaped, preferred_elem...  9.44 us
    dot_general x1, matrix products, on_device(): jnp.einsum('tmep,kmepq->ktmq', hidden, down_shaped, preferred_element_typ...  7.91 us
    another operation x1, local copies, waits for them, and re-layouts, on_device(): up_local.reshape(factors, block_width, model_local, expand, block_width)  7.82 us
    ppermute x2, starting transfers between devices, from_behind(): return lax.ppermute(value, axis, pairs)  7.81 us
    ppermute x4, starting transfers between devices, swapped(): return lax.ppermute(value, axis, pairs)  5.64 us
  transfers between devices with their start and end apart: 6, of which 6 were waited for; matrix products, arithmetic and copies ran while one was open for 27% of the time, Pallas kernels for 0%

commit v1 on v0

v1 whole, which is shorter than its diff:
```python
import math

import jax
import jax.numpy as jnp
from jax import lax
from jax.experimental import pallas as pl
from jax.experimental.pallas import tpu as pltpu
from jax.sharding import PartitionSpec as P

TANH_SCALE = math.sqrt(2.0 / math.pi)
CUBIC = 0.044715
F32 = jnp.float32
BF16 = jnp.bfloat16


def shifted(value, by):
    length = lax.axis_size("section")
    pairs = [(i, i + by) for i in range(length) if 0 <= i + by < length]
    return lax.ppermute(value, "section", pairs)


def swapped(value, mask):
    pairs = [(source, source ^ mask) for source in range(lax.axis_size("tensor"))]
    return lax.ppermute(value, "tensor", pairs)


def mm(a, b, contract):
    return lax.dot_general(a, b, ((contract[:1], contract[1:]), ((), ())), preferred_element_type=F32)


def rows_of(refs):
    return jnp.concatenate([ref[...] for ref in refs], axis=0)


def pick(edge, if_edge, otherwise, start, rows, after=()):
    columns = if_edge.shape[1]

    def kernel(a, b, *rest):
        at_edge = lax.axis_index("section") == edge
        rest[-1][...] = jnp.where(at_edge, rows_at(a), rows_at(b))

    def rows_at(ref):
        at = 0 if ref.shape[0] == rows else start
        return ref[at : at + rows, :]

    vmem = pl.BlockSpec(memory_space=pltpu.VMEM)
    return pl.pallas_call(
        kernel,
        in_specs=[vmem, vmem] + [pl.BlockSpec(memory_space=pl.ANY)] * len(after),
        out_specs=vmem,
        out_shape=jax.ShapeDtypeStruct((rows, columns), if_edge.dtype),
        compiler_params=pltpu.CompilerParams(vmem_limit_bytes=8 * 2**20),
        cost_estimate=pl.CostEstimate(flops=0, bytes_accessed=0, transcendentals=0),
    )(if_edge, otherwise, *after)


def cut(wanted, args):
    columns = args[0].shape[1]

    def kernel(*refs):
        sources, outs, sems = refs[: len(args)], refs[len(args) : -1], refs[-1]
        section = lax.axis_index("section")
        for i, (edge, there, elsewhere, start, rows) in enumerate(wanted):
            piece = pl.ds(start, rows)
            if there != elsewhere:

                @pl.when(section == edge)
                def _():
                    pltpu.make_async_copy(sources[there].at[piece], outs[i], sems.at[i]).start()

                @pl.when(section != edge)
                def _():
                    pltpu.make_async_copy(sources[elsewhere].at[piece], outs[i], sems.at[i]).start()

            else:
                pltpu.make_async_copy(sources[there].at[piece], outs[i], sems.at[i]).start()
        for i, (_, there, _, start, rows) in enumerate(wanted):
            pltpu.make_async_copy(sources[there].at[pl.ds(start, rows)], outs[i], sems.at[i]).wait()

    return pl.pallas_call(
        kernel,
        in_specs=[pl.BlockSpec(memory_space=pl.ANY)] * len(args),
        out_specs=[pl.BlockSpec(memory_space=pltpu.VMEM)] * len(wanted),
        out_shape=[jax.ShapeDtypeStruct((w[4], columns), args[0].dtype) for w in wanted],
        scratch_shapes=[pltpu.SemaphoreType.DMA((len(wanted),))],
        cost_estimate=pl.CostEstimate(flops=0, bytes_accessed=0, transcendentals=0),
    )(*args)


def behind(value, other):
    return lax.optimization_barrier((value, other))[0]


def gate(v):
    return jnp.tanh(TANH_SCALE * (v + CUBIC * (v * v * v)))


def split(refs, counts):
    groups = []
    for count in counts:
        groups.append(refs[:count])
        refs = refs[count:]
    return groups + [refs]


def forward_kernel(counts, expand, *refs):
    own, theirs, rest = split(refs, counts)
    up, down, base, sent = rest[:2] + rest[-2:]
    width = up.shape[1]
    x = jnp.concatenate([rows_of(own), rows_of(theirs)], axis=1)
    kept = x[:, :width].astype(F32)
    away = jnp.zeros((x.shape[0], width), F32)
    for e in range(expand):
        block = slice(e * width, (e + 1) * width)
        pre = mm(x, up[:, :, block].reshape(2 * width, width), (1, 0))
        hidden = (0.5 * pre * (1.0 + gate(pre))).astype(BF16)
        kept = kept + mm(hidden, down[0, block, :], (1, 0))
        away = away + mm(hidden, down[1, block, :], (1, 0))
    base[...] = kept
    sent[...] = away.astype(BF16)


def backward_kernel(counts, expand, *refs):
    own_x, their_x, own_g, their_g, rest = split(refs, counts)
    up, down, base, sent, up_grad, down_grad = rest[:2] + rest[-4:]
    width = up.shape[1]
    x = jnp.concatenate([rows_of(own_x), rows_of(their_x)], axis=1)
    g = jnp.concatenate([rows_of(own_g), rows_of(their_g)], axis=1)
    kept = g[:, :width].astype(F32)
    away = jnp.zeros((x.shape[0], width), F32)
    for e in range(expand):
        block = slice(e * width, (e + 1) * width)
        up_block = up[:, :, block].reshape(2 * width, width)
        pre = mm(x, up_block, (1, 0))
        grad_hidden = mm(g[:, :width], down[0, block, :], (1, 1)) + mm(
            g[:, width:], down[1, block, :], (1, 1)
        )
        t = gate(pre)
        half = 0.5 * (1.0 + t)
        hidden = (pre * half).astype(BF16)
        slope = half + 0.5 * pre * (1.0 - t * t) * (
            TANH_SCALE * (1.0 + 3.0 * CUBIC * (pre * pre))
        )
        grad_pre = (grad_hidden * slope).astype(BF16)
        kept = kept + mm(grad_pre, up[0, :, block], (1, 1))
        away = away + mm(grad_pre, up[1, :, block], (1, 1))
        down_step = mm(hidden, g, (0, 0)).astype(BF16)
        down_grad[0, block, :] = down_step[:, :width]
        down_grad[1, block, :] = down_step[:, width:]
        up_step = mm(x, grad_pre, (0, 0)).astype(BF16)
        up_grad[0, :, block] = up_step[:width]
        up_grad[1, :, block] = up_step[width:]
    base[...] = kept
    sent[...] = away.astype(BF16)


def specs_of(arrays, width):
    return [pl.BlockSpec((a.shape[0], width), lambda m: (0, m)) for a in arrays]


def weight_specs(up, down, model_local):
    factors, width, hidden = up.shape
    per = hidden // model_local
    return [
        pl.BlockSpec((factors, width, per), lambda m: (0, 0, m)),
        pl.BlockSpec((factors, per, width), lambda m: (0, m, 0)),
    ]


def run(kernel, rows, weights, with_grads, products, after):
    up, down = weights
    factors, width, hidden = up.shape
    flat = [a for group in rows for a in group]
    tokens = sum(a.shape[0] for a in rows[0])
    columns = flat[0].shape[1]
    model_local = columns // width
    expand = hidden // columns
    w_specs = weight_specs(up, down, model_local)
    out_shape = [
        jax.ShapeDtypeStruct((tokens, columns), F32),
        jax.ShapeDtypeStruct((tokens, columns), BF16),
    ]
    out_specs = [pl.BlockSpec((tokens, width), lambda m: (0, m))] * 2
    if with_grads:
        out_shape += [jax.ShapeDtypeStruct(w.shape, BF16) for w in weights]
        out_specs += w_specs
    macs = products * factors * tokens * width * hidden
    return pl.pallas_call(
        lambda *refs: kernel([len(group) for group in rows], expand, *refs),
        grid=(model_local,),
        in_specs=specs_of(flat, width)
        + w_specs
        + [pl.BlockSpec(memory_space=pl.ANY)] * len(after),
        out_specs=out_specs,
        out_shape=out_shape,
        compiler_params=pltpu.CompilerParams(vmem_limit_bytes=32 * 2**20),
        cost_estimate=pl.CostEstimate(
            flops=200 * macs,
            bytes_accessed=4 * (up.size + down.size) + 8 * tokens * columns,
            transcendentals=tokens * hidden,
        ),
    )(*flat, *weights, *after)


def on_device(acts_prev, embedded, grads_next, loss_grad, up_weight, down_weight):
    up, down = up_weight[0], down_weight[0]
    levels = up.shape[0] - 1
    mask = lax.axis_size("tensor") >> levels
    tokens = acts_prev.shape[0]
    end = tokens * 3 // 4
    middle = end // 2
    first, last = 0, lax.axis_size("section") - 1

    early_x, cut_a, early_g, cut_b, cut_c = cut(
        [
            (last, 3, 0, end, tokens - end),
            (first, 0, 0, 0, middle),
            (first, 1, 2, end, tokens - end),
            (first, 0, 0, middle, end - middle),
            (first, 0, 0, end, tokens - end),
        ],
        (acts_prev, embedded, grads_next, loss_grad),
    )
    early_x = swapped(early_x, mask)
    came_a = shifted(cut_a, 1)
    early_g = swapped(early_g, mask)
    came_g = shifted(behind(grads_next, cut_a), -1)
    came_b = shifted(behind(cut_b, early_x), 1)
    own_a = pick(first, embedded, came_a, 0, middle)
    their_a = swapped(own_a, mask)
    came_c = shifted(behind(cut_c, early_g), 1)
    own_b = pick(first, embedded, came_b, middle, end - middle, (own_a,))
    their_b = swapped(own_b, mask)
    own_c = pick(first, embedded, came_c, end, tokens - end)
    own_g = pick(last, loss_grad, came_g, 0, tokens, (own_b,))
    sent_g = own_g[:end]
    their_g = swapped(sent_g, mask)
    their_c = pick(first, early_g, shifted(early_x, 1), 0, tokens - end)
    their_g_c = pick(last, early_x, shifted(early_g, -1), 0, tokens - end)
    own_x, their_x = [own_a, own_b, own_c], [their_a, their_b, their_c]
    their_g = [their_g, their_g_c]

    base_out, sent_out = run(
        forward_kernel, (own_x, their_x), (up, down), False, 2, (sent_g,)
    )
    arrived_out = swapped(sent_out, mask)
    base_back, sent_back, up_grad, down_grad = run(
        backward_kernel, (own_x, their_x, [own_g], their_g), (up, down), True, 5, (sent_out,)
    )
    arrived_back = swapped(sent_back, mask)
    mixed = (base_out + arrived_out.astype(F32)).astype(BF16)
    input_grads = (base_back + arrived_back.astype(F32)).astype(BF16)
    return (mixed, input_grads, up_grad[None], down_grad[None])


def solution(mesh):
    in_specs = (
        P("section", "tensor"),
        P(None, "tensor"),
        P("section", "tensor"),
        P(None, "tensor"),
        P("section", None, None, "tensor"),
        P("section", None, "tensor", None),
    )
    out_specs = (
        P("section", "tensor"),
        P("section", "tensor"),
        P("section", None, None, "tensor"),
        P("section", None, "tensor", None),
    )
    return jax.shard_map(
        on_device, mesh=mesh, in_specs=in_specs, out_specs=out_specs, check_vma=False
    )
```

time: 163 us -> 109 us (0.67)
  local copies, waits for them, and re-layouts: 40.8 us -> 2.22 us
  matrix products: 34.6 us -> 0 us
  Pallas kernels: 0 us -> 30.4 us
  waiting for transfers between devices: 66.4 us -> 45.4 us
  starting transfers between devices: 13.4 us -> 26 us
  other arithmetic: 5.94 us -> 3.86 us
    dot_general x6 -> x0, matrix products: 34.6 us -> none  [the longest x1 9.44 us: on_device(): jnp.einsum('ktmq,kmepq->tmep', stacked_grads, down_shaped, preferred_elem...]
    pallas_call x0 -> x9, Pallas kernels: none -> 30.4 us  [the longest x2 27.5 us: run(): pl.pallas_call(lambda *refs: kernel([len(group) for group in rows], expan...]
    ppermute x6 -> x13, waiting for transfers between devices: 66.4 us -> 45.4 us  [the longest x7 28.7 us: swapped(): return lax.ppermute(value, 'tensor', pairs)]
    unnamed x23 -> x16, local copies, waits for them, and re-layouts: 15.7 us -> 1.29 us
    another operation x5 -> x0, local copies, waits for them, and re-layouts: 14.1 us -> none  [the longest x1 7.82 us: on_device(): up_local.reshape(factors, block_width, model_local, expand, block_width)]
    ppermute x6 -> x13, starting transfers between devices: 13.4 us -> 26 us  [the longest x6 18.9 us: shifted(): return lax.ppermute(value, 'section', pairs)]
    convert_element_type x4 -> x0, local copies, waits for them, and re-layouts: 11 us -> none  [the longest x1 4.79 us: on_device(): down_grad_bits.reshape(factors, hidden_local * block_width, block_width)]
    add x2 -> x0, other arithmetic: 3.76 us -> none  [the longest x1 2.17 us: on_device(): back_sum = back_sum + arrived.astype(jnp.float32)]
  transfers between devices with their start and end apart: 6 -> 13, of which waited for: 6 -> 9; matrix products, arithmetic and copies ran while one was open for 27% -> 3% of each run, Pallas kernels for 0% -> 26%
where the time goes in v1:
time: 109 us
  waiting for transfers between devices  45.4 us (42%)
  Pallas kernels  30.4 us (28%)
  starting transfers between devices  26 us (24%)
  other arithmetic  3.86 us (4%)
  local copies, waits for them, and re-layouts  2.22 us (2%)
    ppermute x7, waiting for transfers between devices, swapped(): return lax.ppermute(value, 'tensor', pairs)  28.7 us
    pallas_call x2, Pallas kernels, run(): pl.pallas_call(lambda *refs: kernel([len(group) for group in rows], expan...  27.5 us
    ppermute x6, starting transfers between devices, shifted(): return lax.ppermute(value, 'section', pairs)  18.9 us
    ppermute x6, waiting for transfers between devices, shifted(): return lax.ppermute(value, 'section', pairs)  16.8 us
    ppermute x7, starting transfers between devices, swapped(): return lax.ppermute(value, 'tensor', pairs)  7.17 us
    pallas_call x1, Pallas kernels, cut(): pl.pallas_call(kernel, in_specs=[pl.BlockSpec(memory_space=pl.ANY)] * len...  2.67 us
    convert_element_type x1, other arithmetic, on_device(): mixed = (base_out + arrived_out.astype(F32)).astype(BF16)  2.54 us
  transfers between devices with their start and end apart: 13, of which 9 were waited for; matrix products, arithmetic and copies ran while one was open for 3% of the time, Pallas kernels for 26%

profile of v1, /device:TPU:0, one launch (start us, length us, event | category | flops | bytes accessed | tf_op | source)
XLA Modules:
  0.0 108.8 jit_solution(13424004804982959790)
XLA Ops:
  0.6 0.0 copy-start
  0.6 0.0 copy-start.6
  0.7 2.7 %shard_map.93 = (bf16[128,1024]{1,0:T(8,128)(2,1)}, bf16[192,1024]{1,0:T(8,128)(2,1)}, bf16[128,1024]{1,0:T(8,128)(2,1)}, bf16[192,1024]{1,0:T(8,128)(2,1)}, bf16[128,1024]{1,0:T(8,128)(2,1)}) custom-call(bf16[512,1024]{1,0:T(8,128)(2,1)} %refs_0_.1, bf16[512,1024]{1,0:T(8,128)(2,1)} %a.6, bf16[512,1024]{1,0:T(8,128)(2,1)} %refs_2_.1, bf16[512,1024]{1,0:T(8,128)(2,1)} %a.7), custom_call_target="tpu_custom_call" | custom-call | tf_op jit(solution)/shard_map/pallas_call | solution.py:80
  3.3 0.0 copy-start.7
  3.3 3.0 %collective-permute-start.1 = (bf16[128,1024]{1,0:T(8,128)(2,1)}, bf16[128,1024]{1,0:T(8,128)(2,1)S(1)}, u32[]{:S(2)}, u32[]{:S(2)}) collective-permute-start(bf16[128,1024]{1,0:T(8,128)(2,1)} %get-tuple-element.20), channel_id=1, source_target_pairs={{0,4},{1,5},{2,6},{3,7},{4,0},{5,1},{6,2},{7,3},{8,12},{9,13},{10,... | collective-permute-start | bytes 786440 | tf_op jit(solution)/shard_map/ppermute | solution.py:24
  6.4 0.0 copy-done.6
  6.4 1.3 %collective-permute-start.8 = (bf16[512,1024]{1,0:T(8,128)(2,1)S(1)}, bf16[512,1024]{1,0:T(8,128)(2,1)S(1)}, u32[]{:S(2)}, u32[]{:S(2)}) collective-permute-start(bf16[512,1024]{1,0:T(8,128)(2,1)S(1)} %copy-done.6), channel_id=1, source_target_pairs={{8,0},{16,8},{24,16},{9,1},{17,9},{25,17},{10,2},{18,10},{26,18},{... | collective-permute-start | bytes 3145736 | tf_op jit(solution)/shard_map/ppermute | solution.py:19
  7.7 4.6 %collective-permute-start = (bf16[192,1024]{1,0:T(8,128)(2,1)}, bf16[192,1024]{1,0:T(8,128)(2,1)S(1)}, u32[]{:S(2)}, u32[]{:S(2)}) collective-permute-start(bf16[192,1024]{1,0:T(8,128)(2,1)} %get-tuple-element.18), channel_id=1, source_target_pairs={{0,8},{8,16},{16,24},{1,9},{9,17},{17,25},{2,10},{10,18},{18,26},{... | collective-permute-start | bytes 1179656 | tf_op jit(solution)/shard_map/ppermute | solution.py:19
  12.2 0.6 collective-permute-done.1.a
  12.9 3.7 %collective-permute-start.2 = (bf16[192,1024]{1,0:T(8,128)(2,1)}, bf16[192,1024]{1,0:T(8,128)(2,1)S(1)}, u32[]{:S(2)}, u32[]{:S(2)}) collective-permute-start(bf16[192,1024]{1,0:T(8,128)(2,1)} %get-tuple-element.21), channel_id=1, source_target_pairs={{0,8},{8,16},{16,24},{1,9},{9,17},{17,25},{2,10},{10,18},{18,26},{... | collective-permute-start | bytes 1179656 | tf_op jit(solution)/shard_map/ppermute | solution.py:19
  16.6 1.6 %collective-permute-start.3 = (bf16[128,1024]{1,0:T(8,128)(2,1)}, bf16[128,1024]{1,0:T(8,128)(2,1)S(1)}, u32[]{:S(2)}, u32[]{:S(2)}) collective-permute-start(bf16[128,1024]{1,0:T(8,128)(2,1)} %get-tuple-element.23), channel_id=1, source_target_pairs={{0,4},{1,5},{2,6},{3,7},{4,0},{5,1},{6,2},{7,3},{8,12},{9,13},{10,... | collective-permute-start | bytes 786440 | tf_op jit(solution)/shard_map/ppermute | solution.py:24
  18.2 3.5 %collective-permute-start.7 = (bf16[128,1024]{1,0:T(8,128)(2,1)S(1)}, bf16[128,1024]{1,0:T(8,128)(2,1)S(1)}, u32[]{:S(2)}, u32[]{:S(2)}) collective-permute-start(bf16[128,1024]{1,0:T(8,128)(2,1)S(1)} %collective-permute-done.1.a), channel_id=1, source_target_pairs={{0,8},{8,16},{16,24},{1,9},{9,17},{17,25},{2,10},{10,18},{18,26},{... | collective-permute-start | bytes 786440 | tf_op jit(solution)/shard_map/ppermute | solution.py:19
  21.7 0.4 collective-permute-done.b
  22.1 0.0 copy-done
  22.1 0.2 collective-permute-start.5
  22.3 8.2 %collective-permute-done.2.b = bf16[192,1024]{1,0:T(8,128)(2,1)S(1)} collective-permute-done((bf16[192,1024]{1,0:T(8,128)(2,1)}, bf16[192,1024]{1,0:T(8,128)(2,1)S(1)}, u32[]{:S(2)}, u32[]{:S(2)}) %collective-permute-start.2) | collective-permute-done | bytes 393248 | tf_op jit(solution)/shard_map/ppermute | solution.py:19
  30.5 0.0 copy-start.5
  30.6 0.0 copy-start.1
  30.6 0.1 collective-permute-start.6
  30.7 0.0 collective-permute-done.3.a
  30.7 0.0 copy-done.7
  30.7 4.5 %collective-permute-start.4 = (bf16[128,1024]{1,0:T(8,128)(2,1)S(1)}, bf16[128,1024]{1,0:T(8,128)(2,1)S(1)}, u32[]{:S(2)}, u32[]{:S(2)}) collective-permute-start(bf16[128,1024]{1,0:T(8,128)(2,1)S(1)} %copy-done.7), channel_id=1, source_target_pairs={{0,8},{8,16},{16,24},{1,9},{9,17},{17,25},{2,10},{10,18},{18,26},{... | collective-permute-start | bytes 786440 | tf_op jit(solution)/shard_map/ppermute | solution.py:19
  35.3 0.8 collective-permute-done.7.b
  36.0 1.3 %collective-permute-start.11 = (bf16[128,1024]{1,0:T(8,128)(2,1)S(1)}, bf16[128,1024]{1,0:T(8,128)(2,1)S(1)}, u32[]{:S(2)}, u32[]{:S(2)}) collective-permute-start(bf16[128,1024]{1,0:T(8,128)(2,1)S(1)} %collective-permute-done.3.a), channel_id=1, source_target_pairs={{8,0},{16,8},{24,16},{9,1},{17,9},{25,17},{10,2},{18,10},{26,18},{... | collective-permute-start | bytes 786440 | tf_op jit(solution)/shard_map/ppermute | solution.py:19
  37.4 2.5 %collective-permute-done.4.b = bf16[128,1024]{1,0:T(8,128)(2,1)S(1)} collective-permute-done((bf16[128,1024]{1,0:T(8,128)(2,1)S(1)}, bf16[128,1024]{1,0:T(8,128)(2,1)S(1)}, u32[]{:S(2)}, u32[]{:S(2)}) %collective-permute-start.4) | collective-permute-done | bytes 262176 | tf_op jit(solution)/shard_map/ppermute | solution.py:19
  39.9 4.8 %collective-permute-done.11.b = bf16[128,1024]{1,0:T(8,128)(2,1)S(1)} collective-permute-done((bf16[128,1024]{1,0:T(8,128)(2,1)S(1)}, bf16[128,1024]{1,0:T(8,128)(2,1)S(1)}, u32[]{:S(2)}, u32[]{:S(2)}) %collective-permute-start.11) | collective-permute-done | bytes 262176 | tf_op jit(solution)/shard_map/ppermute | solution.py:19
  44.8 0.0 copy-start.4
  44.8 0.0 collective-permute-done.8.b
  44.8 0.0 copy-done.1
  44.8 0.1 shard_map.98.refs_6_
  44.9 0.9 slice.4.refs_8_
  45.9 0.0 copy-start.2
  45.9 1.0 copy-done.2
  46.8 0.5 collective-permute-start.10
  47.3 0.0 collective-permute-done.5.refs_3_
  47.3 0.0 collective-permute-done.6.refs_4_
  47.3 0.0 copy-done.5
  47.3 0.3 copy-done.4
  47.6 9.8 %shard_map.99 = (f32[512,1024]{1,0:T(8,128)S(1)}, bf16[512,1024]{1,0:T(8,128)(2,1)}) custom-call(bf16[192,1024]{1,0:T(8,128)(2,1)S(1)} %shard_map.94.rest_0_.refs_0_, bf16[192,1024]{1,0:T(8,128)(2,1)S(1)} %shard_map.95.rest_0_.refs_1_, bf16[128,1024]{1,0:T(8,128)(2,1)S(1)} %shard_map.96.refs_2_, bf16[192,1024]{1,0:T(8,128)(2,1)S(1)} %collective-permute-done.5.refs_3_, ...), custom_call_target="tpu_custom_call" | custom-call | flops 429496729600 | bytes 20971520 | tf_op jit(solution)/shard_map/pallas_call | solution.py:188
  57.4 1.3 %collective-permute-start.9 = (bf16[512,1024]{1,0:T(8,128)(2,1)}, bf16[512,1024]{1,0:T(8,128)(2,1)}, u32[]{:S(2)}, u32[]{:S(2)}) collective-permute-start(bf16[512,1024]{1,0:T(8,128)(2,1)} %get-tuple-element.27.refs_11_), channel_id=1, source_target_pairs={{0,4},{1,5},{2,6},{3,7},{4,0},{5,1},{6,2},{7,3},{8,12},{9,13},{10,... | collective-permute-start | bytes 3145736 | tf_op jit(solution)/shard_map/ppermute | solution.py:24
  58.7 9.0 %collective-permute-done.10.refs_7_ = bf16[384,1024]{1,0:T(8,128)(2,1)} collective-permute-done((bf16[384,1024]{1,0:T(8,128)(2,1)}, bf16[384,1024]{1,0:T(8,128)(2,1)}, u32[]{:S(2)}, u32[]{:S(2)}) %collective-permute-start.10) | collective-permute-done | bytes 786464 | tf_op jit(solution)/shard_map/ppermute | solution.py:24
  67.6 0.0 copy-done.3
  67.6 17.7 %shard_map.101 = (f32[512,1024]{1,0:T(8,128)S(1)}, bf16[512,1024]{1,0:T(8,128)(2,1)S(1)}, bf16[2,256,4096]{2,1,0:T(8,128)(2,1)}, bf16[2,4096,256]{2,1,0:T(8,128)(2,1)}) custom-call(bf16[192,1024]{1,0:T(8,128)(2,1)S(1)} %shard_map.94.rest_0_.refs_0_, bf16[192,1024]{1,0:T(8,128)(2,1)S(1)} %shard_map.95.rest_0_.refs_1_, ...), custom_call_target="tpu_custom_call" | custom-call | flops 1073741824000 | bytes 20971520 | tf_op jit(solution)/shard_map/pallas_call | solution.py:188
  85.3 0.5 collective-permute-start.12
  85.8 4.3 %collective-permute-done.9 = bf16[512,1024]{1,0:T(8,128)(2,1)} collective-permute-done((bf16[512,1024]{1,0:T(8,128)(2,1)}, bf16[512,1024]{1,0:T(8,128)(2,1)}, u32[]{:S(2)}, u32[]{:S(2)}) %collective-permute-start.9) | collective-permute-done | bytes 1048608 | tf_op jit(solution)/shard_map/ppermute | solution.py:24
  90.1 2.5 %add_convert_fusion.1 = bf16[512,1024]{1,0:T(8,128)(2,1)} fusion(f32[512,1024]{1,0:T(8,128)S(1)} %get-tuple-element.26, bf16[512,1024]{1,0:T(8,128)(2,1)} %collective-permute-done.9), kind=kLoop, calls=%fused_computation.1 | loop fusion | flops 1572864 | bytes 4194304 | tf_op jit(solution)/shard_map/convert_element_type | solution.py:251
  92.7 14.8 %collective-permute-done.12 = bf16[512,1024]{1,0:T(8,128)(2,1)S(1)} collective-permute-done((bf16[512,1024]{1,0:T(8,128)(2,1)S(1)}, bf16[512,1024]{1,0:T(8,128)(2,1)S(1)}, u32[]{:S(2)}, u32[]{:S(2)}) %collective-permute-start.12) | collective-permute-done | bytes 1048608 | tf_op jit(solution)/shard_map/ppermute | solution.py:24
  107.4 1.3 %add_convert_fusion = bf16[512,1024]{1,0:T(8,128)(2,1)} fusion(f32[512,1024]{1,0:T(8,128)S(1)} %get-tuple-element.28, bf16[512,1024]{1,0:T(8,128)(2,1)S(1)} %collective-permute-done.12), kind=kLoop, calls=%fused_computation | loop fusion | flops 1572864 | bytes 4194304 | tf_op jit(solution)/shard_map/convert_element_type | solution.py:252
  (6 shorter events, 0.2 us)
Async XLA Ops:
  0.6 21.5 %copy-start = (bf16[512,1024]{1,0:T(8,128)(2,1)S(1)}, bf16[512,1024]{1,0:T(8,128)(2,1)}, u32[]{:S(2)}) copy-start(bf16[512,1024]{1,0:T(8,128)(2,1)} %a.6) | copy-start | bytes 3145732
  0.6 5.7 %copy-start.6 = (bf16[512,1024]{1,0:T(8,128)(2,1)S(1)}, bf16[512,1024]{1,0:T(8,128)(2,1)}, u32[]{:S(2)}) copy-start(bf16[512,1024]{1,0:T(8,128)(2,1)} %refs_2_.1) | copy-start | bytes 3145732
  3.3 27.4 %copy-start.7 = (bf16[128,1024]{1,0:T(8,128)(2,1)S(1)}, bf16[128,1024]{1,0:T(8,128)(2,1)}, u32[]{:S(2)}) copy-start(bf16[128,1024]{1,0:T(8,128)(2,1)} %get-tuple-element.24) | copy-start | bytes 786436
  3.3 9.5 %collective-permute-start.1 = (bf16[128,1024]{1,0:T(8,128)(2,1)}, bf16[128,1024]{1,0:T(8,128)(2,1)S(1)}, u32[]{:S(2)}, u32[]{:S(2)}) collective-permute-start(bf16[128,1024]{1,0:T(8,128)(2,1)} %get-tuple-element.20), channel_id=1, source_target_pairs={{0,4},{1,5},{2,6},{3,7},{4,0},{5,1},{6,2},{7,3},{8,12},{9,13},{10,... | collective-permute-start | bytes 786440 | tf_op jit(solution)/shard_map/ppermute | solution.py:24
  6.4 38.4 %collective-permute-start.8 = (bf16[512,1024]{1,0:T(8,128)(2,1)S(1)}, bf16[512,1024]{1,0:T(8,128)(2,1)S(1)}, u32[]{:S(2)}, u32[]{:S(2)}) collective-permute-start(bf16[512,1024]{1,0:T(8,128)(2,1)S(1)} %copy-done.6), channel_id=1, source_target_pairs={{8,0},{16,8},{24,16},{9,1},{17,9},{25,17},{10,2},{18,10},{26,18},{... | collective-permute-start | bytes 3145736 | tf_op jit(solution)/shard_map/ppermute | solution.py:19
  7.7 14.4 %collective-permute-start = (bf16[192,1024]{1,0:T(8,128)(2,1)}, bf16[192,1024]{1,0:T(8,128)(2,1)S(1)}, u32[]{:S(2)}, u32[]{:S(2)}) collective-permute-start(bf16[192,1024]{1,0:T(8,128)(2,1)} %get-tuple-element.18), channel_id=1, source_target_pairs={{0,8},{8,16},{16,24},{1,9},{9,17},{17,25},{2,10},{10,18},{18,26},{... | collective-permute-start | bytes 1179656 | tf_op jit(solution)/shard_map/ppermute | solution.py:19
  12.9 17.6 %collective-permute-start.2 = (bf16[192,1024]{1,0:T(8,128)(2,1)}, bf16[192,1024]{1,0:T(8,128)(2,1)S(1)}, u32[]{:S(2)}, u32[]{:S(2)}) collective-permute-start(bf16[192,1024]{1,0:T(8,128)(2,1)} %get-tuple-element.21), channel_id=1, source_target_pairs={{0,8},{8,16},{16,24},{1,9},{9,17},{17,25},{2,10},{10,18},{18,26},{... | collective-permute-start | bytes 1179656 | tf_op jit(solution)/shard_map/ppermute | solution.py:19
  16.6 14.1 %collective-permute-start.3 = (bf16[128,1024]{1,0:T(8,128)(2,1)}, bf16[128,1024]{1,0:T(8,128)(2,1)S(1)}, u32[]{:S(2)}, u32[]{:S(2)}) collective-permute-start(bf16[128,1024]{1,0:T(8,128)(2,1)} %get-tuple-element.23), channel_id=1, source_target_pairs={{0,4},{1,5},{2,6},{3,7},{4,0},{5,1},{6,2},{7,3},{8,12},{9,13},{10,... | collective-permute-start | bytes 786440 | tf_op jit(solution)/shard_map/ppermute | solution.py:24
  18.2 17.8 %collective-permute-start.7 = (bf16[128,1024]{1,0:T(8,128)(2,1)S(1)}, bf16[128,1024]{1,0:T(8,128)(2,1)S(1)}, u32[]{:S(2)}, u32[]{:S(2)}) collective-permute-start(bf16[128,1024]{1,0:T(8,128)(2,1)S(1)} %collective-permute-done.1.a), channel_id=1, source_target_pairs={{0,8},{8,16},{16,24},{1,9},{9,17},{17,25},{2,10},{10,18},{18,26},{... | collective-permute-start | bytes 786440 | tf_op jit(solution)/shard_map/ppermute | solution.py:19
  22.1 25.2 %collective-permute-start.5 = (bf16[192,1024]{1,0:T(8,128)(2,1)S(1)}, bf16[192,1024]{1,0:T(8,128)(2,1)S(1)}, u32[]{:S(2)}, u32[]{:S(2)}) collective-permute-start(bf16[192,1024]{1,0:T(8,128)(2,1)S(1)} %shard_map.94.rest_0_.refs_0_), channel_id=1, source_target_pairs={{0,4},{1,5},{2,6},{3,7},{4,0},{5,1},{6,2},{7,3},{8,12},{9,13},{10,... | collective-permute-start | bytes 1179656 | tf_op jit(solution)/shard_map/ppermute | solution.py:24
  30.5 16.8 %copy-start.5 = (bf16[1,2,4096,256]{3,2,1,0:T(8,128)(2,1)S(1)}, bf16[1,2,4096,256]{3,2,1,0:T(8,128)(2,1)}, u32[]{:S(2)}) copy-start(bf16[1,2,4096,256]{3,2,1,0:T(8,128)(2,1)} %param.11) | copy-start | bytes 12582916
  30.6 14.2 %copy-start.1 = (bf16[512,1024]{1,0:T(8,128)(2,1)S(1)}, bf16[512,1024]{1,0:T(8,128)(2,1)}, u32[]{:S(2)}) copy-start(bf16[512,1024]{1,0:T(8,128)(2,1)} %a.7) | copy-start | bytes 3145732
  30.6 16.8 %collective-permute-start.6 = (bf16[192,1024]{1,0:T(8,128)(2,1)S(1)}, bf16[192,1024]{1,0:T(8,128)(2,1)S(1)}, u32[]{:S(2)}, u32[]{:S(2)}) collective-permute-start(bf16[192,1024]{1,0:T(8,128)(2,1)S(1)} %shard_map.95.rest_0_.refs_1_), channel_id=1, source_target_pairs={{0,4},{1,5},{2,6},{3,7},{4,0},{5,1},{6,2},{7,3},{8,12},{9,13},{10,... | collective-permute-start | bytes 1179656 | tf_op jit(solution)/shard_map/ppermute | solution.py:24
  30.7 9.2 %collective-permute-start.4 = (bf16[128,1024]{1,0:T(8,128)(2,1)S(1)}, bf16[128,1024]{1,0:T(8,128)(2,1)S(1)}, u32[]{:S(2)}, u32[]{:S(2)}) collective-permute-start(bf16[128,1024]{1,0:T(8,128)(2,1)S(1)} %copy-done.7), channel_id=1, source_target_pairs={{0,8},{8,16},{16,24},{1,9},{9,17},{17,25},{2,10},{10,18},{18,26},{... | collective-permute-start | bytes 786440 | tf_op jit(solution)/shard_map/ppermute | solution.py:19
  36.0 8.7 %collective-permute-start.11 = (bf16[128,1024]{1,0:T(8,128)(2,1)S(1)}, bf16[128,1024]{1,0:T(8,128)(2,1)S(1)}, u32[]{:S(2)}, u32[]{:S(2)}) collective-permute-start(bf16[128,1024]{1,0:T(8,128)(2,1)S(1)} %collective-permute-done.3.a), channel_id=1, source_target_pairs={{8,0},{16,8},{24,16},{9,1},{17,9},{25,17},{10,2},{18,10},{26,18},{... | collective-permute-start | bytes 786440 | tf_op jit(solution)/shard_map/ppermute | solution.py:19
  44.8 2.9 %copy-start.4 = (bf16[1,2,256,4096]{3,2,1,0:T(8,128)(2,1)S(1)}, bf16[1,2,256,4096]{3,2,1,0:T(8,128)(2,1)}, u32[]{:S(2)}) copy-start(bf16[1,2,256,4096]{3,2,1,0:T(8,128)(2,1)} %param.10) | copy-start | bytes 12582916
  45.9 1.0 copy-start.2
  46.8 20.8 %collective-permute-start.10 = (bf16[384,1024]{1,0:T(8,128)(2,1)}, bf16[384,1024]{1,0:T(8,128)(2,1)}, u32[]{:S(2)}, u32[]{:S(2)}) collective-permute-start(bf16[384,1024]{1,0:T(8,128)(2,1)} %slice.4.refs_8_), channel_id=1, source_target_pairs={{0,4},{1,5},{2,6},{3,7},{4,0},{5,1},{6,2},{7,3},{8,12},{9,13},{10,... | collective-permute-start | bytes 2359304 | tf_op jit(solution)/shard_map/ppermute | solution.py:24
  47.6 20.0 %copy-start.3 = (bf16[512,1024]{1,0:T(8,128)(2,1)S(1)}, bf16[512,1024]{1,0:T(8,128)(2,1)}, u32[]{:S(2)}) copy-start(bf16[512,1024]{1,0:T(8,128)(2,1)} %copy-done.2) | copy-start | bytes 3145732
  57.4 32.7 %collective-permute-start.9 = (bf16[512,1024]{1,0:T(8,128)(2,1)}, bf16[512,1024]{1,0:T(8,128)(2,1)}, u32[]{:S(2)}, u32[]{:S(2)}) collective-permute-start(bf16[512,1024]{1,0:T(8,128)(2,1)} %get-tuple-element.27.refs_11_), channel_id=1, source_target_pairs={{0,4},{1,5},{2,6},{3,7},{4,0},{5,1},{6,2},{7,3},{8,12},{9,13},{10,... | collective-permute-start | bytes 3145736 | tf_op jit(solution)/shard_map/ppermute | solution.py:24
  85.3 22.1 %collective-permute-start.12 = (bf16[512,1024]{1,0:T(8,128)(2,1)S(1)}, bf16[512,1024]{1,0:T(8,128)(2,1)S(1)}, u32[]{:S(2)}, u32[]{:S(2)}) collective-permute-start(bf16[512,1024]{1,0:T(8,128)(2,1)S(1)} %get-tuple-element.29), channel_id=1, source_target_pairs={{0,4},{1,5},{2,6},{3,7},{4,0},{5,1},{6,2},{7,3},{8,12},{9,13},{10,... | collective-permute-start | bytes 3145736 | tf_op jit(solution)/shard_map/ppermute | solution.py:24

commit v2 on v1

--- a/solution.py
+++ b/solution.py
@@ -7,6 +7,12 @@
 from jax.experimental.pallas import tpu as pltpu
 from jax.sharding import PartitionSpec as P
 
+EARLY = 224
+BYTES = 0
+COST_A = 6
+COST_J = 2 * 10**9
+COST_C = 0
+COST_B = 10
 TANH_SCALE = math.sqrt(2.0 / math.pi)
 CUBIC = 0.044715
 F32 = jnp.float32
@@ -32,59 +38,93 @@
     return jnp.concatenate([ref[...] for ref in refs], axis=0)
 
 
-def pick(edge, if_edge, otherwise, start, rows, after=()):
-    columns = if_edge.shape[1]
+def pick(edge, at_edge, elsewhere, rows, after=(), sent=0):
+    (one, one_start), (other, other_start) = at_edge, elsewhere
+    columns = one.shape[1]
+    sizes = [rows, sent] if sent else [rows]
 
     def kernel(a, b, *rest):
-        at_edge = lax.axis_index("section") == edge
-        rest[-1][...] = jnp.where(at_edge, rows_at(a), rows_at(b))
-
-    def rows_at(ref):
-        at = 0 if ref.shape[0] == rows else start
-        return ref[at : at + rows, :]
+        there = lax.axis_index("section") == edge
+        value = jnp.where(there, a[one_start : one_start + rows, :], b[other_start : other_start + rows, :])
+        for size, out in zip(sizes, rest[len(after) :]):
+            out[...] = value[:size]
+
+    vmem = pl.BlockSpec(memory_space=pltpu.VMEM)
+    outs = pl.pallas_call(
+        kernel,
+        in_specs=[vmem, vmem] + [pl.BlockSpec(memory_space=pl.ANY)] * len(after),
+        out_specs=[vmem] * len(sizes),
+        out_shape=[jax.ShapeDtypeStruct((size, columns), one.dtype) for size in sizes],
+        compiler_params=pltpu.CompilerParams(vmem_limit_bytes=8 * 2**20),
+        cost_estimate=pl.CostEstimate(flops=0, bytes_accessed=0, transcendentals=0),
+    )(one, other, *after)
+    return outs if sent else outs[0]
+
+
+def cut(outs_wanted, args):
+    columns = args[0].shape[1]
+    pieces = []
+    for o, wanted in enumerate(outs_wanted):
+        at = 0
+        for edge, there, elsewhere, rows in wanted:
+            pieces.append((o, at, edge, there, elsewhere, rows))
+            at += rows
+
+    def kernel(*refs):
+        sources, outs, sems = refs[: len(args)], refs[len(args) : -1], refs[-1]
+        section = lax.axis_index("section")
+
+        def copy(i, which):
+            o, at, rows = pieces[i][0], pieces[i][1], pieces[i][5]
+            arg, start = pieces[i][which]
+            return pltpu.make_async_copy(
+                sources[arg].at[pl.ds(start, rows)], outs[o].at[pl.ds(at, rows)], sems.at[i]
+            )
+
+        for i, (_, _, edge, there, elsewhere, _) in enumerate(pieces):
+            if there == elsewhere:
+                copy(i, 3).start()
+            else:
+                pl.when(section == edge)(lambda i=i: copy(i, 3).start())
+                pl.when(section != edge)(lambda i=i: copy(i, 4).start())
+        for i in range(len(pieces)):
+            copy(i, 3).wait()
+
+    return pl.pallas_call(
+        kernel,
+        in_specs=[pl.BlockSpec(memory_space=pl.ANY)] * len(args),
+        out_specs=[pl.BlockSpec(memory_space=pltpu.VMEM)] * len(outs_wanted),
+        out_shape=[
+            jax.ShapeDtypeStruct((sum(w[3] for w in wanted), columns), args[0].dtype)
+            for wanted in outs_wanted
+        ],
+        scratch_shapes=[pltpu.SemaphoreType.DMA((len(pieces),))],
+        cost_estimate=pl.CostEstimate(flops=0, bytes_accessed=0, transcendentals=0),
+    )(*args)
+
+
+def join(outs_wanted, args, after, cost=0):
+    columns = args[0].shape[1]
+
+    def kernel(*refs):
+        for wanted, out in zip(outs_wanted, refs[len(args) + len(after) :]):
+            at = 0
+            for arg, start, rows in wanted:
+                out[at : at + rows, :] = refs[arg][start : start + rows, :]
+                at += rows
 
     vmem = pl.BlockSpec(memory_space=pltpu.VMEM)
     return pl.pallas_call(
         kernel,
-        in_specs=[vmem, vmem] + [pl.BlockSpec(memory_space=pl.ANY)] * len(after),
-        out_specs=vmem,
-        out_shape=jax.ShapeDtypeStruct((rows, columns), if_edge.dtype),
+        in_specs=[vmem] * len(args) + [pl.BlockSpec(memory_space=pl.ANY)] * len(after),
+        out_specs=[vmem] * len(outs_wanted),
+        out_shape=[
+            jax.ShapeDtypeStruct((sum(w[2] for w in wanted), columns), args[0].dtype)
+            for wanted in outs_wanted
+        ],
         compiler_params=pltpu.CompilerParams(vmem_limit_bytes=8 * 2**20),
-        cost_estimate=pl.CostEstimate(flops=0, bytes_accessed=0, transcendentals=0),
-    )(if_edge, otherwise, *after)
-
-
-def cut(wanted, args):
-    columns = args[0].shape[1]
-
-    def kernel(*refs):
-        sources, outs, sems = refs[: len(args)], refs[len(args) : -1], refs[-1]
-        section = lax.axis_index("section")
-        for i, (edge, there, elsewhere, start, rows) in enumerate(wanted):
-            piece = pl.ds(start, rows)
-            if there != elsewhere:
-
-                @pl.when(section == edge)
-                def _():
-                    pltpu.make_async_copy(sources[there].at[piece], outs[i], sems.at[i]).start()
-
-                @pl.when(section != edge)
-                def _():
-                    pltpu.make_async_copy(sources[elsewhere].at[piece], outs[i], sems.at[i]).start()
-
-            else:
-                pltpu.make_async_copy(sources[there].at[piece], outs[i], sems.at[i]).start()
-        for i, (_, there, _, start, rows) in enumerate(wanted):
-            pltpu.make_async_copy(sources[there].at[pl.ds(start, rows)], outs[i], sems.at[i]).wait()
-
-    return pl.pallas_call(
-        kernel,
-        in_specs=[pl.BlockSpec(memory_space=pl.ANY)] * len(args),
-        out_specs=[pl.BlockSpec(memory_space=pltpu.VMEM)] * len(wanted),
-        out_shape=[jax.ShapeDtypeStruct((w[4], columns), args[0].dtype) for w in wanted],
-        scratch_shapes=[pltpu.SemaphoreType.DMA((len(wanted),))],
-        cost_estimate=pl.CostEstimate(flops=0, bytes_accessed=0, transcendentals=0),
-    )(*args)
+        cost_estimate=pl.CostEstimate(flops=cost, bytes_accessed=0, transcendentals=0),
+    )(*args, *after)
 
 
 def behind(value, other):
@@ -167,7 +207,7 @@
     ]
 
 
-def run(kernel, rows, weights, with_grads, products, after):
+def run(kernel, rows, weights, with_grads, weight, after):
     up, down = weights
     factors, width, hidden = up.shape
     flat = [a for group in rows for a in group]
@@ -184,7 +224,7 @@
     if with_grads:
         out_shape += [jax.ShapeDtypeStruct(w.shape, BF16) for w in weights]
         out_specs += w_specs
-    macs = products * factors * tokens * width * hidden
+    macs = factors * tokens * width * hidden
     return pl.pallas_call(
         lambda *refs: kernel([len(group) for group in rows], expand, *refs),
         grid=(model_local,),
@@ -195,9 +235,9 @@
         out_shape=out_shape,
         compiler_params=pltpu.CompilerParams(vmem_limit_bytes=32 * 2**20),
         cost_estimate=pl.CostEstimate(
-            flops=200 * macs,
-            bytes_accessed=4 * (up.size + down.size) + 8 * tokens * columns,
-            transcendentals=tokens * hidden,
+            flops=int(weight * macs),
+            bytes_accessed=BYTES,
+            transcendentals=0,
         ),
     )(*flat, *weights, *after)
 
@@ -207,48 +247,49 @@
     levels = up.shape[0] - 1
     mask = lax.axis_size("tensor") >> levels
     tokens = acts_prev.shape[0]
-    end = tokens * 3 // 4
-    middle = end // 2
+    early = tokens * EARLY // 512 // 16 * 16
+    end = tokens - early
     first, last = 0, lax.axis_size("section") - 1
 
-    early_x, cut_a, early_g, cut_b, cut_c = cut(
-        [
-            (last, 3, 0, end, tokens - end),
-            (first, 0, 0, 0, middle),
-            (first, 1, 2, end, tokens - end),
-            (first, 0, 0, middle, end - middle),
-            (first, 0, 0, end, tokens - end),
-        ],
+    (crossing,) = cut(
+        [[(last, (3, end), (0, end), early), (first, (1, end), (2, end), early)]],
         (acts_prev, embedded, grads_next, loss_grad),
     )
-    early_x = swapped(early_x, mask)
+    crossed = swapped(crossing, mask)
+    cut_a, cut_c = join([[(0, 0, end)], [(0, end, early)]], (acts_prev,), ())
     came_a = shifted(cut_a, 1)
-    early_g = swapped(early_g, mask)
-    came_g = shifted(behind(grads_next, cut_a), -1)
-    came_b = shifted(behind(cut_b, early_x), 1)
-    own_a = pick(first, embedded, came_a, 0, middle)
+    came_g = shifted(behind(grads_next, crossing), -1)
+    own_a = pick(first, (embedded, 0), (came_a, 0), end)
     their_a = swapped(own_a, mask)
-    came_c = shifted(behind(cut_c, early_g), 1)
-    own_b = pick(first, embedded, came_b, middle, end - middle, (own_a,))
-    their_b = swapped(own_b, mask)
-    own_c = pick(first, embedded, came_c, end, tokens - end)
-    own_g = pick(last, loss_grad, came_g, 0, tokens, (own_b,))
-    sent_g = own_g[:end]
+    onward_x, onward_g = join(
+        [[(0, 0, early), (1, 0, early)], [(1, early, early)]], (cut_c, crossed), (own_a,), COST_J
+    )
+    came_c = shifted(onward_x, 1)
+    came_g_c = shifted(onward_g, -1)
+    own_g, sent_g = pick(last, (loss_grad, 0), (came_g, 0), tokens, (own_a, onward_g), end)
     their_g = swapped(sent_g, mask)
-    their_c = pick(first, early_g, shifted(early_x, 1), 0, tokens - end)
-    their_g_c = pick(last, early_x, shifted(early_g, -1), 0, tokens - end)
-    own_x, their_x = [own_a, own_b, own_c], [their_a, their_b, their_c]
+    base_a, sent_a = run(
+        forward_kernel, ([own_a], [their_a]), (up, down), False, COST_A, (sent_g,)
+    )
+    arrived_a = swapped(sent_a, mask)
+    own_c = pick(first, (embedded, end), (came_c, 0), early, (sent_a,))
+    their_c = pick(first, (crossed, early), (came_c, early), early, (sent_a,))
+    their_g_c = pick(last, (crossed, 0), (came_g_c, 0), early, (sent_a,))
+    base_c, sent_c = run(forward_kernel, ([own_c], [their_c]), (up, down), False, COST_C, (sent_a,))
+    arrived_c = swapped(sent_c, mask)
+    base_out = jnp.concatenate([base_a, base_c])
+    arrived_out = jnp.concatenate([arrived_a, arrived_c])
+    own_x, their_x = [own_a, own_c], [their_a, their_c]
     their_g = [their_g, their_g_c]
-
-    base_out, sent_out = run(
-        forward_kernel, (own_x, their_x), (up, down), False, 2, (sent_g,)
-    )
-    arrived_out = swapped(sent_out, mask)
     base_back, sent_back, up_grad, down_grad = run(
-        backward_kernel, (own_x, their_x, [own_g], their_g), (up, down), True, 5, (sent_out,)
-    )
-    arrived_back = swapped(sent_back, mask)
+        backward_kernel, (own_x, their_x, [own_g], their_g), (up, down), True, COST_B, (sent_c,)
+    )
+    quarter = tokens // 4
+    arrived_back = jnp.concatenate(
+        [swapped(sent_back[i * quarter : (i + 1) * quarter], mask) for i in range(4)]
+    )
     mixed = (base_out + arrived_out.astype(F32)).astype(BF16)
+    base_back = behind(base_back, mixed)
     input_grads = (base_back + arrived_back.astype(F32)).astype(BF16)
     return (mixed, input_grads, up_grad[None], down_grad[None])
 

time: 109 us -> 98.3 us (0.902)
  waiting for transfers between devices: 45.4 us -> 39.2 us
  starting transfers between devices: 26 us -> 22.4 us
  Pallas kernels: 30.4 us -> 32.9 us
  local copies, waits for them, and re-layouts: 2.22 us -> 0.09 us
  other arithmetic: 3.86 us -> 2.65 us
    ppermute x6 -> x4, starting transfers between devices: 18.9 us -> 10.4 us  [shifted(): return lax.ppermute(value, 'section', pairs)]
    ppermute x7 -> x9, starting transfers between devices: 7.17 us -> 12 us  [swapped(): return lax.ppermute(value, 'tensor', pairs)]
    ppermute x7 -> x9, waiting for transfers between devices: 28.7 us -> 23.9 us  [swapped(): return lax.ppermute(value, 'tensor', pairs)]
    pallas_call x2 -> x3, Pallas kernels: 27.5 us -> 30.1 us  [run(): pl.pallas_call(lambda *refs: kernel([len(group) for group in rows], expan...]
    ppermute x6 -> x4, waiting for transfers between devices: 16.8 us -> 15.3 us  [shifted(): return lax.ppermute(value, 'section', pairs)]
    unnamed x16 -> x12, local copies, waits for them, and re-layouts: 1.29 us -> 0.02 us
    convert_element_type x1, other arithmetic: 2.54 us -> 1.33 us  [on_device(): mixed = (base_out + arrived_out.astype(F32)).astype(BF16)]
  transfers between devices with their start and end apart: 13 -> 13, of which waited for: 9 -> 9; matrix products, arithmetic and copies ran while one was open for 3% -> 1% of each run, Pallas kernels for 26% -> 31%
where the time goes in v2:
time: 98.3 us; the launch traced here: 98.1 us
  waiting for transfers between devices  39.2 us (40%)
  Pallas kernels  32.9 us (33%)
  starting transfers between devices  22.4 us (23%)
  other arithmetic  2.65 us (3%)
    pallas_call x3, Pallas kernels, run(): pl.pallas_call(lambda *refs: kernel([len(group) for group in rows], expan...  30.1 us
    ppermute x9, waiting for transfers between devices, swapped(): return lax.ppermute(value, 'tensor', pairs)  23.9 us
    ppermute x4, waiting for transfers between devices, shifted(): return lax.ppermute(value, 'section', pairs)  15.3 us
    ppermute x9, starting transfers between devices, swapped(): return lax.ppermute(value, 'tensor', pairs)  12 us
    ppermute x4, starting transfers between devices, shifted(): return lax.ppermute(value, 'section', pairs)  10.4 us
    pallas_call x1, Pallas kernels, cut(): pl.pallas_call(kernel, in_specs=[pl.BlockSpec(memory_space=pl.ANY)] * len...  2.27 us
  transfers between devices with their start and end apart: 13, of which 9 were waited for; matrix products, arithmetic and copies ran while one was open for 1% of the time, Pallas kernels for 31%

profile of v2, /device:TPU:0, one launch (start us, length us, event | category | flops | bytes accessed | tf_op | source)
XLA Modules:
  0.0 98.1 jit_solution(4671554038822673622)
XLA Ops:
  0.6 0.0 copy-start
  0.6 0.0 copy-start.5
  0.7 0.0 copy-start.4
  0.7 2.3 %shard_map.95 = bf16[448,1024]{1,0:T(8,128)(2,1)} custom-call(bf16[512,1024]{1,0:T(8,128)(2,1)} %refs_0_.3, bf16[512,1024]{1,0:T(8,128)(2,1)} %a.5, bf16[512,1024]{1,0:T(8,128)(2,1)} %refs_2_.1, bf16[512,1024]{1,0:T(8,128)(2,1)} %a.4), custom_call_target="tpu_custom_call" | custom-call | tf_op jit(solution)/shard_map/pallas_call | solution.py:93
  2.9 3.0 %collective-permute-start.3 = (bf16[448,1024]{1,0:T(8,128)(2,1)}, bf16[448,1024]{1,0:T(8,128)(2,1)S(1)}, u32[]{:S(2)}, u32[]{:S(2)}) collective-permute-start(bf16[448,1024]{1,0:T(8,128)(2,1)} %shard_map.95), channel_id=1, source_target_pairs={{0,4},{1,5},{2,6},{3,7},{4,0},{5,1},{6,2},{7,3},{8,12},{9,13},{10,... | collective-permute-start | bytes 2752520 | tf_op jit(solution)/shard_map/ppermute | solution.py:30
  6.0 0.0 copy-done.4
  6.0 0.1 shard_map.93
  6.0 3.5 %collective-permute-start = (bf16[288,1024]{1,0:T(8,128)(2,1)S(1)}, bf16[288,1024]{1,0:T(8,128)(2,1)S(1)}, u32[]{:S(2)}, u32[]{:S(2)}) collective-permute-start(bf16[288,1024]{1,0:T(8,128)(2,1)S(1)} %get-tuple-element.20), channel_id=1, source_target_pairs={{0,8},{8,16},{16,24},{1,9},{9,17},{17,25},{2,10},{10,18},{18,26},{... | collective-permute-start | bytes 1769480 | tf_op jit(solution)/shard_map/ppermute | solution.py:25
  9.6 0.0 copy-done.5
  9.6 1.3 %collective-permute-start.2 = (bf16[512,1024]{1,0:T(8,128)(2,1)S(1)}, bf16[512,1024]{1,0:T(8,128)(2,1)S(1)}, u32[]{:S(2)}, u32[]{:S(2)}) collective-permute-start(bf16[512,1024]{1,0:T(8,128)(2,1)S(1)} %copy-done.5), channel_id=1, source_target_pairs={{8,0},{16,8},{24,16},{9,1},{17,9},{25,17},{10,2},{18,10},{26,18},{... | collective-permute-start | bytes 3145736 | tf_op jit(solution)/shard_map/ppermute | solution.py:25
  10.9 10.9 %collective-permute-done.b = bf16[288,1024]{1,0:T(8,128)(2,1)S(1)} collective-permute-done((bf16[288,1024]{1,0:T(8,128)(2,1)S(1)}, bf16[288,1024]{1,0:T(8,128)(2,1)S(1)}, u32[]{:S(2)}, u32[]{:S(2)}) %collective-permute-start) | collective-permute-done | bytes 589856 | tf_op jit(solution)/shard_map/ppermute | solution.py:25
  21.8 0.0 copy-done
  21.8 0.1 shard_map.94.refs_2_.rest_0_.refs_0_
  21.9 0.6 collective-permute-start.1
  22.5 4.9 %collective-permute-done.3.refs_1_.a = bf16[448,1024]{1,0:T(8,128)(2,1)S(1)} collective-permute-done((bf16[448,1024]{1,0:T(8,128)(2,1)}, bf16[448,1024]{1,0:T(8,128)(2,1)S(1)}, u32[]{:S(2)}, u32[]{:S(2)}) %collective-permute-start.3) | collective-permute-done | bytes 917536 | tf_op jit(solution)/shard_map/ppermute | solution.py:30
  27.4 0.1 shard_map.96
  27.5 4.3 %collective-permute-start.4 = (bf16[448,1024]{1,0:T(8,128)(2,1)S(1)}, bf16[448,1024]{1,0:T(8,128)(2,1)S(1)}, u32[]{:S(2)}, u32[]{:S(2)}) collective-permute-start(bf16[448,1024]{1,0:T(8,128)(2,1)S(1)} %get-tuple-element.26), channel_id=1, source_target_pairs={{0,8},{8,16},{16,24},{1,9},{9,17},{17,25},{2,10},{10,18},{18,26},{... | collective-permute-start | bytes 2752520 | tf_op jit(solution)/shard_map/ppermute | solution.py:25
  31.8 4.0 %collective-permute-done.2.b = bf16[512,1024]{1,0:T(8,128)(2,1)S(1)} collective-permute-done((bf16[512,1024]{1,0:T(8,128)(2,1)S(1)}, bf16[512,1024]{1,0:T(8,128)(2,1)S(1)}, u32[]{:S(2)}, u32[]{:S(2)}) %collective-permute-start.2) | collective-permute-done | bytes 1048608 | tf_op jit(solution)/shard_map/ppermute | solution.py:25
  35.8 0.0 copy-done.1
  35.8 0.1 shard_map.97
  36.0 0.6 collective-permute-start.7
  36.5 1.3 %collective-permute-start.8 = (bf16[224,1024]{1,0:T(8,128)(2,1)S(1)}, bf16[224,1024]{1,0:T(8,128)(2,1)S(1)}, u32[]{:S(2)}, u32[]{:S(2)}) collective-permute-start(bf16[224,1024]{1,0:T(8,128)(2,1)S(1)} %get-tuple-element.23.rest_1_), channel_id=1, source_target_pairs={{8,0},{16,8},{24,16},{9,1},{17,9},{25,17},{10,2},{18,10},{26,18},{... | collective-permute-start | bytes 1376264 | tf_op jit(solution)/shard_map/ppermute | solution.py:25
  37.8 2.2 %collective-permute-done.1.refs_1_.refs_2_ = bf16[288,1024]{1,0:T(8,128)(2,1)S(1)} collective-permute-done((bf16[288,1024]{1,0:T(8,128)(2,1)S(1)}, bf16[288,1024]{1,0:T(8,128)(2,1)S(1)}, u32[]{:S(2)}, u32[]{:S(2)}) %collective-permute-start.1) | collective-permute-done | bytes 589856 | tf_op jit(solution)/shard_map/ppermute | solution.py:30
  40.0 0.0 copy-done.2
  40.0 6.8 %shard_map.98 = (f32[288,1024]{1,0:T(8,128)S(1)}, bf16[288,1024]{1,0:T(8,128)(2,1)S(1)}) custom-call(bf16[288,1024]{1,0:T(8,128)(2,1)S(1)} %shard_map.94.refs_2_.rest_0_.refs_0_, bf16[288,1024]{1,0:T(8,128)(2,1)S(1)} %collective-permute-done.1.refs_1_.refs_2_, bf16[2,256,4096]{2,1,0:T(8,128)(2,1)S(1)} %bitcast.4, bf16[2,4096,256]{2,1,0:T(8,128)(2,1)S(1)} %bitcast.7, ...), custom_call_target="tpu_custom_call" | custom-call | flops 3623878656 | tf_op jit(solution)/shard_map/pallas_call | solution.py:228
  46.8 2.1 %collective-permute-start.5 = (bf16[288,1024]{1,0:T(8,128)(2,1)S(1)}, bf16[288,1024]{1,0:T(8,128)(2,1)S(1)}, u32[]{:S(2)}, u32[]{:S(2)}) collective-permute-start(bf16[288,1024]{1,0:T(8,128)(2,1)S(1)} %get-tuple-element.27.rest_0_.refs_4_), channel_id=1, source_target_pairs={{0,4},{1,5},{2,6},{3,7},{4,0},{5,1},{6,2},{7,3},{8,12},{9,13},{10,... | collective-permute-start | bytes 1769480 | tf_op jit(solution)/shard_map/ppermute | solution.py:30
  48.9 0.0 collective-permute-done.8.b
  48.9 0.1 shard_map.102.refs_6_
  49.0 0.3 collective-permute-done.4.b
  49.3 0.1 shard_map.100.refs_1_.refs_3_
  49.4 0.1 shard_map.99.refs_0_.refs_1_
  49.4 6.1 %shard_map.101 = (f32[224,1024]{1,0:T(8,128)S(1)}, bf16[224,1024]{1,0:T(8,128)(2,1)S(1)}) custom-call(bf16[224,1024]{1,0:T(8,128)(2,1)S(1)} %shard_map.99.refs_0_.refs_1_, bf16[224,1024]{1,0:T(8,128)(2,1)S(1)} %shard_map.100.refs_1_.refs_3_, bf16[2,256,4096]{2,1,0:T(8,128)(2,1)S(1)} %bitcast.5, bf16[2,4096,256]{2,1,0:T(8,128)(2,1)S(1)} %bitcast.8, ...), custom_call_target="tpu_custom_call" | custom-call | tf_op jit(solution)/shard_map/pallas_call | solution.py:228
  55.6 1.6 %collective-permute-start.6 = (bf16[224,1024]{1,0:T(8,128)(2,1)S(1)}, bf16[224,1024]{1,0:T(8,128)(2,1)S(1)}, u32[]{:S(2)}, u32[]{:S(2)}) collective-permute-start(bf16[224,1024]{1,0:T(8,128)(2,1)S(1)} %get-tuple-element.29.refs_9_), channel_id=1, source_target_pairs={{0,4},{1,5},{2,6},{3,7},{4,0},{5,1},{6,2},{7,3},{8,12},{9,13},{10,... | collective-permute-start | bytes 1376264 | tf_op jit(solution)/shard_map/ppermute | solution.py:30
  57.1 0.0 collective-permute-done.7.refs_5_
  57.1 17.3 %shard_map.103 = (f32[512,1024]{1,0:T(8,128)S(1)}, bf16[512,1024]{1,0:T(8,128)(2,1)S(1)}, bf16[2,256,4096]{2,1,0:T(8,128)(2,1)}, bf16[2,4096,256]{2,1,0:T(8,128)(2,1)}) custom-call(bf16[288,1024]{1,0:T(8,128)(2,1)S(1)} %shard_map.94.refs_2_.rest_0_.refs_0_, bf16[224,1024]{1,0:T(8,128)(2,1)S(1)} %shard_map.99.refs_0_.refs_1_, ...), custom_call_target="tpu_custom_call" | custom-call | flops 10737418240 | tf_op jit(solution)/shard_map/pallas_call | solution.py:228
  74.4 0.1 fusion.1
  74.5 0.6 collective-permute-start.9
  75.1 1.5 %collective-permute-start.12 = (bf16[128,1024]{1,0:T(8,128)(2,1)S(1)}, bf16[128,1024]{1,0:T(8,128)(2,1)S(1)}, u32[]{:S(2)}, u32[]{:S(2)}) collective-permute-start(bf16[128,1024]{1,0:T(8,128)(2,1)S(1)} %get-tuple-element.37), channel_id=1, source_target_pairs={{0,4},{1,5},{2,6},{3,7},{4,0},{5,1},{6,2},{7,3},{8,12},{9,13},{10,... | collective-permute-start | bytes 786440 | tf_op jit(solution)/shard_map/ppermute | solution.py:30
  76.6 0.5 collective-permute-start.11
  77.1 0.0 collective-permute-done.5
  77.1 1.5 %collective-permute-start.10 = (bf16[128,1024]{1,0:T(8,128)(2,1)S(1)}, bf16[128,1024]{1,0:T(8,128)(2,1)S(1)}, u32[]{:S(2)}, u32[]{:S(2)}) collective-permute-start(bf16[128,1024]{1,0:T(8,128)(2,1)S(1)} %get-tuple-element.39), channel_id=1, source_target_pairs={{0,4},{1,5},{2,6},{3,7},{4,0},{5,1},{6,2},{7,3},{8,12},{9,13},{10,... | collective-permute-start | bytes 786440 | tf_op jit(solution)/shard_map/ppermute | solution.py:30
  78.6 0.0 collective-permute-done.6
  78.6 1.3 %fusion = bf16[512,1024]{1,0:T(8,128)(2,1)} fusion(f32[224,1024]{1,0:T(8,128)S(1)} %get-tuple-element.28, f32[288,1024]{1,0:T(8,128)S(1)} %get-tuple-element.25, bf16[224,1024]{1,0:T(8,128)(2,1)S(1)} %collective-permute-done.6, bf16[288,1024]{1,0:T(8,128)(2,1)S(1)} %collective-permute-done.5), kind=kLoop, calls=%fused_computation.1 | loop fusion | flops 3670016 | bytes 4194304 | tf_op jit(solution)/shard_map/convert_element_type | solution.py:291
  79.9 3.9 %collective-permute-done.9 = bf16[128,1024]{1,0:T(8,128)(2,1)S(1)} collective-permute-done((bf16[128,1024]{1,0:T(8,128)(2,1)S(1)}, bf16[128,1024]{1,0:T(8,128)(2,1)S(1)}, u32[]{:S(2)}, u32[]{:S(2)}) %collective-permute-start.9) | collective-permute-done | bytes 262176 | tf_op jit(solution)/shard_map/ppermute | solution.py:30
  83.8 5.6 %collective-permute-done.12 = bf16[128,1024]{1,0:T(8,128)(2,1)S(1)} collective-permute-done((bf16[128,1024]{1,0:T(8,128)(2,1)S(1)}, bf16[128,1024]{1,0:T(8,128)(2,1)S(1)}, u32[]{:S(2)}, u32[]{:S(2)}) %collective-permute-start.12) | collective-permute-done | bytes 262176 | tf_op jit(solution)/shard_map/ppermute | solution.py:30
  89.4 4.5 %collective-permute-done.11 = bf16[128,1024]{1,0:T(8,128)(2,1)S(1)} collective-permute-done((bf16[128,1024]{1,0:T(8,128)(2,1)S(1)}, bf16[128,1024]{1,0:T(8,128)(2,1)S(1)}, u32[]{:S(2)}, u32[]{:S(2)}) %collective-permute-start.11) | collective-permute-done | bytes 262176 | tf_op jit(solution)/shard_map/ppermute | solution.py:30
  93.9 2.8 %collective-permute-done.10 = bf16[128,1024]{1,0:T(8,128)(2,1)S(1)} collective-permute-done((bf16[128,1024]{1,0:T(8,128)(2,1)S(1)}, bf16[128,1024]{1,0:T(8,128)(2,1)S(1)}, u32[]{:S(2)}, u32[]{:S(2)}) %collective-permute-start.10) | collective-permute-done | bytes 262176 | tf_op jit(solution)/shard_map/ppermute | solution.py:30
  96.8 1.3 %add_convert_fusion = bf16[512,1024]{1,0:T(8,128)(2,1)} fusion(f32[512,1024]{1,0:T(8,128)S(1)} %get-tuple-element.32, bf16[128,1024]{1,0:T(8,128)(2,1)S(1)} %collective-permute-done.12, bf16[128,1024]{1,0:T(8,128)(2,1)S(1)} %collective-permute-done.11, bf16[128,1024]{1,0:T(8,128)(2,1)S(1)} %collective-permute-done.10, ...), kind=kLoop, calls=%fused_computation.2 | loop fusion | flops 5242880 | bytes 4194304 | tf_op jit(solution)/shard_map/convert_element_type | solution.py:293
  (4 shorter events, 0.0 us)
Async XLA Ops:
  0.6 21.2 %copy-start = (bf16[512,1024]{1,0:T(8,128)(2,1)S(1)}, bf16[512,1024]{1,0:T(8,128)(2,1)}, u32[]{:S(2)}) copy-start(bf16[512,1024]{1,0:T(8,128)(2,1)} %a.5) | copy-start | bytes 3145732
  0.6 8.9 %copy-start.5 = (bf16[512,1024]{1,0:T(8,128)(2,1)S(1)}, bf16[512,1024]{1,0:T(8,128)(2,1)}, u32[]{:S(2)}) copy-start(bf16[512,1024]{1,0:T(8,128)(2,1)} %refs_2_.1) | copy-start | bytes 3145732
  0.7 5.3 %copy-start.4 = (bf16[512,1024]{1,0:T(8,128)(2,1)S(1)}, bf16[512,1024]{1,0:T(8,128)(2,1)}, u32[]{:S(2)}) copy-start(bf16[512,1024]{1,0:T(8,128)(2,1)} %refs_0_.3) | copy-start | bytes 3145732
  2.9 24.4 %collective-permute-start.3 = (bf16[448,1024]{1,0:T(8,128)(2,1)}, bf16[448,1024]{1,0:T(8,128)(2,1)S(1)}, u32[]{:S(2)}, u32[]{:S(2)}) collective-permute-start(bf16[448,1024]{1,0:T(8,128)(2,1)} %shard_map.95), channel_id=1, source_target_pairs={{0,4},{1,5},{2,6},{3,7},{4,0},{5,1},{6,2},{7,3},{8,12},{9,13},{10,... | collective-permute-start | bytes 2752520 | tf_op jit(solution)/shard_map/ppermute | solution.py:30
  6.0 15.8 %collective-permute-start = (bf16[288,1024]{1,0:T(8,128)(2,1)S(1)}, bf16[288,1024]{1,0:T(8,128)(2,1)S(1)}, u32[]{:S(2)}, u32[]{:S(2)}) collective-permute-start(bf16[288,1024]{1,0:T(8,128)(2,1)S(1)} %get-tuple-element.20), channel_id=1, source_target_pairs={{0,8},{8,16},{16,24},{1,9},{9,17},{17,25},{2,10},{10,18},{18,26},{... | collective-permute-start | bytes 1769480 | tf_op jit(solution)/shard_map/ppermute | solution.py:25
  9.6 26.2 %collective-permute-start.2 = (bf16[512,1024]{1,0:T(8,128)(2,1)S(1)}, bf16[512,1024]{1,0:T(8,128)(2,1)S(1)}, u32[]{:S(2)}, u32[]{:S(2)}) collective-permute-start(bf16[512,1024]{1,0:T(8,128)(2,1)S(1)} %copy-done.5), channel_id=1, source_target_pairs={{8,0},{16,8},{24,16},{9,1},{17,9},{25,17},{10,2},{18,10},{26,18},{... | collective-permute-start | bytes 3145736 | tf_op jit(solution)/shard_map/ppermute | solution.py:25
  21.9 18.1 %collective-permute-start.1 = (bf16[288,1024]{1,0:T(8,128)(2,1)S(1)}, bf16[288,1024]{1,0:T(8,128)(2,1)S(1)}, u32[]{:S(2)}, u32[]{:S(2)}) collective-permute-start(bf16[288,1024]{1,0:T(8,128)(2,1)S(1)} %shard_map.94.refs_2_.rest_0_.refs_0_), channel_id=1, source_target_pairs={{0,4},{1,5},{2,6},{3,7},{4,0},{5,1},{6,2},{7,3},{8,12},{9,13},{10,... | collective-permute-start | bytes 1769480 | tf_op jit(solution)/shard_map/ppermute | solution.py:30
  27.4 8.5 %copy-start.1 = (bf16[512,1024]{1,0:T(8,128)(2,1)S(1)}, bf16[512,1024]{1,0:T(8,128)(2,1)}, u32[]{:S(2)}) copy-start(bf16[512,1024]{1,0:T(8,128)(2,1)} %a.4) | copy-start | bytes 3145732
  27.4 12.6 %copy-start.2 = (bf16[1,2,256,4096]{3,2,1,0:T(8,128)(2,1)S(1)}, bf16[1,2,256,4096]{3,2,1,0:T(8,128)(2,1)}, u32[]{:S(2)}) copy-start(bf16[1,2,256,4096]{3,2,1,0:T(8,128)(2,1)} %param.10) | copy-start | bytes 12582916
  27.4 12.6 %copy-start.3 = (bf16[1,2,4096,256]{3,2,1,0:T(8,128)(2,1)S(1)}, bf16[1,2,4096,256]{3,2,1,0:T(8,128)(2,1)}, u32[]{:S(2)}) copy-start(bf16[1,2,4096,256]{3,2,1,0:T(8,128)(2,1)} %param.11) | copy-start | bytes 12582916
  27.5 21.9 %collective-permute-start.4 = (bf16[448,1024]{1,0:T(8,128)(2,1)S(1)}, bf16[448,1024]{1,0:T(8,128)(2,1)S(1)}, u32[]{:S(2)}, u32[]{:S(2)}) collective-permute-start(bf16[448,1024]{1,0:T(8,128)(2,1)S(1)} %get-tuple-element.26), channel_id=1, source_target_pairs={{0,8},{8,16},{16,24},{1,9},{9,17},{17,25},{2,10},{10,18},{18,26},{... | collective-permute-start | bytes 2752520 | tf_op jit(solution)/shard_map/ppermute | solution.py:25
  36.0 21.2 %collective-permute-start.7 = (bf16[288,1024]{1,0:T(8,128)(2,1)S(1)}, bf16[288,1024]{1,0:T(8,128)(2,1)S(1)}, u32[]{:S(2)}, u32[]{:S(2)}) collective-permute-start(bf16[288,1024]{1,0:T(8,128)(2,1)S(1)} %get-tuple-element.24.refs_4_), channel_id=1, source_target_pairs={{0,4},{1,5},{2,6},{3,7},{4,0},{5,1},{6,2},{7,3},{8,12},{9,13},{10,... | collective-permute-start | bytes 1769480 | tf_op jit(solution)/shard_map/ppermute | solution.py:30
  36.5 12.4 %collective-permute-start.8 = (bf16[224,1024]{1,0:T(8,128)(2,1)S(1)}, bf16[224,1024]{1,0:T(8,128)(2,1)S(1)}, u32[]{:S(2)}, u32[]{:S(2)}) collective-permute-start(bf16[224,1024]{1,0:T(8,128)(2,1)S(1)} %get-tuple-element.23.rest_1_), channel_id=1, source_target_pairs={{8,0},{16,8},{24,16},{9,1},{17,9},{25,17},{10,2},{18,10},{26,18},{... | collective-permute-start | bytes 1376264 | tf_op jit(solution)/shard_map/ppermute | solution.py:25
  46.8 30.3 %collective-permute-start.5 = (bf16[288,1024]{1,0:T(8,128)(2,1)S(1)}, bf16[288,1024]{1,0:T(8,128)(2,1)S(1)}, u32[]{:S(2)}, u32[]{:S(2)}) collective-permute-start(bf16[288,1024]{1,0:T(8,128)(2,1)S(1)} %get-tuple-element.27.rest_0_.refs_4_), channel_id=1, source_target_pairs={{0,4},{1,5},{2,6},{3,7},{4,0},{5,1},{6,2},{7,3},{8,12},{9,13},{10,... | collective-permute-start | bytes 1769480 | tf_op jit(solution)/shard_map/ppermute | solution.py:30
  55.6 23.1 %collective-permute-start.6 = (bf16[224,1024]{1,0:T(8,128)(2,1)S(1)}, bf16[224,1024]{1,0:T(8,128)(2,1)S(1)}, u32[]{:S(2)}, u32[]{:S(2)}) collective-permute-start(bf16[224,1024]{1,0:T(8,128)(2,1)S(1)} %get-tuple-element.29.refs_9_), channel_id=1, source_target_pairs={{0,4},{1,5},{2,6},{3,7},{4,0},{5,1},{6,2},{7,3},{8,12},{9,13},{10,... | collective-permute-start | bytes 1376264 | tf_op jit(solution)/shard_map/ppermute | solution.py:30
  74.5 9.3 %collective-permute-start.9 = (bf16[128,1024]{1,0:T(8,128)(2,1)S(1)}, bf16[128,1024]{1,0:T(8,128)(2,1)S(1)}, u32[]{:S(2)}, u32[]{:S(2)}) collective-permute-start(bf16[128,1024]{1,0:T(8,128)(2,1)S(1)} %get-tuple-element.36), channel_id=1, source_target_pairs={{0,4},{1,5},{2,6},{3,7},{4,0},{5,1},{6,2},{7,3},{8,12},{9,13},{10,... | collective-permute-start | bytes 786440 | tf_op jit(solution)/shard_map/ppermute | solution.py:30
  75.1 14.4 %collective-permute-start.12 = (bf16[128,1024]{1,0:T(8,128)(2,1)S(1)}, bf16[128,1024]{1,0:T(8,128)(2,1)S(1)}, u32[]{:S(2)}, u32[]{:S(2)}) collective-permute-start(bf16[128,1024]{1,0:T(8,128)(2,1)S(1)} %get-tuple-element.37), channel_id=1, source_target_pairs={{0,4},{1,5},{2,6},{3,7},{4,0},{5,1},{6,2},{7,3},{8,12},{9,13},{10,... | collective-permute-start | bytes 786440 | tf_op jit(solution)/shard_map/ppermute | solution.py:30
  76.6 17.4 %collective-permute-start.11 = (bf16[128,1024]{1,0:T(8,128)(2,1)S(1)}, bf16[128,1024]{1,0:T(8,128)(2,1)S(1)}, u32[]{:S(2)}, u32[]{:S(2)}) collective-permute-start(bf16[128,1024]{1,0:T(8,128)(2,1)S(1)} %get-tuple-element.38), channel_id=1, source_target_pairs={{0,4},{1,5},{2,6},{3,7},{4,0},{5,1},{6,2},{7,3},{8,12},{9,13},{10,... | collective-permute-start | bytes 786440 | tf_op jit(solution)/shard_map/ppermute | solution.py:30
  77.1 19.7 %collective-permute-start.10 = (bf16[128,1024]{1,0:T(8,128)(2,1)S(1)}, bf16[128,1024]{1,0:T(8,128)(2,1)S(1)}, u32[]{:S(2)}, u32[]{:S(2)}) collective-permute-start(bf16[128,1024]{1,0:T(8,128)(2,1)S(1)} %get-tuple-element.39), channel_id=1, source_target_pairs={{0,4},{1,5},{2,6},{3,7},{4,0},{5,1},{6,2},{7,3},{8,12},{9,13},{10,... | collective-permute-start | bytes 786440 | tf_op jit(solution)/shard_map/ppermute | solution.py:30

commit v3 on v0

v3 whole, which is shorter than its diff:
```python
import math

import jax
import jax.numpy as jnp
from jax import lax
from jax.experimental import pallas as pl
from jax.experimental.pallas import tpu as pltpu
from jax.sharding import PartitionSpec as P

COST_A = 3 * 10**9
COST_G = 10**9
COST_B = 4 * 10**9
COST_BACK = 6 * 10**9
LIMIT = 8
BYTES = 8 * 2**20
TANH_SCALE = math.sqrt(2.0 / math.pi)
CUBIC = 0.044715
F32 = jnp.float32
BF16 = jnp.bfloat16


def shifted(value, by):
    length = lax.axis_size("section")
    pairs = [(i, i + by) for i in range(length) if 0 <= i + by < length]
    return lax.ppermute(value, "section", pairs)


def swapped(value, mask):
    pairs = [(source, source ^ mask) for source in range(lax.axis_size("tensor"))]
    return lax.ppermute(value, "tensor", pairs)


def exchanged(value, mask, sections):
    size = lax.axis_size("tensor")
    pairs = []
    for s in range(lax.axis_size("section")):
        distance = mask if s in sections else 1
        pairs += [(s * size + t, s * size + (t ^ distance)) for t in range(size)]
    return lax.ppermute(value, ("section", "tensor"), pairs)


def mm(a, b, contract):
    return lax.dot_general(a, b, ((contract[:1], contract[1:]), ((), ())), preferred_element_type=F32)


def rows_of(refs):
    return jnp.concatenate([ref[...] for ref in refs], axis=0)


def pick(edge, at_edge, elsewhere, rows, after=(), cost=0):
    (one, one_start), (other, other_start) = at_edge, elsewhere

    def kernel(a, b, *rest):
        there = lax.axis_index("section") == edge
        rest[-1][...] = jnp.where(
            there, a[one_start : one_start + rows, :], b[other_start : other_start + rows, :]
        )

    vmem = pl.BlockSpec(memory_space=pltpu.VMEM)
    return pl.pallas_call(
        kernel,
        in_specs=[vmem, vmem] + [pl.BlockSpec(memory_space=pl.ANY)] * len(after),
        out_specs=vmem,
        out_shape=jax.ShapeDtypeStruct((rows, one.shape[1]), one.dtype),
        compiler_params=pltpu.CompilerParams(vmem_limit_bytes=8 * 2**20),
        cost_estimate=pl.CostEstimate(flops=cost, bytes_accessed=0, transcendentals=0),
    )(one, other, *after)


def join(outs_wanted, args, after, cost=0):
    columns = args[0].shape[1]

    def kernel(*refs):
        for wanted, out in zip(outs_wanted, refs[len(args) + len(after) :]):
            at = 0
            for arg, start, rows in wanted:
                out[at : at + rows, :] = refs[arg][start : start + rows, :]
                at += rows

    vmem = pl.BlockSpec(memory_space=pltpu.VMEM)
    return pl.pallas_call(
        kernel,
        in_specs=[vmem] * len(args) + [pl.BlockSpec(memory_space=pl.ANY)] * len(after),
        out_specs=[vmem] * len(outs_wanted),
        out_shape=[
            jax.ShapeDtypeStruct((sum(w[2] for w in wanted), columns), args[0].dtype)
            for wanted in outs_wanted
        ],
        compiler_params=pltpu.CompilerParams(vmem_limit_bytes=8 * 2**20),
        cost_estimate=pl.CostEstimate(flops=cost, bytes_accessed=BYTES, transcendentals=0),
    )(*args, *after)


def gate(v):
    return jnp.tanh(TANH_SCALE * (v + CUBIC * (v * v * v)))


def split(refs, counts):
    groups = []
    for count in counts:
        groups.append(refs[:count])
        refs = refs[count:]
    return groups + [refs]


def columns_of(refs, block):
    return jnp.concatenate([ref[:, block] for ref in refs], axis=0)


def over_blocks(width, columns, expand, body):
    @pl.loop(0, columns // width)
    def _(m):
        model = pl.ds(pl.multiple_of(m * width, width), width)
        body(
            model,
            [pl.ds(pl.multiple_of((m * expand + e) * width, width), width) for e in range(expand)],
        )


def forward_kernel(counts, *refs):
    own, theirs, rest = split(refs, counts)
    up, down = rest[:2]
    base, sent = rest[-2:]
    width, columns = up.shape[1], base.shape[1]

    def body(model, blocks):
        x = jnp.concatenate([columns_of(own, model), columns_of(theirs, model)], axis=1)
        kept = x[:, :width].astype(F32)
        away = jnp.zeros((x.shape[0], width), F32)
        for block in blocks:
            pre = mm(x, up[:, :, block].reshape(2 * width, width), (1, 0))
            hidden = (0.5 * pre * (1.0 + gate(pre))).astype(BF16)
            kept = kept + mm(hidden, down[0, block, :], (1, 0))
            away = away + mm(hidden, down[1, block, :], (1, 0))
        base[:, model] = kept
        sent[:, model] = away.astype(BF16)

    over_blocks(width, columns, up.shape[2] // columns, body)


def backward_kernel(counts, *refs):
    own_x, their_x, own_g, their_g, rest = split(refs, counts)
    up, down = rest[:2]
    base, sent, hidden_out, grad_pre_out = rest[-4:]
    width, columns = up.shape[1], base.shape[1]

    def body(model, blocks):
        x = jnp.concatenate([columns_of(own_x, model), columns_of(their_x, model)], axis=1)
        own, theirs = columns_of(own_g, model), columns_of(their_g, model)
        kept = own.astype(F32)
        away = jnp.zeros((x.shape[0], width), F32)
        for block in blocks:
            pre = mm(x, up[:, :, block].reshape(2 * width, width), (1, 0))
            grad_hidden = mm(own, down[0, block, :], (1, 1)) + mm(theirs, down[1, block, :], (1, 1))
            t = gate(pre)
            half = 0.5 * (1.0 + t)
            slope = half + 0.5 * pre * (1.0 - t * t) * (
                TANH_SCALE * (1.0 + 3.0 * CUBIC * (pre * pre))
            )
            grad_pre = (grad_hidden * slope).astype(BF16)
            kept = kept + mm(grad_pre, up[0, :, block], (1, 1))
            away = away + mm(grad_pre, up[1, :, block], (1, 1))
            hidden_out[:, block] = (pre * half).astype(BF16)
            grad_pre_out[:, block] = grad_pre
        base[:, model] = kept
        sent[:, model] = away.astype(BF16)

    over_blocks(width, columns, up.shape[2] // columns, body)


def in_vmem(kernel, rows, others, outs, cost, after=()):
    flat = [a for group in rows for a in group]
    vmem = pl.BlockSpec(memory_space=pltpu.VMEM)
    return pl.pallas_call(
        lambda *refs: kernel([len(group) for group in rows], *refs),
        in_specs=[vmem] * (len(flat) + len(others))
        + [pl.BlockSpec(memory_space=pl.ANY)] * len(after),
        out_specs=[vmem] * len(outs),
        out_shape=outs,
        compiler_params=pltpu.CompilerParams(vmem_limit_bytes=LIMIT * 2**20),
        cost_estimate=pl.CostEstimate(flops=cost, bytes_accessed=0, transcendentals=0),
    )(*flat, *others, *after)


def load(args, after=()):
    def kernel(*refs):
        sems = refs[-1]
        copies = [
            pltpu.make_async_copy(refs[i], refs[len(args) + len(after) + i], sems.at[i])
            for i in range(len(args))
        ]
        for copy in copies:
            copy.start()
        for copy in copies:
            copy.wait()

    return pl.pallas_call(
        kernel,
        in_specs=[pl.BlockSpec(memory_space=pl.ANY)] * (len(args) + len(after)),
        out_specs=[pl.BlockSpec(memory_space=pltpu.VMEM)] * len(args),
        out_shape=[jax.ShapeDtypeStruct(a.shape, a.dtype) for a in args],
        scratch_shapes=[pltpu.SemaphoreType.DMA((len(args),))],
        compiler_params=pltpu.CompilerParams(vmem_limit_bytes=2 * 2**20),
        cost_estimate=pl.CostEstimate(flops=0, bytes_accessed=0, transcendentals=0),
    )(*args, *after)


def weight_kernel(counts, expand, *refs):
    own_x, their_x, own_g, their_g, rest = split(refs, counts)
    hidden, grad_pre = rest[:2]
    up_grad, down_grad = rest[-2:]
    width = up_grad.shape[1]
    x = jnp.concatenate([rows_of(own_x), rows_of(their_x)], axis=1)
    g = jnp.concatenate([rows_of(own_g), rows_of(their_g)], axis=1)
    for e in range(expand):
        block = slice(e * width, (e + 1) * width)
        down_step = mm(hidden[:, block], g, (0, 0)).astype(BF16)
        down_grad[0, block, :] = down_step[:, :width]
        down_grad[1, block, :] = down_step[:, width:]
        up_step = mm(x, grad_pre[:, block], (0, 0)).astype(BF16)
        up_grad[0, :, block] = up_step[:width]
        up_grad[1, :, block] = up_step[width:]


def run(kernel, rows, others, outs, width, cost, after=()):
    flat = [a for group in rows for a in group]
    model_local = flat[0].shape[1] // width

    def spec(a):
        if len(a.shape) == 2:
            return pl.BlockSpec((a.shape[0], a.shape[1] // model_local), lambda m: (0, m))
        if a.shape[2] == width:
            return pl.BlockSpec((a.shape[0], a.shape[1] // model_local, width), lambda m: (0, m, 0))
        return pl.BlockSpec((a.shape[0], width, a.shape[2] // model_local), lambda m: (0, 0, m))

    expand = max(max(a.shape) for a in others) // (width * model_local)
    return pl.pallas_call(
        lambda *refs: kernel([len(group) for group in rows], expand, *refs),
        grid=(model_local,),
        in_specs=[spec(a) for a in (*flat, *others)]
        + [pl.BlockSpec(memory_space=pl.ANY)] * len(after),
        out_specs=[spec(a) for a in outs],
        out_shape=outs,
        compiler_params=pltpu.CompilerParams(vmem_limit_bytes=20 * 2**20),
        cost_estimate=pl.CostEstimate(flops=cost, bytes_accessed=BYTES, transcendentals=0),
    )(*flat, *others, *after)


def finish(base, pieces, start, total, result=None, after=()):
    rows, columns = base.shape

    def kernel(*refs):
        base_ref, piece_refs = refs[0], refs[1 : 1 + len(pieces)]
        out, rounded, sem = refs[-3:]
        rounded[...] = (base_ref[...] + rows_of(piece_refs).astype(F32)).astype(BF16)
        copy = pltpu.make_async_copy(rounded, out.at[pl.ds(start, rows)], sem)
        copy.start()
        copy.wait()

    vmem, anywhere = pl.BlockSpec(memory_space=pltpu.VMEM), pl.BlockSpec(memory_space=pl.ANY)
    rest = after if result is None else (result, *after)
    return pl.pallas_call(
        kernel,
        in_specs=[vmem] * (1 + len(pieces)) + [anywhere] * len(rest),
        out_specs=anywhere,
        out_shape=jax.ShapeDtypeStruct((total, columns), BF16),
        scratch_shapes=[pltpu.VMEM((rows, columns), BF16), pltpu.SemaphoreType.DMA],
        input_output_aliases={} if result is None else {1 + len(pieces): 0},
        compiler_params=pltpu.CompilerParams(vmem_limit_bytes=8 * 2**20),
        cost_estimate=pl.CostEstimate(flops=0, bytes_accessed=0, transcendentals=0),
    )(base, *pieces, *rest)


def on_device(acts_prev, embedded, grads_next, loss_grad, up_weight, down_weight):
    up, down = up_weight[0], down_weight[0]
    levels = up.shape[0] - 1
    mask = lax.axis_size("tensor") >> levels
    factors, width, hidden_local = up.shape
    tokens, columns = acts_prev.shape
    half, quarter = tokens // 2, tokens // 4
    sections = lax.axis_size("section")
    first, last = 0, sections - 1

    crossed_g = exchanged(grads_next, mask, range(1, sections))
    crossed_loss = exchanged(loss_grad, mask, range(1))
    acts_a, acts_b = join([[(0, 0, half)], [(0, half, tokens - half)]], (acts_prev,), ())
    came_a = shifted(acts_a, 1)
    came_b = shifted(acts_b, 1)
    came_g = shifted(grads_next, -1)
    up, embedded = load((up, embedded), (acts_a,))
    own_a = pick(first, (embedded, 0), (came_a, 0), half)
    their_a = swapped(own_a, mask)
    down, loss_grad = load((down, loss_grad), (own_a,))
    own_b = pick(first, (embedded, half), (came_b, 0), tokens - half, (down,))
    their_b = swapped(own_b, mask)
    onward_g = lax.ppermute(
        pick(first, (crossed_loss, 0), (crossed_g, 0), tokens, (own_b,)),
        "section",
        [(s, (s - 1) % sections) for s in range(sections)],
    )
    own_g = pick(last, (loss_grad, 0), (came_g, 0), tokens, (own_b,), COST_G)

    def forward(own, theirs, cost, after):
        shape = own.shape
        return in_vmem(
            forward_kernel,
            ([own], [theirs]),
            (up, down),
            [jax.ShapeDtypeStruct(shape, F32), jax.ShapeDtypeStruct(shape, BF16)],
            cost,
            after,
        )

    base_a, sent_a = forward(own_a, their_a, COST_A, (own_b, own_g))
    arrived_a = swapped(sent_a, mask)
    base_b, sent_b = forward(own_b, their_b, COST_B, (sent_a,))
    arrived_b = swapped(sent_b, mask)
    rows = ([own_a, own_b], [their_a, their_b], [own_g], [onward_g])
    base_back, sent_back, hidden, grad_pre = in_vmem(
        backward_kernel,
        rows,
        (up, down),
        [
            jax.ShapeDtypeStruct((tokens, columns), F32),
            jax.ShapeDtypeStruct((tokens, columns), BF16),
            jax.ShapeDtypeStruct((tokens, hidden_local), BF16),
            jax.ShapeDtypeStruct((tokens, hidden_local), BF16),
        ],
        COST_BACK,
        (sent_b,),
    )
    arrived_back = [
        swapped(sent_back[i * quarter : (i + 1) * quarter], mask) for i in range(4)
    ]
    up_grad, down_grad = run(
        weight_kernel,
        rows,
        (hidden, grad_pre),
        [jax.ShapeDtypeStruct(w.shape, BF16) for w in (up, down)],
        width,
        0,
    )
    mixed = finish(base_a, [arrived_a], 0, tokens, None, (up_grad,))
    mixed = finish(base_b, [arrived_b], half, tokens, mixed)
    end = 3 * quarter
    input_grads = finish(base_back[:end], arrived_back[:3], 0, tokens, None, (mixed,))
    input_grads = finish(base_back[end:], arrived_back[3:], end, tokens, input_grads)
    return (mixed, input_grads, up_grad[None], down_grad[None])


def solution(mesh):
    in_specs = (
        P("section", "tensor"),
        P(None, "tensor"),
        P("section", "tensor"),
        P(None, "tensor"),
        P("section", None, None, "tensor"),
        P("section", None, "tensor", None),
    )
    out_specs = (
        P("section", "tensor"),
        P("section", "tensor"),
        P("section", None, None, "tensor"),
        P("section", None, "tensor", None),
    )
    return jax.shard_map(
        on_device, mesh=mesh, in_specs=in_specs, out_specs=out_specs, check_vma=False
    )
```

time: 163 us -> 96.9 us (0.59)
  waiting for transfers between devices: 66.4 us -> 29 us
  matrix products: 34.6 us -> 0 us
  Pallas kernels: 0 us -> 34.4 us
  local copies, waits for them, and re-layouts: 40.8 us -> 8.32 us
  starting transfers between devices: 13.4 us -> 23.9 us
  other arithmetic: 5.94 us -> 0 us
    ppermute x6 -> x14, waiting for transfers between devices: 66.4 us -> 29 us  [the longest x3 14.7 us: shifted(): return lax.ppermute(value, 'section', pairs)]
    dot_general x6 -> x0, matrix products: 34.6 us -> none  [the longest x1 9.44 us: on_device(): jnp.einsum('ktmq,kmepq->tmep', stacked_grads, down_shaped, preferred_elem...]
    pallas_call x0 -> x15, Pallas kernels: none -> 34.4 us  [the longest x3 21.9 us: in_vmem(): pl.pallas_call(lambda *refs: kernel([len(group) for group in rows], *refs...]
    another operation x5 -> x0, local copies, waits for them, and re-layouts: 14.1 us -> none  [the longest x1 7.82 us: on_device(): up_local.reshape(factors, block_width, model_local, expand, block_width)]
    convert_element_type x4 -> x0, local copies, waits for them, and re-layouts: 11 us -> none  [the longest x1 4.79 us: on_device(): down_grad_bits.reshape(factors, hidden_local * block_width, block_width)]
    ppermute x6 -> x14, starting transfers between devices: 13.4 us -> 23.9 us  [the longest x3 9.55 us: shifted(): return lax.ppermute(value, 'section', pairs)]
    unnamed x23 -> x14, local copies, waits for them, and re-layouts: 15.7 us -> 8.04 us
    add x2 -> x0, other arithmetic: 3.76 us -> none  [the longest x1 2.17 us: on_device(): back_sum = back_sum + arrived.astype(jnp.float32)]
  transfers between devices with their start and end apart: 6 -> 14, of which waited for: 6 -> 6; matrix products, arithmetic and copies ran while one was open for 27% -> 0% of each run, Pallas kernels for 0% -> 35%
where the time goes in v3:
time: 96.9 us; the launch traced here: 96.6 us
  Pallas kernels  34.4 us (36%)
  waiting for transfers between devices  29 us (30%)
  starting transfers between devices  23.9 us (25%)
  local copies, waits for them, and re-layouts  8.32 us (9%)
    pallas_call x3, Pallas kernels, in_vmem(): pl.pallas_call(lambda *refs: kernel([len(group) for group in rows], *refs...  21.9 us
    ppermute x3, waiting for transfers between devices, shifted(): return lax.ppermute(value, 'section', pairs)  14.7 us
    ppermute x8, waiting for transfers between devices, swapped(): return lax.ppermute(value, 'tensor', pairs)  13.8 us
    ppermute x3, starting transfers between devices, shifted(): return lax.ppermute(value, 'section', pairs)  9.55 us
    unnamed x14, local copies, waits for them, and re-layouts  8.04 us
    pallas_call x1, Pallas kernels, run(): pl.pallas_call(lambda *refs: kernel([len(group) for group in rows], expan...  7.8 us
    ppermute x8, starting transfers between devices, swapped(): return lax.ppermute(value, 'tensor', pairs)  7 us
    ppermute x1, starting transfers between devices, on_device(): lax.ppermute(pick(first, (crossed_loss, 0), (crossed_g, 0), tokens, (own_...  4.36 us
  transfers between devices with their start and end apart: 14, of which 6 were waited for; matrix products, arithmetic and copies ran while one was open for 0% of the time, Pallas kernels for 35%

profile of v3, /device:TPU:0, one launch (start us, length us, event | category | flops | bytes accessed | tf_op | source)
XLA Modules:
  0.0 96.6 jit_solution(8922836593002697917)
XLA Ops:
  0.6 3.0 %collective-permute-start.7 = (bf16[512,1024]{1,0:T(8,128)(2,1)}, bf16[512,1024]{1,0:T(8,128)(2,1)S(1)}, u32[]{:S(2)}, u32[]{:S(2)}) collective-permute-start(bf16[512,1024]{1,0:T(8,128)(2,1)} %refs_1_.3), channel_id=1, source_target_pairs={{0,4},{1,5},{2,6},{3,7},{4,0},{5,1},{6,2},{7,3},{8,9},{9,8},{10,11... | collective-permute-start | bytes 3145736 | tf_op jit(solution)/shard_map/ppermute | solution.py:39
  3.7 0.0 collective-permute-start.8
  3.7 1.3 %collective-permute-start.4 = (bf16[512,1024]{1,0:T(8,128)(2,1)}, bf16[512,1024]{1,0:T(8,128)(2,1)S(1)}, u32[]{:S(2)}, u32[]{:S(2)}) collective-permute-start(bf16[512,1024]{1,0:T(8,128)(2,1)} %param.8), channel_id=1, source_target_pairs={{8,0},{16,8},{24,16},{9,1},{17,9},{25,17},{10,2},{18,10},{26,18},{... | collective-permute-start | bytes 3145736 | tf_op jit(solution)/shard_map/ppermute | solution.py:25
  5.0 1.2 %copy-done.4 = bf16[512,1024]{1,0:T(8,128)(2,1)S(1)} copy-done((bf16[512,1024]{1,0:T(8,128)(2,1)S(1)}, bf16[512,1024]{1,0:T(8,128)(2,1)}, u32[]{:S(2)}) %copy-start.4) | copy-done | bytes 1048600
  6.2 0.1 shard_map.93
  6.3 4.7 %collective-permute-start.1 = (bf16[256,1024]{1,0:T(8,128)(2,1)S(1)}, bf16[256,1024]{1,0:T(8,128)(2,1)S(1)}, u32[]{:S(2)}, u32[]{:S(2)}) collective-permute-start(bf16[256,1024]{1,0:T(8,128)(2,1)S(1)} %get-tuple-element.20.refs_2_), channel_id=1, source_target_pairs={{0,8},{8,16},{16,24},{1,9},{9,17},{17,25},{2,10},{10,18},{18,26},{... | collective-permute-start | bytes 1572872 | tf_op jit(solution)/shard_map/ppermute | solution.py:25
  11.0 3.6 %collective-permute-start = (bf16[256,1024]{1,0:T(8,128)(2,1)S(1)}, bf16[256,1024]{1,0:T(8,128)(2,1)S(1)}, u32[]{:S(2)}, u32[]{:S(2)}) collective-permute-start(bf16[256,1024]{1,0:T(8,128)(2,1)S(1)} %get-tuple-element.22), channel_id=1, source_target_pairs={{0,8},{8,16},{16,24},{1,9},{9,17},{17,25},{2,10},{10,18},{18,26},{... | collective-permute-start | bytes 1572872 | tf_op jit(solution)/shard_map/ppermute | solution.py:25
  14.5 0.0 copy-start.1
  14.6 2.2 %copy-done.1 = bf16[1,2,256,4096]{3,2,1,0:T(8,128)(2,1)S(1)} copy-done((bf16[1,2,256,4096]{3,2,1,0:T(8,128)(2,1)S(1)}, bf16[1,2,256,4096]{3,2,1,0:T(8,128)(2,1)}, u32[]{:S(2)}) %copy-start.1) | copy-done | bytes 4194328
  16.7 1.2 %copy-done.5 = bf16[512,1024]{1,0:T(8,128)(2,1)S(1)} copy-done((bf16[512,1024]{1,0:T(8,128)(2,1)S(1)}, bf16[512,1024]{1,0:T(8,128)(2,1)}, u32[]{:S(2)}) %copy-start.5) | copy-done | bytes 1048600
  18.0 0.4 shard_map.94
  18.3 4.9 %collective-permute-done.1.b = bf16[256,1024]{1,0:T(8,128)(2,1)S(1)} collective-permute-done((bf16[256,1024]{1,0:T(8,128)(2,1)S(1)}, bf16[256,1024]{1,0:T(8,128)(2,1)S(1)}, u32[]{:S(2)}, u32[]{:S(2)}) %collective-permute-start.1) | collective-permute-done | bytes 524320 | tf_op jit(solution)/shard_map/ppermute | solution.py:25
  23.2 0.1 shard_map.95.refs_2_.refs_0_
  23.3 0.2 collective-permute-start.3
  23.5 0.4 shard_map.96
  23.9 9.9 %collective-permute-done.b = bf16[256,1024]{1,0:T(8,128)(2,1)S(1)} collective-permute-done((bf16[256,1024]{1,0:T(8,128)(2,1)S(1)}, bf16[256,1024]{1,0:T(8,128)(2,1)S(1)}, u32[]{:S(2)}, u32[]{:S(2)}) %collective-permute-start) | collective-permute-done | bytes 524320 | tf_op jit(solution)/shard_map/ppermute | solution.py:25
  33.7 0.1 shard_map.97.rest_0_.refs_4_.refs_0_.refs_1_
  33.8 0.0 collective-permute-done.7.a
  33.8 0.1 shard_map.101
  33.9 4.4 %collective-permute-start.9 = (bf16[512,1024]{1,0:T(8,128)(2,1)S(1)}, bf16[512,1024]{1,0:T(8,128)(2,1)S(1)}, u32[]{:S(2)}, u32[]{:S(2)}) collective-permute-start(bf16[512,1024]{1,0:T(8,128)(2,1)S(1)} %shard_map.101), channel_id=1, source_target_pairs={{0,24},{8,0},{16,8},{24,16},{1,25},{9,1},{17,9},{25,17},{2,26},{10... | collective-permute-start | bytes 3145736 | tf_op jit(solution)/shard_map/ppermute | solution.py:296
  38.3 0.5 collective-permute-start.2
  38.8 0.0 collective-permute-done.4.b
  38.8 0.1 shard_map.98.refs_5_.refs_4_
  38.9 5.6 %shard_map.99 = (f32[256,1024]{1,0:T(8,128)S(1)}, bf16[256,1024]{1,0:T(8,128)(2,1)S(1)}) custom-call(bf16[256,1024]{1,0:T(8,128)(2,1)S(1)} %shard_map.95.refs_2_.refs_0_, bf16[256,1024]{1,0:T(8,128)(2,1)S(1)} %collective-permute-done.3.refs_1_.refs_2_, bf16[2,256,4096]{2,1,0:T(8,128)(2,1)S(1)} %get-tuple-element.24.refs_2_.refs_6_, ...), custom_call_target="tpu_custom_call" | custom-call | flops 3000000000 | tf_op jit(solution)/shard_map/pallas_call | solution.py:174
  44.6 1.6 %collective-permute-start.6 = (bf16[256,1024]{1,0:T(8,128)(2,1)S(1)}, bf16[256,1024]{1,0:T(8,128)(2,1)S(1)}, u32[]{:S(2)}, u32[]{:S(2)}) collective-permute-start(bf16[256,1024]{1,0:T(8,128)(2,1)S(1)} %get-tuple-element.26.refs_4_), channel_id=1, source_target_pairs={{0,4},{1,5},{2,6},{3,7},{4,0},{5,1},{6,2},{7,3},{8,12},{9,13},{10,... | collective-permute-start | bytes 1572872 | tf_op jit(solution)/shard_map/ppermute | solution.py:30
  46.1 7.0 %collective-permute-done.2.refs_1_.refs_3_ = bf16[256,1024]{1,0:T(8,128)(2,1)S(1)} collective-permute-done((bf16[256,1024]{1,0:T(8,128)(2,1)S(1)}, bf16[256,1024]{1,0:T(8,128)(2,1)S(1)}, u32[]{:S(2)}, u32[]{:S(2)}) %collective-permute-start.2) | collective-permute-done | bytes 524320 | tf_op jit(solution)/shard_map/ppermute | solution.py:30
  53.2 5.6 %shard_map.100 = (f32[256,1024]{1,0:T(8,128)S(1)}, bf16[256,1024]{1,0:T(8,128)(2,1)S(1)}) custom-call(bf16[256,1024]{1,0:T(8,128)(2,1)S(1)} %shard_map.97.rest_0_.refs_4_.refs_0_.refs_1_, bf16[256,1024]{1,0:T(8,128)(2,1)S(1)} %collective-permute-done.2.refs_1_.refs_3_, bf16[2,256,4096]{2,1,0:T(8,128)(2,1)S(1)} %get-tuple-element.24.refs_2_.refs_6_, ...), custom_call_target="tpu_custom_call" | custom-call | flops 4000000000 | tf_op jit(solution)/shard_map/pallas_call | solution.py:174
  58.8 0.6 collective-permute-start.5
  59.3 0.5 collective-permute-done.9.refs_5_
  59.9 10.7 %shard_map.102 = (f32[512,1024]{1,0:T(8,128)S(1)}, bf16[512,1024]{1,0:T(8,128)(2,1)S(1)}, bf16[512,4096]{1,0:T(8,128)(2,1)S(1)}, bf16[512,4096]{1,0:T(8,128)(2,1)S(1)}) custom-call(bf16[256,1024]{1,0:T(8,128)(2,1)S(1)} %shard_map.95.refs_2_.refs_0_, bf16[256,1024]{1,0:T(8,128)(2,1)S(1)} %shard_map.97.rest_0_.refs_4_.refs_0_.refs_1_, ...), custom_call_target="tpu_custom_call" | custom-call | flops 6000000000 | tf_op jit(solution)/shard_map/pallas_call | solution.py:174
  70.6 0.1 fusion
  70.6 1.0 %collective-permute-start.11 = (bf16[128,1024]{1,0:T(8,128)(2,1)S(1)}, bf16[128,1024]{1,0:T(8,128)(2,1)S(1)}, u32[]{:S(2)}, u32[]{:S(2)}) collective-permute-start(bf16[128,1024]{1,0:T(8,128)(2,1)S(1)} %get-tuple-element.38), channel_id=1, source_target_pairs={{0,4},{1,5},{2,6},{3,7},{4,0},{5,1},{6,2},{7,3},{8,12},{9,13},{10,... | collective-permute-start | bytes 786440 | tf_op jit(solution)/shard_map/ppermute | solution.py:30
  71.7 1.1 %collective-permute-start.12 = (bf16[128,1024]{1,0:T(8,128)(2,1)S(1)}, bf16[128,1024]{1,0:T(8,128)(2,1)S(1)}, u32[]{:S(2)}, u32[]{:S(2)}) collective-permute-start(bf16[128,1024]{1,0:T(8,128)(2,1)S(1)} %get-tuple-element.37), channel_id=1, source_target_pairs={{0,4},{1,5},{2,6},{3,7},{4,0},{5,1},{6,2},{7,3},{8,12},{9,13},{10,... | collective-permute-start | bytes 786440 | tf_op jit(solution)/shard_map/ppermute | solution.py:30
  72.7 1.0 collective-permute-start.13
  73.7 0.0 collective-permute-done.6.refs_1_
  73.7 1.1 %collective-permute-start.10 = (bf16[128,1024]{1,0:T(8,128)(2,1)S(1)}, bf16[128,1024]{1,0:T(8,128)(2,1)S(1)}, u32[]{:S(2)}, u32[]{:S(2)}) collective-permute-start(bf16[128,1024]{1,0:T(8,128)(2,1)S(1)} %get-tuple-element.39), channel_id=1, source_target_pairs={{0,4},{1,5},{2,6},{3,7},{4,0},{5,1},{6,2},{7,3},{8,12},{9,13},{10,... | collective-permute-start | bytes 786440 | tf_op jit(solution)/shard_map/ppermute | solution.py:30
  74.8 0.2 slice.20.refs_0_
  75.0 7.8 %shard_map.103 = (bf16[2,256,4096]{2,1,0:T(8,128)(2,1)}, bf16[2,4096,256]{2,1,0:T(8,128)(2,1)}) custom-call(bf16[256,1024]{1,0:T(8,128)(2,1)S(1)} %shard_map.95.refs_2_.refs_0_, bf16[256,1024]{1,0:T(8,128)(2,1)S(1)} %shard_map.97.rest_0_.refs_4_.refs_0_.refs_1_, bf16[256,1024]{1,0:T(8,128)(2,1)S(1)} %collective-permute-done.3.refs_1_.refs_2_, ...), custom_call_target="tpu_custom_call" | custom-call | bytes 8388608 | tf_op jit(solution)/shard_map/pallas_call | solution.py:237
  82.8 2.2 %copy-done.3 = bf16[2,256,4096]{2,1,0:T(8,128)(2,1)S(1)} copy-done((bf16[2,256,4096]{2,1,0:T(8,128)(2,1)S(1)}, bf16[2,256,4096]{2,1,0:T(8,128)(2,1)}, u32[]{:S(2)}) %copy-start.3) | copy-done | bytes 4194328
  85.0 0.9 shard_map.104.refs_2_
  85.9 0.0 collective-permute-done.5.refs_1_
  85.9 0.9 shard_map.105.refs_4_
  86.8 0.0 collective-permute-done.11.refs_1_
  86.8 5.3 %collective-permute-done.13.refs_3_ = bf16[128,1024]{1,0:T(8,128)(2,1)S(1)} collective-permute-done((bf16[128,1024]{1,0:T(8,128)(2,1)S(1)}, bf16[128,1024]{1,0:T(8,128)(2,1)S(1)}, u32[]{:S(2)}, u32[]{:S(2)}) %collective-permute-start.13) | collective-permute-done | bytes 262176 | tf_op jit(solution)/shard_map/ppermute | solution.py:30
  92.1 1.2 %copy-done = bf16[512,1024]{1,0:T(8,128)(2,1)S(1)} copy-done((bf16[512,1024]{1,0:T(8,128)(2,1)S(1)}, bf16[512,1024]{1,0:T(8,128)(2,1)}, u32[]{:S(2)}) %copy-start) | copy-done | bytes 1048600
  93.3 1.0 %shard_map.106.refs_2_ = bf16[512,1024]{1,0:T(8,128)(2,1)} custom-call(f32[384,1024]{1,0:T(8,128)S(1)} %slice.20.refs_0_, bf16[128,1024]{1,0:T(8,128)(2,1)S(1)} %collective-permute-done.11.refs_1_, bf16[128,1024]{1,0:T(8,128)(2,1)S(1)} %collective-permute-done.12.refs_2_, bf16[128,1024]{1,0:T(8,128)(2,1)S(1)} %collective-permute-done.13.refs_3_, ...), custom_call_target="tpu_custom_call" | custom-call | tf_op jit(solution)/shard_map/pallas_call | solution.py:262
  94.3 1.5 %collective-permute-done.10.refs_1_ = bf16[128,1024]{1,0:T(8,128)(2,1)S(1)} collective-permute-done((bf16[128,1024]{1,0:T(8,128)(2,1)S(1)}, bf16[128,1024]{1,0:T(8,128)(2,1)S(1)}, u32[]{:S(2)}, u32[]{:S(2)}) %collective-permute-start.10) | collective-permute-done | bytes 262176 | tf_op jit(solution)/shard_map/ppermute | solution.py:30
  95.8 0.8 shard_map.107
  (12 shorter events, 0.1 us)
Async XLA Ops:
  0.6 33.2 %collective-permute-start.7 = (bf16[512,1024]{1,0:T(8,128)(2,1)}, bf16[512,1024]{1,0:T(8,128)(2,1)S(1)}, u32[]{:S(2)}, u32[]{:S(2)}) collective-permute-start(bf16[512,1024]{1,0:T(8,128)(2,1)} %refs_1_.3), channel_id=1, source_target_pairs={{0,4},{1,5},{2,6},{3,7},{4,0},{5,1},{6,2},{7,3},{8,9},{9,8},{10,11... | collective-permute-start | bytes 3145736 | tf_op jit(solution)/shard_map/ppermute | solution.py:39
  3.7 30.1 %collective-permute-start.8 = (bf16[512,1024]{1,0:T(8,128)(2,1)}, bf16[512,1024]{1,0:T(8,128)(2,1)S(1)}, u32[]{:S(2)}, u32[]{:S(2)}) collective-permute-start(bf16[512,1024]{1,0:T(8,128)(2,1)} %param.8), channel_id=1, source_target_pairs={{0,1},{1,0},{2,3},{3,2},{4,5},{5,4},{6,7},{7,6},{8,12},{9,13},{10,... | collective-permute-start | bytes 3145736 | tf_op jit(solution)/shard_map/ppermute | solution.py:39
  3.7 35.1 %collective-permute-start.4 = (bf16[512,1024]{1,0:T(8,128)(2,1)}, bf16[512,1024]{1,0:T(8,128)(2,1)S(1)}, u32[]{:S(2)}, u32[]{:S(2)}) collective-permute-start(bf16[512,1024]{1,0:T(8,128)(2,1)} %param.8), channel_id=1, source_target_pairs={{8,0},{16,8},{24,16},{9,1},{17,9},{25,17},{10,2},{18,10},{26,18},{... | collective-permute-start | bytes 3145736 | tf_op jit(solution)/shard_map/ppermute | solution.py:25
  5.0 1.2 %copy-start.4 = (bf16[512,1024]{1,0:T(8,128)(2,1)S(1)}, bf16[512,1024]{1,0:T(8,128)(2,1)}, u32[]{:S(2)}) copy-start(bf16[512,1024]{1,0:T(8,128)(2,1)} %refs_0_.1) | copy-start | bytes 3145732
  6.2 17.3 %copy-start.6 = (bf16[512,1024]{1,0:T(8,128)(2,1)S(1)}, bf16[512,1024]{1,0:T(8,128)(2,1)}, u32[]{:S(2)}) copy-start(bf16[512,1024]{1,0:T(8,128)(2,1)} %refs_1_.3) | copy-start | bytes 3145732
  6.3 16.9 %collective-permute-start.1 = (bf16[256,1024]{1,0:T(8,128)(2,1)S(1)}, bf16[256,1024]{1,0:T(8,128)(2,1)S(1)}, u32[]{:S(2)}, u32[]{:S(2)}) collective-permute-start(bf16[256,1024]{1,0:T(8,128)(2,1)S(1)} %get-tuple-element.20.refs_2_), channel_id=1, source_target_pairs={{0,8},{8,16},{16,24},{1,9},{9,17},{17,25},{2,10},{10,18},{18,26},{... | collective-permute-start | bytes 1572872 | tf_op jit(solution)/shard_map/ppermute | solution.py:25
  11.0 22.8 %collective-permute-start = (bf16[256,1024]{1,0:T(8,128)(2,1)S(1)}, bf16[256,1024]{1,0:T(8,128)(2,1)S(1)}, u32[]{:S(2)}, u32[]{:S(2)}) collective-permute-start(bf16[256,1024]{1,0:T(8,128)(2,1)S(1)} %get-tuple-element.22), channel_id=1, source_target_pairs={{0,8},{8,16},{16,24},{1,9},{9,17},{17,25},{2,10},{10,18},{18,26},{... | collective-permute-start | bytes 1572872 | tf_op jit(solution)/shard_map/ppermute | solution.py:25
  14.5 2.2 %copy-start.1 = (bf16[1,2,256,4096]{3,2,1,0:T(8,128)(2,1)S(1)}, bf16[1,2,256,4096]{3,2,1,0:T(8,128)(2,1)}, u32[]{:S(2)}) copy-start(bf16[1,2,256,4096]{3,2,1,0:T(8,128)(2,1)} %param.10) | copy-start | bytes 12582916
  16.7 1.2 %copy-start.5 = (bf16[512,1024]{1,0:T(8,128)(2,1)S(1)}, bf16[512,1024]{1,0:T(8,128)(2,1)}, u32[]{:S(2)}) copy-start(bf16[512,1024]{1,0:T(8,128)(2,1)} %refs_1_.2) | copy-start | bytes 3145732
  18.0 5.5 %copy-start.2 = (bf16[1,2,4096,256]{3,2,1,0:T(8,128)(2,1)S(1)}, bf16[1,2,4096,256]{3,2,1,0:T(8,128)(2,1)}, u32[]{:S(2)}) copy-start(bf16[1,2,4096,256]{3,2,1,0:T(8,128)(2,1)} %param.11) | copy-start | bytes 12582916
  23.3 15.7 %collective-permute-start.3 = (bf16[256,1024]{1,0:T(8,128)(2,1)S(1)}, bf16[256,1024]{1,0:T(8,128)(2,1)S(1)}, u32[]{:S(2)}, u32[]{:S(2)}) collective-permute-start(bf16[256,1024]{1,0:T(8,128)(2,1)S(1)} %shard_map.95.refs_2_.refs_0_), channel_id=1, source_target_pairs={{0,4},{1,5},{2,6},{3,7},{4,0},{5,1},{6,2},{7,3},{8,12},{9,13},{10,... | collective-permute-start | bytes 1572872 | tf_op jit(solution)/shard_map/ppermute | solution.py:30
  33.9 26.0 %collective-permute-start.9 = (bf16[512,1024]{1,0:T(8,128)(2,1)S(1)}, bf16[512,1024]{1,0:T(8,128)(2,1)S(1)}, u32[]{:S(2)}, u32[]{:S(2)}) collective-permute-start(bf16[512,1024]{1,0:T(8,128)(2,1)S(1)} %shard_map.101), channel_id=1, source_target_pairs={{0,24},{8,0},{16,8},{24,16},{1,25},{9,1},{17,9},{25,17},{2,26},{10... | collective-permute-start | bytes 3145736 | tf_op jit(solution)/shard_map/ppermute | solution.py:296
  38.3 14.9 %collective-permute-start.2 = (bf16[256,1024]{1,0:T(8,128)(2,1)S(1)}, bf16[256,1024]{1,0:T(8,128)(2,1)S(1)}, u32[]{:S(2)}, u32[]{:S(2)}) collective-permute-start(bf16[256,1024]{1,0:T(8,128)(2,1)S(1)} %shard_map.97.rest_0_.refs_4_.refs_0_.refs_1_), channel_id=1, source_target_pairs={{0,4},{1,5},{2,6},{3,7},{4,0},{5,1},{6,2},{7,3},{8,12},{9,13},{10,... | collective-permute-start | bytes 1572872 | tf_op jit(solution)/shard_map/ppermute | solution.py:30
  44.6 29.1 %collective-permute-start.6 = (bf16[256,1024]{1,0:T(8,128)(2,1)S(1)}, bf16[256,1024]{1,0:T(8,128)(2,1)S(1)}, u32[]{:S(2)}, u32[]{:S(2)}) collective-permute-start(bf16[256,1024]{1,0:T(8,128)(2,1)S(1)} %get-tuple-element.26.refs_4_), channel_id=1, source_target_pairs={{0,4},{1,5},{2,6},{3,7},{4,0},{5,1},{6,2},{7,3},{8,12},{9,13},{10,... | collective-permute-start | bytes 1572872 | tf_op jit(solution)/shard_map/ppermute | solution.py:30
  58.8 27.1 %collective-permute-start.5 = (bf16[256,1024]{1,0:T(8,128)(2,1)S(1)}, bf16[256,1024]{1,0:T(8,128)(2,1)S(1)}, u32[]{:S(2)}, u32[]{:S(2)}) collective-permute-start(bf16[256,1024]{1,0:T(8,128)(2,1)S(1)} %get-tuple-element.28.refs_8_), channel_id=1, source_target_pairs={{0,4},{1,5},{2,6},{3,7},{4,0},{5,1},{6,2},{7,3},{8,12},{9,13},{10,... | collective-permute-start | bytes 1572872 | tf_op jit(solution)/shard_map/ppermute | solution.py:30
  70.6 16.1 %collective-permute-start.11 = (bf16[128,1024]{1,0:T(8,128)(2,1)S(1)}, bf16[128,1024]{1,0:T(8,128)(2,1)S(1)}, u32[]{:S(2)}, u32[]{:S(2)}) collective-permute-start(bf16[128,1024]{1,0:T(8,128)(2,1)S(1)} %get-tuple-element.38), channel_id=1, source_target_pairs={{0,4},{1,5},{2,6},{3,7},{4,0},{5,1},{6,2},{7,3},{8,12},{9,13},{10,... | collective-permute-start | bytes 786440 | tf_op jit(solution)/shard_map/ppermute | solution.py:30
  71.7 15.1 %collective-permute-start.12 = (bf16[128,1024]{1,0:T(8,128)(2,1)S(1)}, bf16[128,1024]{1,0:T(8,128)(2,1)S(1)}, u32[]{:S(2)}, u32[]{:S(2)}) collective-permute-start(bf16[128,1024]{1,0:T(8,128)(2,1)S(1)} %get-tuple-element.37), channel_id=1, source_target_pairs={{0,4},{1,5},{2,6},{3,7},{4,0},{5,1},{6,2},{7,3},{8,12},{9,13},{10,... | collective-permute-start | bytes 786440 | tf_op jit(solution)/shard_map/ppermute | solution.py:30
  72.7 19.3 %collective-permute-start.13 = (bf16[128,1024]{1,0:T(8,128)(2,1)S(1)}, bf16[128,1024]{1,0:T(8,128)(2,1)S(1)}, u32[]{:S(2)}, u32[]{:S(2)}) collective-permute-start(bf16[128,1024]{1,0:T(8,128)(2,1)S(1)} %get-tuple-element.36), channel_id=1, source_target_pairs={{0,4},{1,5},{2,6},{3,7},{4,0},{5,1},{6,2},{7,3},{8,12},{9,13},{10,... | collective-permute-start | bytes 786440 | tf_op jit(solution)/shard_map/ppermute | solution.py:30
  73.7 22.1 %collective-permute-start.10 = (bf16[128,1024]{1,0:T(8,128)(2,1)S(1)}, bf16[128,1024]{1,0:T(8,128)(2,1)S(1)}, u32[]{:S(2)}, u32[]{:S(2)}) collective-permute-start(bf16[128,1024]{1,0:T(8,128)(2,1)S(1)} %get-tuple-element.39), channel_id=1, source_target_pairs={{0,4},{1,5},{2,6},{3,7},{4,0},{5,1},{6,2},{7,3},{8,12},{9,13},{10,... | collective-permute-start | bytes 786440 | tf_op jit(solution)/shard_map/ppermute | solution.py:30
  82.8 2.2 %copy-start.3 = (bf16[2,256,4096]{2,1,0:T(8,128)(2,1)S(1)}, bf16[2,256,4096]{2,1,0:T(8,128)(2,1)}, u32[]{:S(2)}) copy-start(bf16[2,256,4096]{2,1,0:T(8,128)(2,1)} %get-tuple-element.32.refs_2_) | copy-start | bytes 12582916
  92.1 1.2 %copy-start = (bf16[512,1024]{1,0:T(8,128)(2,1)S(1)}, bf16[512,1024]{1,0:T(8,128)(2,1)}, u32[]{:S(2)}) copy-start(bf16[512,1024]{1,0:T(8,128)(2,1)} %shard_map.105.refs_4_) | copy-start | bytes 3145732

commit v4 on v3

--- a/solution.py
+++ b/solution.py
@@ -9,7 +9,7 @@
 
 COST_A = 3 * 10**9
 COST_G = 10**9
-COST_B = 4 * 10**9
+COST_B = 7 * 10**9
 COST_BACK = 6 * 10**9
 LIMIT = 8
 BYTES = 8 * 2**20

time: 96.9 us -> 95.6 us (0.987)
  waiting for transfers between devices: 29 us -> 25.6 us
  starting transfers between devices: 23.9 us -> 26.1 us
    ppermute x8, waiting for transfers between devices: 13.8 us -> 8.73 us  [swapped(): return lax.ppermute(value, 'tensor', pairs)]
    ppermute x8, starting transfers between devices: 7 us -> 8.74 us  [swapped(): return lax.ppermute(value, 'tensor', pairs)]
    ppermute x1, waiting for transfers between devices: 0.55 us -> 2.09 us  [on_device(): lax.ppermute(pick(first, (crossed_loss, 0), (crossed_g, 0), tokens, (own_...]
  transfers between devices with their start and end apart: 14 -> 14, of which waited for: 6 -> 7; matrix products, arithmetic and copies ran while one was open for 0% -> 0% of each run, Pallas kernels for 35% -> 35%
where the time goes in v4:
time: 95.6 us; the launch traced here: 95.2 us
  Pallas kernels  34.4 us (36%)
  starting transfers between devices  26.1 us (27%)
  waiting for transfers between devices  25.6 us (27%)
  local copies, waits for them, and re-layouts  8.32 us (9%)
    pallas_call x3, Pallas kernels, in_vmem(): pl.pallas_call(lambda *refs: kernel([len(group) for group in rows], *refs...  21.9 us
    ppermute x3, waiting for transfers between devices, shifted(): return lax.ppermute(value, 'section', pairs)  14.7 us
    ppermute x3, starting transfers between devices, shifted(): return lax.ppermute(value, 'section', pairs)  9.55 us
    ppermute x8, starting transfers between devices, swapped(): return lax.ppermute(value, 'tensor', pairs)  8.74 us
    ppermute x8, waiting for transfers between devices, swapped(): return lax.ppermute(value, 'tensor', pairs)  8.73 us
    unnamed x14, local copies, waits for them, and re-layouts  8.04 us
    pallas_call x1, Pallas kernels, run(): pl.pallas_call(lambda *refs: kernel([len(group) for group in rows], expan...  7.8 us
    ppermute x1, starting transfers between devices, on_device(): lax.ppermute(pick(first, (crossed_loss, 0), (crossed_g, 0), tokens, (own_...  4.78 us
  transfers between devices with their start and end apart: 14, of which 7 were waited for; matrix products, arithmetic and copies ran while one was open for 0% of the time, Pallas kernels for 35%

profile of v4, /device:TPU:0, one launch (start us, length us, event | category | flops | bytes accessed | tf_op | source)
XLA Modules:
  0.0 95.2 jit_solution(7097589642951357864)
XLA Ops:
  0.6 3.0 %collective-permute-start.7 = (bf16[512,1024]{1,0:T(8,128)(2,1)}, bf16[512,1024]{1,0:T(8,128)(2,1)S(1)}, u32[]{:S(2)}, u32[]{:S(2)}) collective-permute-start(bf16[512,1024]{1,0:T(8,128)(2,1)} %refs_1_.3), channel_id=1, source_target_pairs={{0,4},{1,5},{2,6},{3,7},{4,0},{5,1},{6,2},{7,3},{8,9},{9,8},{10,11... | collective-permute-start | bytes 3145736 | tf_op jit(solution)/shard_map/ppermute | solution.py:39
  3.7 0.0 collective-permute-start.8
  3.7 1.3 %collective-permute-start.4 = (bf16[512,1024]{1,0:T(8,128)(2,1)}, bf16[512,1024]{1,0:T(8,128)(2,1)S(1)}, u32[]{:S(2)}, u32[]{:S(2)}) collective-permute-start(bf16[512,1024]{1,0:T(8,128)(2,1)} %param.8), channel_id=1, source_target_pairs={{8,0},{16,8},{24,16},{9,1},{17,9},{25,17},{10,2},{18,10},{26,18},{... | collective-permute-start | bytes 3145736 | tf_op jit(solution)/shard_map/ppermute | solution.py:25
  5.0 1.2 %copy-done.4 = bf16[512,1024]{1,0:T(8,128)(2,1)S(1)} copy-done((bf16[512,1024]{1,0:T(8,128)(2,1)S(1)}, bf16[512,1024]{1,0:T(8,128)(2,1)}, u32[]{:S(2)}) %copy-start.4) | copy-done | bytes 1048600
  6.2 0.1 shard_map.93
  6.3 4.7 %collective-permute-start.1 = (bf16[256,1024]{1,0:T(8,128)(2,1)S(1)}, bf16[256,1024]{1,0:T(8,128)(2,1)S(1)}, u32[]{:S(2)}, u32[]{:S(2)}) collective-permute-start(bf16[256,1024]{1,0:T(8,128)(2,1)S(1)} %get-tuple-element.20.refs_2_), channel_id=1, source_target_pairs={{0,8},{8,16},{16,24},{1,9},{9,17},{17,25},{2,10},{10,18},{18,26},{... | collective-permute-start | bytes 1572872 | tf_op jit(solution)/shard_map/ppermute | solution.py:25
  11.0 3.6 %collective-permute-start = (bf16[256,1024]{1,0:T(8,128)(2,1)S(1)}, bf16[256,1024]{1,0:T(8,128)(2,1)S(1)}, u32[]{:S(2)}, u32[]{:S(2)}) collective-permute-start(bf16[256,1024]{1,0:T(8,128)(2,1)S(1)} %get-tuple-element.22), channel_id=1, source_target_pairs={{0,8},{8,16},{16,24},{1,9},{9,17},{17,25},{2,10},{10,18},{18,26},{... | collective-permute-start | bytes 1572872 | tf_op jit(solution)/shard_map/ppermute | solution.py:25
  14.5 0.0 copy-start.1
  14.6 2.2 %copy-done.1 = bf16[1,2,256,4096]{3,2,1,0:T(8,128)(2,1)S(1)} copy-done((bf16[1,2,256,4096]{3,2,1,0:T(8,128)(2,1)S(1)}, bf16[1,2,256,4096]{3,2,1,0:T(8,128)(2,1)}, u32[]{:S(2)}) %copy-start.1) | copy-done | bytes 4194328
  16.7 1.2 %copy-done.5 = bf16[512,1024]{1,0:T(8,128)(2,1)S(1)} copy-done((bf16[512,1024]{1,0:T(8,128)(2,1)S(1)}, bf16[512,1024]{1,0:T(8,128)(2,1)}, u32[]{:S(2)}) %copy-start.5) | copy-done | bytes 1048600
  18.0 0.4 shard_map.94
  18.3 4.9 %collective-permute-done.1.b = bf16[256,1024]{1,0:T(8,128)(2,1)S(1)} collective-permute-done((bf16[256,1024]{1,0:T(8,128)(2,1)S(1)}, bf16[256,1024]{1,0:T(8,128)(2,1)S(1)}, u32[]{:S(2)}, u32[]{:S(2)}) %collective-permute-start.1) | collective-permute-done | bytes 524320 | tf_op jit(solution)/shard_map/ppermute | solution.py:25
  23.2 0.1 shard_map.95.refs_2_.refs_0_
  23.3 0.2 collective-permute-start.3
  23.5 0.4 shard_map.96
  23.9 9.9 %collective-permute-done.b = bf16[256,1024]{1,0:T(8,128)(2,1)S(1)} collective-permute-done((bf16[256,1024]{1,0:T(8,128)(2,1)S(1)}, bf16[256,1024]{1,0:T(8,128)(2,1)S(1)}, u32[]{:S(2)}, u32[]{:S(2)}) %collective-permute-start) | collective-permute-done | bytes 524320 | tf_op jit(solution)/shard_map/ppermute | solution.py:25
  33.7 0.1 shard_map.97.rest_0_.refs_4_.refs_0_.refs_1_
  33.8 0.1 collective-permute-start.2
  33.9 0.0 collective-permute-done.7.a
  33.9 0.0 collective-permute-done.8.b
  33.9 0.1 shard_map.101
  34.1 4.8 %collective-permute-start.9 = (bf16[512,1024]{1,0:T(8,128)(2,1)S(1)}, bf16[512,1024]{1,0:T(8,128)(2,1)S(1)}, u32[]{:S(2)}, u32[]{:S(2)}) collective-permute-start(bf16[512,1024]{1,0:T(8,128)(2,1)S(1)} %shard_map.101), channel_id=1, source_target_pairs={{0,24},{8,0},{16,8},{24,16},{1,25},{9,1},{17,9},{25,17},{2,26},{10... | collective-permute-start | bytes 3145736 | tf_op jit(solution)/shard_map/ppermute | solution.py:296
  38.8 0.0 collective-permute-done.4.b
  38.8 0.1 shard_map.98.refs_5_.refs_4_
  39.0 0.1 collective-permute-done.3.refs_1_.refs_2_
  39.1 5.6 %shard_map.99 = (f32[256,1024]{1,0:T(8,128)S(1)}, bf16[256,1024]{1,0:T(8,128)(2,1)S(1)}) custom-call(bf16[256,1024]{1,0:T(8,128)(2,1)S(1)} %shard_map.95.refs_2_.refs_0_, bf16[256,1024]{1,0:T(8,128)(2,1)S(1)} %collective-permute-done.3.refs_1_.refs_2_, bf16[2,256,4096]{2,1,0:T(8,128)(2,1)S(1)} %get-tuple-element.24.refs_2_.refs_6_, ...), custom_call_target="tpu_custom_call" | custom-call | flops 3000000000 | tf_op jit(solution)/shard_map/pallas_call | solution.py:174
  44.7 2.1 %collective-permute-start.6 = (bf16[256,1024]{1,0:T(8,128)(2,1)S(1)}, bf16[256,1024]{1,0:T(8,128)(2,1)S(1)}, u32[]{:S(2)}, u32[]{:S(2)}) collective-permute-start(bf16[256,1024]{1,0:T(8,128)(2,1)S(1)} %get-tuple-element.26.refs_4_), channel_id=1, source_target_pairs={{0,4},{1,5},{2,6},{3,7},{4,0},{5,1},{6,2},{7,3},{8,12},{9,13},{10,... | collective-permute-start | bytes 1572872 | tf_op jit(solution)/shard_map/ppermute | solution.py:30
  46.8 3.5 %collective-permute-done.2.refs_1_.refs_3_ = bf16[256,1024]{1,0:T(8,128)(2,1)S(1)} collective-permute-done((bf16[256,1024]{1,0:T(8,128)(2,1)S(1)}, bf16[256,1024]{1,0:T(8,128)(2,1)S(1)}, u32[]{:S(2)}, u32[]{:S(2)}) %collective-permute-start.2) | collective-permute-done | bytes 524320 | tf_op jit(solution)/shard_map/ppermute | solution.py:30
  50.3 5.6 %shard_map.100 = (f32[256,1024]{1,0:T(8,128)S(1)}, bf16[256,1024]{1,0:T(8,128)(2,1)S(1)}) custom-call(bf16[256,1024]{1,0:T(8,128)(2,1)S(1)} %shard_map.97.rest_0_.refs_4_.refs_0_.refs_1_, bf16[256,1024]{1,0:T(8,128)(2,1)S(1)} %collective-permute-done.2.refs_1_.refs_3_, bf16[2,256,4096]{2,1,0:T(8,128)(2,1)S(1)} %get-tuple-element.24.refs_2_.refs_6_, ...), custom_call_target="tpu_custom_call" | custom-call | flops 7000000000 | tf_op jit(solution)/shard_map/pallas_call | solution.py:174
  55.9 2.1 %collective-permute-start.5 = (bf16[256,1024]{1,0:T(8,128)(2,1)S(1)}, bf16[256,1024]{1,0:T(8,128)(2,1)S(1)}, u32[]{:S(2)}, u32[]{:S(2)}) collective-permute-start(bf16[256,1024]{1,0:T(8,128)(2,1)S(1)} %get-tuple-element.28.refs_8_), channel_id=1, source_target_pairs={{0,4},{1,5},{2,6},{3,7},{4,0},{5,1},{6,2},{7,3},{8,12},{9,13},{10,... | collective-permute-start | bytes 1572872 | tf_op jit(solution)/shard_map/ppermute | solution.py:30
  58.1 2.1 %collective-permute-done.9.refs_5_ = bf16[512,1024]{1,0:T(8,128)(2,1)S(1)} collective-permute-done((bf16[512,1024]{1,0:T(8,128)(2,1)S(1)}, bf16[512,1024]{1,0:T(8,128)(2,1)S(1)}, u32[]{:S(2)}, u32[]{:S(2)}) %collective-permute-start.9) | collective-permute-done | bytes 1048608 | tf_op jit(solution)/shard_map/ppermute | solution.py:296
  60.2 10.7 %shard_map.102 = (f32[512,1024]{1,0:T(8,128)S(1)}, bf16[512,1024]{1,0:T(8,128)(2,1)S(1)}, bf16[512,4096]{1,0:T(8,128)(2,1)S(1)}, bf16[512,4096]{1,0:T(8,128)(2,1)S(1)}) custom-call(bf16[256,1024]{1,0:T(8,128)(2,1)S(1)} %shard_map.95.refs_2_.refs_0_, bf16[256,1024]{1,0:T(8,128)(2,1)S(1)} %shard_map.97.rest_0_.refs_4_.refs_0_.refs_1_, ...), custom_call_target="tpu_custom_call" | custom-call | flops 6000000000 | tf_op jit(solution)/shard_map/pallas_call | solution.py:174
  70.8 0.1 fusion
  70.9 1.6 %collective-permute-start.11 = (bf16[128,1024]{1,0:T(8,128)(2,1)S(1)}, bf16[128,1024]{1,0:T(8,128)(2,1)S(1)}, u32[]{:S(2)}, u32[]{:S(2)}) collective-permute-start(bf16[128,1024]{1,0:T(8,128)(2,1)S(1)} %get-tuple-element.38), channel_id=1, source_target_pairs={{0,4},{1,5},{2,6},{3,7},{4,0},{5,1},{6,2},{7,3},{8,12},{9,13},{10,... | collective-permute-start | bytes 786440 | tf_op jit(solution)/shard_map/ppermute | solution.py:30
  72.5 0.5 collective-permute-start.12
  73.0 1.5 %collective-permute-start.13 = (bf16[128,1024]{1,0:T(8,128)(2,1)S(1)}, bf16[128,1024]{1,0:T(8,128)(2,1)S(1)}, u32[]{:S(2)}, u32[]{:S(2)}) collective-permute-start(bf16[128,1024]{1,0:T(8,128)(2,1)S(1)} %get-tuple-element.36), channel_id=1, source_target_pairs={{0,4},{1,5},{2,6},{3,7},{4,0},{5,1},{6,2},{7,3},{8,12},{9,13},{10,... | collective-permute-start | bytes 786440 | tf_op jit(solution)/shard_map/ppermute | solution.py:30
  74.5 0.5 collective-permute-start.10
  75.0 0.2 slice.20.refs_0_
  75.3 7.8 %shard_map.103 = (bf16[2,256,4096]{2,1,0:T(8,128)(2,1)}, bf16[2,4096,256]{2,1,0:T(8,128)(2,1)}) custom-call(bf16[256,1024]{1,0:T(8,128)(2,1)S(1)} %shard_map.95.refs_2_.refs_0_, bf16[256,1024]{1,0:T(8,128)(2,1)S(1)} %shard_map.97.rest_0_.refs_4_.refs_0_.refs_1_, bf16[256,1024]{1,0:T(8,128)(2,1)S(1)} %collective-permute-done.3.refs_1_.refs_2_, ...), custom_call_target="tpu_custom_call" | custom-call | bytes 8388608 | tf_op jit(solution)/shard_map/pallas_call | solution.py:237
  83.1 2.2 %copy-done.3 = bf16[2,256,4096]{2,1,0:T(8,128)(2,1)S(1)} copy-done((bf16[2,256,4096]{2,1,0:T(8,128)(2,1)S(1)}, bf16[2,256,4096]{2,1,0:T(8,128)(2,1)}, u32[]{:S(2)}) %copy-start.3) | copy-done | bytes 4194328
  85.2 0.9 shard_map.104.refs_2_
  86.1 0.9 shard_map.105.refs_4_
  87.0 0.0 collective-permute-done.11.refs_1_
  87.1 4.4 %collective-permute-done.13.refs_3_ = bf16[128,1024]{1,0:T(8,128)(2,1)S(1)} collective-permute-done((bf16[128,1024]{1,0:T(8,128)(2,1)S(1)}, bf16[128,1024]{1,0:T(8,128)(2,1)S(1)}, u32[]{:S(2)}, u32[]{:S(2)}) %collective-permute-start.13) | collective-permute-done | bytes 262176 | tf_op jit(solution)/shard_map/ppermute | solution.py:30
  91.5 1.2 %copy-done = bf16[512,1024]{1,0:T(8,128)(2,1)S(1)} copy-done((bf16[512,1024]{1,0:T(8,128)(2,1)S(1)}, bf16[512,1024]{1,0:T(8,128)(2,1)}, u32[]{:S(2)}) %copy-start) | copy-done | bytes 1048600
  92.7 1.0 %shard_map.106.refs_2_ = bf16[512,1024]{1,0:T(8,128)(2,1)} custom-call(f32[384,1024]{1,0:T(8,128)S(1)} %slice.20.refs_0_, bf16[128,1024]{1,0:T(8,128)(2,1)S(1)} %collective-permute-done.11.refs_1_, bf16[128,1024]{1,0:T(8,128)(2,1)S(1)} %collective-permute-done.12.refs_2_, bf16[128,1024]{1,0:T(8,128)(2,1)S(1)} %collective-permute-done.13.refs_3_, ...), custom_call_target="tpu_custom_call" | custom-call | tf_op jit(solution)/shard_map/pallas_call | solution.py:262
  93.7 0.7 collective-permute-done.10.refs_1_
  94.4 0.8 shard_map.107
  (12 shorter events, 0.1 us)
Async XLA Ops:
  0.6 33.3 %collective-permute-start.7 = (bf16[512,1024]{1,0:T(8,128)(2,1)}, bf16[512,1024]{1,0:T(8,128)(2,1)S(1)}, u32[]{:S(2)}, u32[]{:S(2)}) collective-permute-start(bf16[512,1024]{1,0:T(8,128)(2,1)} %refs_1_.3), channel_id=1, source_target_pairs={{0,4},{1,5},{2,6},{3,7},{4,0},{5,1},{6,2},{7,3},{8,9},{9,8},{10,11... | collective-permute-start | bytes 3145736 | tf_op jit(solution)/shard_map/ppermute | solution.py:39
  3.7 30.3 %collective-permute-start.8 = (bf16[512,1024]{1,0:T(8,128)(2,1)}, bf16[512,1024]{1,0:T(8,128)(2,1)S(1)}, u32[]{:S(2)}, u32[]{:S(2)}) collective-permute-start(bf16[512,1024]{1,0:T(8,128)(2,1)} %param.8), channel_id=1, source_target_pairs={{0,1},{1,0},{2,3},{3,2},{4,5},{5,4},{6,7},{7,6},{8,12},{9,13},{10,... | collective-permute-start | bytes 3145736 | tf_op jit(solution)/shard_map/ppermute | solution.py:39
  3.7 35.2 %collective-permute-start.4 = (bf16[512,1024]{1,0:T(8,128)(2,1)}, bf16[512,1024]{1,0:T(8,128)(2,1)S(1)}, u32[]{:S(2)}, u32[]{:S(2)}) collective-permute-start(bf16[512,1024]{1,0:T(8,128)(2,1)} %param.8), channel_id=1, source_target_pairs={{8,0},{16,8},{24,16},{9,1},{17,9},{25,17},{10,2},{18,10},{26,18},{... | collective-permute-start | bytes 3145736 | tf_op jit(solution)/shard_map/ppermute | solution.py:25
  5.0 1.2 %copy-start.4 = (bf16[512,1024]{1,0:T(8,128)(2,1)S(1)}, bf16[512,1024]{1,0:T(8,128)(2,1)}, u32[]{:S(2)}) copy-start(bf16[512,1024]{1,0:T(8,128)(2,1)} %refs_0_.1) | copy-start | bytes 3145732
  6.2 17.3 %copy-start.6 = (bf16[512,1024]{1,0:T(8,128)(2,1)S(1)}, bf16[512,1024]{1,0:T(8,128)(2,1)}, u32[]{:S(2)}) copy-start(bf16[512,1024]{1,0:T(8,128)(2,1)} %refs_1_.3) | copy-start | bytes 3145732
  6.3 16.9 %collective-permute-start.1 = (bf16[256,1024]{1,0:T(8,128)(2,1)S(1)}, bf16[256,1024]{1,0:T(8,128)(2,1)S(1)}, u32[]{:S(2)}, u32[]{:S(2)}) collective-permute-start(bf16[256,1024]{1,0:T(8,128)(2,1)S(1)} %get-tuple-element.20.refs_2_), channel_id=1, source_target_pairs={{0,8},{8,16},{16,24},{1,9},{9,17},{17,25},{2,10},{10,18},{18,26},{... | collective-permute-start | bytes 1572872 | tf_op jit(solution)/shard_map/ppermute | solution.py:25
  11.0 22.8 %collective-permute-start = (bf16[256,1024]{1,0:T(8,128)(2,1)S(1)}, bf16[256,1024]{1,0:T(8,128)(2,1)S(1)}, u32[]{:S(2)}, u32[]{:S(2)}) collective-permute-start(bf16[256,1024]{1,0:T(8,128)(2,1)S(1)} %get-tuple-element.22), channel_id=1, source_target_pairs={{0,8},{8,16},{16,24},{1,9},{9,17},{17,25},{2,10},{10,18},{18,26},{... | collective-permute-start | bytes 1572872 | tf_op jit(solution)/shard_map/ppermute | solution.py:25
  14.5 2.2 %copy-start.1 = (bf16[1,2,256,4096]{3,2,1,0:T(8,128)(2,1)S(1)}, bf16[1,2,256,4096]{3,2,1,0:T(8,128)(2,1)}, u32[]{:S(2)}) copy-start(bf16[1,2,256,4096]{3,2,1,0:T(8,128)(2,1)} %param.10) | copy-start | bytes 12582916
  16.7 1.2 %copy-start.5 = (bf16[512,1024]{1,0:T(8,128)(2,1)S(1)}, bf16[512,1024]{1,0:T(8,128)(2,1)}, u32[]{:S(2)}) copy-start(bf16[512,1024]{1,0:T(8,128)(2,1)} %refs_1_.2) | copy-start | bytes 3145732
  18.0 5.5 %copy-start.2 = (bf16[1,2,4096,256]{3,2,1,0:T(8,128)(2,1)S(1)}, bf16[1,2,4096,256]{3,2,1,0:T(8,128)(2,1)}, u32[]{:S(2)}) copy-start(bf16[1,2,4096,256]{3,2,1,0:T(8,128)(2,1)} %param.11) | copy-start | bytes 12582916
  23.3 15.8 %collective-permute-start.3 = (bf16[256,1024]{1,0:T(8,128)(2,1)S(1)}, bf16[256,1024]{1,0:T(8,128)(2,1)S(1)}, u32[]{:S(2)}, u32[]{:S(2)}) collective-permute-start(bf16[256,1024]{1,0:T(8,128)(2,1)S(1)} %shard_map.95.refs_2_.refs_0_), channel_id=1, source_target_pairs={{0,4},{1,5},{2,6},{3,7},{4,0},{5,1},{6,2},{7,3},{8,12},{9,13},{10,... | collective-permute-start | bytes 1572872 | tf_op jit(solution)/shard_map/ppermute | solution.py:30
  33.8 16.5 %collective-permute-start.2 = (bf16[256,1024]{1,0:T(8,128)(2,1)S(1)}, bf16[256,1024]{1,0:T(8,128)(2,1)S(1)}, u32[]{:S(2)}, u32[]{:S(2)}) collective-permute-start(bf16[256,1024]{1,0:T(8,128)(2,1)S(1)} %shard_map.97.rest_0_.refs_4_.refs_0_.refs_1_), channel_id=1, source_target_pairs={{0,4},{1,5},{2,6},{3,7},{4,0},{5,1},{6,2},{7,3},{8,12},{9,13},{10,... | collective-permute-start | bytes 1572872 | tf_op jit(solution)/shard_map/ppermute | solution.py:30
  34.1 26.1 %collective-permute-start.9 = (bf16[512,1024]{1,0:T(8,128)(2,1)S(1)}, bf16[512,1024]{1,0:T(8,128)(2,1)S(1)}, u32[]{:S(2)}, u32[]{:S(2)}) collective-permute-start(bf16[512,1024]{1,0:T(8,128)(2,1)S(1)} %shard_map.101), channel_id=1, source_target_pairs={{0,24},{8,0},{16,8},{24,16},{1,25},{9,1},{17,9},{25,17},{2,26},{10... | collective-permute-start | bytes 3145736 | tf_op jit(solution)/shard_map/ppermute | solution.py:296
  44.7 29.8 %collective-permute-start.6 = (bf16[256,1024]{1,0:T(8,128)(2,1)S(1)}, bf16[256,1024]{1,0:T(8,128)(2,1)S(1)}, u32[]{:S(2)}, u32[]{:S(2)}) collective-permute-start(bf16[256,1024]{1,0:T(8,128)(2,1)S(1)} %get-tuple-element.26.refs_4_), channel_id=1, source_target_pairs={{0,4},{1,5},{2,6},{3,7},{4,0},{5,1},{6,2},{7,3},{8,12},{9,13},{10,... | collective-permute-start | bytes 1572872 | tf_op jit(solution)/shard_map/ppermute | solution.py:30
  55.9 30.2 %collective-permute-start.5 = (bf16[256,1024]{1,0:T(8,128)(2,1)S(1)}, bf16[256,1024]{1,0:T(8,128)(2,1)S(1)}, u32[]{:S(2)}, u32[]{:S(2)}) collective-permute-start(bf16[256,1024]{1,0:T(8,128)(2,1)S(1)} %get-tuple-element.28.refs_8_), channel_id=1, source_target_pairs={{0,4},{1,5},{2,6},{3,7},{4,0},{5,1},{6,2},{7,3},{8,12},{9,13},{10,... | collective-permute-start | bytes 1572872 | tf_op jit(solution)/shard_map/ppermute | solution.py:30
  70.9 16.1 %collective-permute-start.11 = (bf16[128,1024]{1,0:T(8,128)(2,1)S(1)}, bf16[128,1024]{1,0:T(8,128)(2,1)S(1)}, u32[]{:S(2)}, u32[]{:S(2)}) collective-permute-start(bf16[128,1024]{1,0:T(8,128)(2,1)S(1)} %get-tuple-element.38), channel_id=1, source_target_pairs={{0,4},{1,5},{2,6},{3,7},{4,0},{5,1},{6,2},{7,3},{8,12},{9,13},{10,... | collective-permute-start | bytes 786440 | tf_op jit(solution)/shard_map/ppermute | solution.py:30
  72.5 14.6 %collective-permute-start.12 = (bf16[128,1024]{1,0:T(8,128)(2,1)S(1)}, bf16[128,1024]{1,0:T(8,128)(2,1)S(1)}, u32[]{:S(2)}, u32[]{:S(2)}) collective-permute-start(bf16[128,1024]{1,0:T(8,128)(2,1)S(1)} %get-tuple-element.37), channel_id=1, source_target_pairs={{0,4},{1,5},{2,6},{3,7},{4,0},{5,1},{6,2},{7,3},{8,12},{9,13},{10,... | collective-permute-start | bytes 786440 | tf_op jit(solution)/shard_map/ppermute | solution.py:30
  73.0 18.5 %collective-permute-start.13 = (bf16[128,1024]{1,0:T(8,128)(2,1)S(1)}, bf16[128,1024]{1,0:T(8,128)(2,1)S(1)}, u32[]{:S(2)}, u32[]{:S(2)}) collective-permute-start(bf16[128,1024]{1,0:T(8,128)(2,1)S(1)} %get-tuple-element.36), channel_id=1, source_target_pairs={{0,4},{1,5},{2,6},{3,7},{4,0},{5,1},{6,2},{7,3},{8,12},{9,13},{10,... | collective-permute-start | bytes 786440 | tf_op jit(solution)/shard_map/ppermute | solution.py:30
  74.5 19.9 %collective-permute-start.10 = (bf16[128,1024]{1,0:T(8,128)(2,1)S(1)}, bf16[128,1024]{1,0:T(8,128)(2,1)S(1)}, u32[]{:S(2)}, u32[]{:S(2)}) collective-permute-start(bf16[128,1024]{1,0:T(8,128)(2,1)S(1)} %get-tuple-element.39), channel_id=1, source_target_pairs={{0,4},{1,5},{2,6},{3,7},{4,0},{5,1},{6,2},{7,3},{8,12},{9,13},{10,... | collective-permute-start | bytes 786440 | tf_op jit(solution)/shard_map/ppermute | solution.py:30
  83.1 2.2 %copy-start.3 = (bf16[2,256,4096]{2,1,0:T(8,128)(2,1)S(1)}, bf16[2,256,4096]{2,1,0:T(8,128)(2,1)}, u32[]{:S(2)}) copy-start(bf16[2,256,4096]{2,1,0:T(8,128)(2,1)} %get-tuple-element.32.refs_2_) | copy-start | bytes 12582916
  91.4 1.2 %copy-start = (bf16[512,1024]{1,0:T(8,128)(2,1)S(1)}, bf16[512,1024]{1,0:T(8,128)(2,1)}, u32[]{:S(2)}) copy-start(bf16[512,1024]{1,0:T(8,128)(2,1)} %shard_map.105.refs_4_) | copy-start | bytes 3145732

commit v5 on v4

--- a/solution.py
+++ b/solution.py
@@ -30,11 +30,11 @@
     return lax.ppermute(value, "tensor", pairs)
 
 
-def exchanged(value, mask, sections):
+def exchanged(value, mask, sections, otherwise):
     size = lax.axis_size("tensor")
     pairs = []
     for s in range(lax.axis_size("section")):
-        distance = mask if s in sections else 1
+        distance = mask if s in sections else otherwise
         pairs += [(s * size + t, s * size + (t ^ distance)) for t in range(size)]
     return lax.ppermute(value, ("section", "tensor"), pairs)
 
@@ -277,12 +277,12 @@
     mask = lax.axis_size("tensor") >> levels
     factors, width, hidden_local = up.shape
     tokens, columns = acts_prev.shape
-    half, quarter = tokens // 2, tokens // 4
+    half = tokens // 2
     sections = lax.axis_size("section")
     first, last = 0, sections - 1
 
-    crossed_g = exchanged(grads_next, mask, range(1, sections))
-    crossed_loss = exchanged(loss_grad, mask, range(1))
+    crossed_g = exchanged(grads_next, mask, range(1, sections), 2)
+    crossed_loss = exchanged(loss_grad, mask, range(1), 1)
     acts_a, acts_b = join([[(0, 0, half)], [(0, half, tokens - half)]], (acts_prev,), ())
     came_a = shifted(acts_a, 1)
     came_b = shifted(acts_b, 1)
@@ -329,8 +329,9 @@
         COST_BACK,
         (sent_b,),
     )
+    ends = [tokens * i // 32 for i in (11, 22, 30, 32)]
     arrived_back = [
-        swapped(sent_back[i * quarter : (i + 1) * quarter], mask) for i in range(4)
+        swapped(sent_back[at:end], mask) for at, end in zip([0] + ends[:-1], ends)
     ]
     up_grad, down_grad = run(
         weight_kernel,
@@ -342,9 +343,10 @@
     )
     mixed = finish(base_a, [arrived_a], 0, tokens, None, (up_grad,))
     mixed = finish(base_b, [arrived_b], half, tokens, mixed)
-    end = 3 * quarter
-    input_grads = finish(base_back[:end], arrived_back[:3], 0, tokens, None, (mixed,))
-    input_grads = finish(base_back[end:], arrived_back[3:], end, tokens, input_grads)
+    input_grads = finish(base_back[: ends[1]], arrived_back[:2], 0, tokens, None, (mixed,))
+    for i in range(2, len(ends)):
+        start, end = ends[i - 1], ends[i]
+        input_grads = finish(base_back[start:end], arrived_back[i : i + 1], start, tokens, input_grads)
     return (mixed, input_grads, up_grad[None], down_grad[None])
 
 

time: 95.6 us -> 95.5 us (level)
  starting transfers between devices: 26.1 us -> 25 us
    ppermute x3, starting transfers between devices: 9.55 us -> 8.06 us  [shifted(): return lax.ppermute(value, 'section', pairs)]
    ppermute x2, starting transfers between devices: 3.03 us -> 4.52 us  [exchanged(): return lax.ppermute(value, ('section', 'tensor'), pairs)]
    pallas_call x4 -> x5, Pallas kernels: 3.58 us -> 4.2 us  [finish(): pl.pallas_call(kernel, in_specs=[vmem] * (1 + len(pieces)) + [anywhere] *...]
  transfers between devices with their start and end apart: 14 -> 14, of which waited for: 7 -> 7; matrix products, arithmetic and copies ran while one was open for 0% -> 0% of each run, Pallas kernels for 35% -> 36%
where the time goes in v5:
time: 95.5 us; the launch traced here: 95.2 us
  Pallas kernels  35 us (37%)
  waiting for transfers between devices  26 us (27%)
  starting transfers between devices  25 us (26%)
  local copies, waits for them, and re-layouts  8.32 us (9%)
    pallas_call x3, Pallas kernels, in_vmem(): pl.pallas_call(lambda *refs: kernel([len(group) for group in rows], *refs...  21.9 us
    ppermute x3, waiting for transfers between devices, shifted(): return lax.ppermute(value, 'section', pairs)  14.6 us
    ppermute x8, waiting for transfers between devices, swapped(): return lax.ppermute(value, 'tensor', pairs)  9.3 us
    ppermute x8, starting transfers between devices, swapped(): return lax.ppermute(value, 'tensor', pairs)  8.28 us
    ppermute x3, starting transfers between devices, shifted(): return lax.ppermute(value, 'section', pairs)  8.06 us
    unnamed x14, local copies, waits for them, and re-layouts  8.04 us
    pallas_call x1, Pallas kernels, run(): pl.pallas_call(lambda *refs: kernel([len(group) for group in rows], expan...  7.8 us
    ppermute x2, starting transfers between devices, exchanged(): return lax.ppermute(value, ('section', 'tensor'), pairs)  4.52 us
  transfers between devices with their start and end apart: 14, of which 7 were waited for; matrix products, arithmetic and copies ran while one was open for 0% of the time, Pallas kernels for 36%

profile of v5, /device:TPU:0, one launch (start us, length us, event | category | flops | bytes accessed | tf_op | source)
XLA Modules:
  0.0 95.2 jit_solution(1612401387219088209)
XLA Ops:
  0.6 3.0 %collective-permute-start.7 = (bf16[512,1024]{1,0:T(8,128)(2,1)}, bf16[512,1024]{1,0:T(8,128)(2,1)S(1)}, u32[]{:S(2)}, u32[]{:S(2)}) collective-permute-start(bf16[512,1024]{1,0:T(8,128)(2,1)} %refs_1_.3), channel_id=1, source_target_pairs={{0,4},{1,5},{2,6},{3,7},{4,0},{5,1},{6,2},{7,3},{8,9},{9,8},{10,11... | collective-permute-start | bytes 3145736 | tf_op jit(solution)/shard_map/ppermute | solution.py:39
  3.7 1.5 %collective-permute-start.8 = (bf16[512,1024]{1,0:T(8,128)(2,1)}, bf16[512,1024]{1,0:T(8,128)(2,1)S(1)}, u32[]{:S(2)}, u32[]{:S(2)}) collective-permute-start(bf16[512,1024]{1,0:T(8,128)(2,1)} %param.8), channel_id=1, source_target_pairs={{0,2},{1,3},{2,0},{3,1},{4,6},{5,7},{6,4},{7,5},{8,12},{9,13},{10,... | collective-permute-start | bytes 3145736 | tf_op jit(solution)/shard_map/ppermute | solution.py:39
  5.2 1.3 %collective-permute-start.4 = (bf16[512,1024]{1,0:T(8,128)(2,1)}, bf16[512,1024]{1,0:T(8,128)(2,1)S(1)}, u32[]{:S(2)}, u32[]{:S(2)}) collective-permute-start(bf16[512,1024]{1,0:T(8,128)(2,1)} %param.8), channel_id=1, source_target_pairs={{8,0},{16,8},{24,16},{9,1},{17,9},{25,17},{10,2},{18,10},{26,18},{... | collective-permute-start | bytes 3145736 | tf_op jit(solution)/shard_map/ppermute | solution.py:25
  6.5 1.2 %copy-done.4 = bf16[512,1024]{1,0:T(8,128)(2,1)S(1)} copy-done((bf16[512,1024]{1,0:T(8,128)(2,1)S(1)}, bf16[512,1024]{1,0:T(8,128)(2,1)}, u32[]{:S(2)}) %copy-start.4) | copy-done | bytes 1048600
  7.7 0.1 shard_map.93
  7.7 4.7 %collective-permute-start.1 = (bf16[256,1024]{1,0:T(8,128)(2,1)S(1)}, bf16[256,1024]{1,0:T(8,128)(2,1)S(1)}, u32[]{:S(2)}, u32[]{:S(2)}) collective-permute-start(bf16[256,1024]{1,0:T(8,128)(2,1)S(1)} %get-tuple-element.20.refs_2_), channel_id=1, source_target_pairs={{0,8},{8,16},{16,24},{1,9},{9,17},{17,25},{2,10},{10,18},{18,26},{... | collective-permute-start | bytes 1572872 | tf_op jit(solution)/shard_map/ppermute | solution.py:25
  12.5 2.1 %collective-permute-start = (bf16[256,1024]{1,0:T(8,128)(2,1)S(1)}, bf16[256,1024]{1,0:T(8,128)(2,1)S(1)}, u32[]{:S(2)}, u32[]{:S(2)}) collective-permute-start(bf16[256,1024]{1,0:T(8,128)(2,1)S(1)} %get-tuple-element.22), channel_id=1, source_target_pairs={{0,8},{8,16},{16,24},{1,9},{9,17},{17,25},{2,10},{10,18},{18,26},{... | collective-permute-start | bytes 1572872 | tf_op jit(solution)/shard_map/ppermute | solution.py:25
  14.5 0.0 copy-start.1
  14.6 2.2 %copy-done.1 = bf16[1,2,256,4096]{3,2,1,0:T(8,128)(2,1)S(1)} copy-done((bf16[1,2,256,4096]{3,2,1,0:T(8,128)(2,1)S(1)}, bf16[1,2,256,4096]{3,2,1,0:T(8,128)(2,1)}, u32[]{:S(2)}) %copy-start.1) | copy-done | bytes 4194328
  16.7 1.2 %copy-done.5 = bf16[512,1024]{1,0:T(8,128)(2,1)S(1)} copy-done((bf16[512,1024]{1,0:T(8,128)(2,1)S(1)}, bf16[512,1024]{1,0:T(8,128)(2,1)}, u32[]{:S(2)}) %copy-start.5) | copy-done | bytes 1048600
  18.0 0.4 shard_map.94
  18.3 6.5 %collective-permute-done.1.b = bf16[256,1024]{1,0:T(8,128)(2,1)S(1)} collective-permute-done((bf16[256,1024]{1,0:T(8,128)(2,1)S(1)}, bf16[256,1024]{1,0:T(8,128)(2,1)S(1)}, u32[]{:S(2)}, u32[]{:S(2)}) %collective-permute-start.1) | collective-permute-done | bytes 524320 | tf_op jit(solution)/shard_map/ppermute | solution.py:25
  24.8 0.1 shard_map.95.refs_2_.refs_0_
  24.9 0.6 collective-permute-start.3
  25.4 0.4 shard_map.96
  25.8 8.2 %collective-permute-done.b = bf16[256,1024]{1,0:T(8,128)(2,1)S(1)} collective-permute-done((bf16[256,1024]{1,0:T(8,128)(2,1)S(1)}, bf16[256,1024]{1,0:T(8,128)(2,1)S(1)}, u32[]{:S(2)}, u32[]{:S(2)}) %collective-permute-start) | collective-permute-done | bytes 524320 | tf_op jit(solution)/shard_map/ppermute | solution.py:25
  34.0 0.1 shard_map.97.rest_0_.refs_4_.refs_0_.refs_1_
  34.0 0.6 collective-permute-start.2
  34.6 0.0 collective-permute-done.7.a
  34.6 0.1 shard_map.101
  34.7 4.1 %collective-permute-start.9 = (bf16[512,1024]{1,0:T(8,128)(2,1)S(1)}, bf16[512,1024]{1,0:T(8,128)(2,1)S(1)}, u32[]{:S(2)}, u32[]{:S(2)}) collective-permute-start(bf16[512,1024]{1,0:T(8,128)(2,1)S(1)} %shard_map.101), channel_id=1, source_target_pairs={{0,24},{8,0},{16,8},{24,16},{1,25},{9,1},{17,9},{25,17},{2,26},{10... | collective-permute-start | bytes 3145736 | tf_op jit(solution)/shard_map/ppermute | solution.py:296
  38.8 0.0 collective-permute-done.4.b
  38.8 0.1 shard_map.98.refs_5_.refs_4_
  39.0 0.8 collective-permute-done.3.refs_1_.refs_2_
  39.8 5.6 %shard_map.99 = (f32[256,1024]{1,0:T(8,128)S(1)}, bf16[256,1024]{1,0:T(8,128)(2,1)S(1)}) custom-call(bf16[256,1024]{1,0:T(8,128)(2,1)S(1)} %shard_map.95.refs_2_.refs_0_, bf16[256,1024]{1,0:T(8,128)(2,1)S(1)} %collective-permute-done.3.refs_1_.refs_2_, bf16[2,256,4096]{2,1,0:T(8,128)(2,1)S(1)} %get-tuple-element.24.refs_2_.refs_6_, ...), custom_call_target="tpu_custom_call" | custom-call | flops 3000000000 | tf_op jit(solution)/shard_map/pallas_call | solution.py:174
  45.4 1.4 %collective-permute-start.6 = (bf16[256,1024]{1,0:T(8,128)(2,1)S(1)}, bf16[256,1024]{1,0:T(8,128)(2,1)S(1)}, u32[]{:S(2)}, u32[]{:S(2)}) collective-permute-start(bf16[256,1024]{1,0:T(8,128)(2,1)S(1)} %get-tuple-element.26.refs_4_), channel_id=1, source_target_pairs={{0,4},{1,5},{2,6},{3,7},{4,0},{5,1},{6,2},{7,3},{8,12},{9,13},{10,... | collective-permute-start | bytes 1572872 | tf_op jit(solution)/shard_map/ppermute | solution.py:30
  46.8 4.2 %collective-permute-done.2.refs_1_.refs_3_ = bf16[256,1024]{1,0:T(8,128)(2,1)S(1)} collective-permute-done((bf16[256,1024]{1,0:T(8,128)(2,1)S(1)}, bf16[256,1024]{1,0:T(8,128)(2,1)S(1)}, u32[]{:S(2)}, u32[]{:S(2)}) %collective-permute-start.2) | collective-permute-done | bytes 524320 | tf_op jit(solution)/shard_map/ppermute | solution.py:30
  51.0 5.6 %shard_map.100 = (f32[256,1024]{1,0:T(8,128)S(1)}, bf16[256,1024]{1,0:T(8,128)(2,1)S(1)}) custom-call(bf16[256,1024]{1,0:T(8,128)(2,1)S(1)} %shard_map.97.rest_0_.refs_4_.refs_0_.refs_1_, bf16[256,1024]{1,0:T(8,128)(2,1)S(1)} %collective-permute-done.2.refs_1_.refs_3_, bf16[2,256,4096]{2,1,0:T(8,128)(2,1)S(1)} %get-tuple-element.24.refs_2_.refs_6_, ...), custom_call_target="tpu_custom_call" | custom-call | flops 7000000000 | tf_op jit(solution)/shard_map/pallas_call | solution.py:174
  56.6 1.4 %collective-permute-start.5 = (bf16[256,1024]{1,0:T(8,128)(2,1)S(1)}, bf16[256,1024]{1,0:T(8,128)(2,1)S(1)}, u32[]{:S(2)}, u32[]{:S(2)}) collective-permute-start(bf16[256,1024]{1,0:T(8,128)(2,1)S(1)} %get-tuple-element.28.refs_8_), channel_id=1, source_target_pairs={{0,4},{1,5},{2,6},{3,7},{4,0},{5,1},{6,2},{7,3},{8,12},{9,13},{10,... | collective-permute-start | bytes 1572872 | tf_op jit(solution)/shard_map/ppermute | solution.py:30
  58.1 2.1 %collective-permute-done.9.refs_5_ = bf16[512,1024]{1,0:T(8,128)(2,1)S(1)} collective-permute-done((bf16[512,1024]{1,0:T(8,128)(2,1)S(1)}, bf16[512,1024]{1,0:T(8,128)(2,1)S(1)}, u32[]{:S(2)}, u32[]{:S(2)}) %collective-permute-start.9) | collective-permute-done | bytes 1048608 | tf_op jit(solution)/shard_map/ppermute | solution.py:296
  60.2 10.7 %shard_map.102 = (f32[512,1024]{1,0:T(8,128)S(1)}, bf16[512,1024]{1,0:T(8,128)(2,1)S(1)}, bf16[512,4096]{1,0:T(8,128)(2,1)S(1)}, bf16[512,4096]{1,0:T(8,128)(2,1)S(1)}) custom-call(bf16[256,1024]{1,0:T(8,128)(2,1)S(1)} %shard_map.95.refs_2_.refs_0_, bf16[256,1024]{1,0:T(8,128)(2,1)S(1)} %shard_map.97.rest_0_.refs_4_.refs_0_.refs_1_, ...), custom_call_target="tpu_custom_call" | custom-call | flops 6000000000 | tf_op jit(solution)/shard_map/pallas_call | solution.py:174
  70.9 1.6 %collective-permute-start.12 = (bf16[176,1024]{1,0:T(8,128)(2,1)S(1)}, bf16[176,1024]{1,0:T(8,128)(2,1)S(1)}, u32[]{:S(2)}, u32[]{:S(2)}) collective-permute-start(bf16[176,1024]{1,0:T(8,128)(2,1)S(1)} %get-tuple-element.37), channel_id=1, source_target_pairs={{0,4},{1,5},{2,6},{3,7},{4,0},{5,1},{6,2},{7,3},{8,12},{9,13},{10,... | collective-permute-start | bytes 1081352 | tf_op jit(solution)/shard_map/ppermute | solution.py:30
  72.5 0.5 collective-permute-start.13
  73.0 1.6 %collective-permute-start.11 = (bf16[128,1024]{1,0:T(8,128)(2,1)S(1)}, bf16[128,1024]{1,0:T(8,128)(2,1)S(1)}, u32[]{:S(2)}, u32[]{:S(2)}) collective-permute-start(bf16[128,1024]{1,0:T(8,128)(2,1)S(1)} %slice.24), channel_id=1, source_target_pairs={{0,4},{1,5},{2,6},{3,7},{4,0},{5,1},{6,2},{7,3},{8,12},{9,13},{10,... | collective-permute-start | bytes 786440 | tf_op jit(solution)/shard_map/ppermute | solution.py:30
  74.6 0.0 collective-permute-done.6.refs_1_
  74.6 0.6 collective-permute-start.10
  75.2 0.2 slice.25.refs_0_
  75.4 7.8 %shard_map.103 = (bf16[2,256,4096]{2,1,0:T(8,128)(2,1)}, bf16[2,4096,256]{2,1,0:T(8,128)(2,1)}) custom-call(bf16[256,1024]{1,0:T(8,128)(2,1)S(1)} %shard_map.95.refs_2_.refs_0_, bf16[256,1024]{1,0:T(8,128)(2,1)S(1)} %shard_map.97.rest_0_.refs_4_.refs_0_.refs_1_, bf16[256,1024]{1,0:T(8,128)(2,1)S(1)} %collective-permute-done.3.refs_1_.refs_2_, ...), custom_call_target="tpu_custom_call" | custom-call | bytes 8388608 | tf_op jit(solution)/shard_map/pallas_call | solution.py:237
  83.2 2.2 %copy-done.3 = bf16[2,256,4096]{2,1,0:T(8,128)(2,1)S(1)} copy-done((bf16[2,256,4096]{2,1,0:T(8,128)(2,1)S(1)}, bf16[2,256,4096]{2,1,0:T(8,128)(2,1)}, u32[]{:S(2)}) %copy-start.3) | copy-done | bytes 4194328
  85.4 0.9 shard_map.104.refs_2_
  86.3 0.9 shard_map.105.refs_3_
  87.2 2.8 %collective-permute-done.13.refs_2_ = bf16[176,1024]{1,0:T(8,128)(2,1)S(1)} collective-permute-done((bf16[176,1024]{1,0:T(8,128)(2,1)S(1)}, bf16[176,1024]{1,0:T(8,128)(2,1)S(1)}, u32[]{:S(2)}, u32[]{:S(2)}) %collective-permute-start.13) | collective-permute-done | bytes 360480 | tf_op jit(solution)/shard_map/ppermute | solution.py:30
  90.0 1.2 %copy-done = bf16[512,1024]{1,0:T(8,128)(2,1)S(1)} copy-done((bf16[512,1024]{1,0:T(8,128)(2,1)S(1)}, bf16[512,1024]{1,0:T(8,128)(2,1)}, u32[]{:S(2)}) %copy-start) | copy-done | bytes 1048600
  91.2 1.0 %shard_map.106.refs_2_ = bf16[512,1024]{1,0:T(8,128)(2,1)} custom-call(f32[352,1024]{1,0:T(8,128)S(1)} %slice.25.refs_0_, bf16[176,1024]{1,0:T(8,128)(2,1)S(1)} %collective-permute-done.12.refs_1_, bf16[176,1024]{1,0:T(8,128)(2,1)S(1)} %collective-permute-done.13.refs_2_, bf16[512,1024]{1,0:T(8,128)(2,1)S(1)} %copy-done), custom_call_target="tpu_custom_call" | custom-call | tf_op jit(solution)/shard_map/pallas_call | solution.py:262
  92.3 1.5 %collective-permute-done.11.refs_1_ = bf16[128,1024]{1,0:T(8,128)(2,1)S(1)} collective-permute-done((bf16[128,1024]{1,0:T(8,128)(2,1)S(1)}, bf16[128,1024]{1,0:T(8,128)(2,1)S(1)}, u32[]{:S(2)}, u32[]{:S(2)}) %collective-permute-start.11) | collective-permute-done | bytes 262176 | tf_op jit(solution)/shard_map/ppermute | solution.py:30
  93.7 0.8 shard_map.107.refs_2_
  94.5 0.0 collective-permute-done.10.refs_1_
  94.5 0.7 shard_map.108
  (16 shorter events, 0.1 us)
Async XLA Ops:
  0.6 34.0 %collective-permute-start.7 = (bf16[512,1024]{1,0:T(8,128)(2,1)}, bf16[512,1024]{1,0:T(8,128)(2,1)S(1)}, u32[]{:S(2)}, u32[]{:S(2)}) collective-permute-start(bf16[512,1024]{1,0:T(8,128)(2,1)} %refs_1_.3), channel_id=1, source_target_pairs={{0,4},{1,5},{2,6},{3,7},{4,0},{5,1},{6,2},{7,3},{8,9},{9,8},{10,11... | collective-permute-start | bytes 3145736 | tf_op jit(solution)/shard_map/ppermute | solution.py:39
  3.7 31.0 %collective-permute-start.8 = (bf16[512,1024]{1,0:T(8,128)(2,1)}, bf16[512,1024]{1,0:T(8,128)(2,1)S(1)}, u32[]{:S(2)}, u32[]{:S(2)}) collective-permute-start(bf16[512,1024]{1,0:T(8,128)(2,1)} %param.8), channel_id=1, source_target_pairs={{0,2},{1,3},{2,0},{3,1},{4,6},{5,7},{6,4},{7,5},{8,12},{9,13},{10,... | collective-permute-start | bytes 3145736 | tf_op jit(solution)/shard_map/ppermute | solution.py:39
  5.2 33.7 %collective-permute-start.4 = (bf16[512,1024]{1,0:T(8,128)(2,1)}, bf16[512,1024]{1,0:T(8,128)(2,1)S(1)}, u32[]{:S(2)}, u32[]{:S(2)}) collective-permute-start(bf16[512,1024]{1,0:T(8,128)(2,1)} %param.8), channel_id=1, source_target_pairs={{8,0},{16,8},{24,16},{9,1},{17,9},{25,17},{10,2},{18,10},{26,18},{... | collective-permute-start | bytes 3145736 | tf_op jit(solution)/shard_map/ppermute | solution.py:25
  6.4 1.2 %copy-start.4 = (bf16[512,1024]{1,0:T(8,128)(2,1)S(1)}, bf16[512,1024]{1,0:T(8,128)(2,1)}, u32[]{:S(2)}) copy-start(bf16[512,1024]{1,0:T(8,128)(2,1)} %refs_0_.1) | copy-start | bytes 3145732
  7.7 17.8 %copy-start.6 = (bf16[512,1024]{1,0:T(8,128)(2,1)S(1)}, bf16[512,1024]{1,0:T(8,128)(2,1)}, u32[]{:S(2)}) copy-start(bf16[512,1024]{1,0:T(8,128)(2,1)} %refs_1_.3) | copy-start | bytes 3145732
  7.7 17.1 %collective-permute-start.1 = (bf16[256,1024]{1,0:T(8,128)(2,1)S(1)}, bf16[256,1024]{1,0:T(8,128)(2,1)S(1)}, u32[]{:S(2)}, u32[]{:S(2)}) collective-permute-start(bf16[256,1024]{1,0:T(8,128)(2,1)S(1)} %get-tuple-element.20.refs_2_), channel_id=1, source_target_pairs={{0,8},{8,16},{16,24},{1,9},{9,17},{17,25},{2,10},{10,18},{18,26},{... | collective-permute-start | bytes 1572872 | tf_op jit(solution)/shard_map/ppermute | solution.py:25
  12.5 21.5 %collective-permute-start = (bf16[256,1024]{1,0:T(8,128)(2,1)S(1)}, bf16[256,1024]{1,0:T(8,128)(2,1)S(1)}, u32[]{:S(2)}, u32[]{:S(2)}) collective-permute-start(bf16[256,1024]{1,0:T(8,128)(2,1)S(1)} %get-tuple-element.22), channel_id=1, source_target_pairs={{0,8},{8,16},{16,24},{1,9},{9,17},{17,25},{2,10},{10,18},{18,26},{... | collective-permute-start | bytes 1572872 | tf_op jit(solution)/shard_map/ppermute | solution.py:25
  14.5 2.2 %copy-start.1 = (bf16[1,2,256,4096]{3,2,1,0:T(8,128)(2,1)S(1)}, bf16[1,2,256,4096]{3,2,1,0:T(8,128)(2,1)}, u32[]{:S(2)}) copy-start(bf16[1,2,256,4096]{3,2,1,0:T(8,128)(2,1)} %param.10) | copy-start | bytes 12582916
  16.7 1.2 %copy-start.5 = (bf16[512,1024]{1,0:T(8,128)(2,1)S(1)}, bf16[512,1024]{1,0:T(8,128)(2,1)}, u32[]{:S(2)}) copy-start(bf16[512,1024]{1,0:T(8,128)(2,1)} %refs_1_.2) | copy-start | bytes 3145732
  18.0 7.5 %copy-start.2 = (bf16[1,2,4096,256]{3,2,1,0:T(8,128)(2,1)S(1)}, bf16[1,2,4096,256]{3,2,1,0:T(8,128)(2,1)}, u32[]{:S(2)}) copy-start(bf16[1,2,4096,256]{3,2,1,0:T(8,128)(2,1)} %param.11) | copy-start | bytes 12582916
  24.9 14.9 %collective-permute-start.3 = (bf16[256,1024]{1,0:T(8,128)(2,1)S(1)}, bf16[256,1024]{1,0:T(8,128)(2,1)S(1)}, u32[]{:S(2)}, u32[]{:S(2)}) collective-permute-start(bf16[256,1024]{1,0:T(8,128)(2,1)S(1)} %shard_map.95.refs_2_.refs_0_), channel_id=1, source_target_pairs={{0,4},{1,5},{2,6},{3,7},{4,0},{5,1},{6,2},{7,3},{8,12},{9,13},{10,... | collective-permute-start | bytes 1572872 | tf_op jit(solution)/shard_map/ppermute | solution.py:30
  34.0 17.0 %collective-permute-start.2 = (bf16[256,1024]{1,0:T(8,128)(2,1)S(1)}, bf16[256,1024]{1,0:T(8,128)(2,1)S(1)}, u32[]{:S(2)}, u32[]{:S(2)}) collective-permute-start(bf16[256,1024]{1,0:T(8,128)(2,1)S(1)} %shard_map.97.rest_0_.refs_4_.refs_0_.refs_1_), channel_id=1, source_target_pairs={{0,4},{1,5},{2,6},{3,7},{4,0},{5,1},{6,2},{7,3},{8,12},{9,13},{10,... | collective-permute-start | bytes 1572872 | tf_op jit(solution)/shard_map/ppermute | solution.py:30
  34.7 25.4 %collective-permute-start.9 = (bf16[512,1024]{1,0:T(8,128)(2,1)S(1)}, bf16[512,1024]{1,0:T(8,128)(2,1)S(1)}, u32[]{:S(2)}, u32[]{:S(2)}) collective-permute-start(bf16[512,1024]{1,0:T(8,128)(2,1)S(1)} %shard_map.101), channel_id=1, source_target_pairs={{0,24},{8,0},{16,8},{24,16},{1,25},{9,1},{17,9},{25,17},{2,26},{10... | collective-permute-start | bytes 3145736 | tf_op jit(solution)/shard_map/ppermute | solution.py:296
  45.4 29.2 %collective-permute-start.6 = (bf16[256,1024]{1,0:T(8,128)(2,1)S(1)}, bf16[256,1024]{1,0:T(8,128)(2,1)S(1)}, u32[]{:S(2)}, u32[]{:S(2)}) collective-permute-start(bf16[256,1024]{1,0:T(8,128)(2,1)S(1)} %get-tuple-element.26.refs_4_), channel_id=1, source_target_pairs={{0,4},{1,5},{2,6},{3,7},{4,0},{5,1},{6,2},{7,3},{8,12},{9,13},{10,... | collective-permute-start | bytes 1572872 | tf_op jit(solution)/shard_map/ppermute | solution.py:30
  56.6 29.6 %collective-permute-start.5 = (bf16[256,1024]{1,0:T(8,128)(2,1)S(1)}, bf16[256,1024]{1,0:T(8,128)(2,1)S(1)}, u32[]{:S(2)}, u32[]{:S(2)}) collective-permute-start(bf16[256,1024]{1,0:T(8,128)(2,1)S(1)} %get-tuple-element.28.refs_8_), channel_id=1, source_target_pairs={{0,4},{1,5},{2,6},{3,7},{4,0},{5,1},{6,2},{7,3},{8,12},{9,13},{10,... | collective-permute-start | bytes 1572872 | tf_op jit(solution)/shard_map/ppermute | solution.py:30
  70.9 16.3 %collective-permute-start.12 = (bf16[176,1024]{1,0:T(8,128)(2,1)S(1)}, bf16[176,1024]{1,0:T(8,128)(2,1)S(1)}, u32[]{:S(2)}, u32[]{:S(2)}) collective-permute-start(bf16[176,1024]{1,0:T(8,128)(2,1)S(1)} %get-tuple-element.37), channel_id=1, source_target_pairs={{0,4},{1,5},{2,6},{3,7},{4,0},{5,1},{6,2},{7,3},{8,12},{9,13},{10,... | collective-permute-start | bytes 1081352 | tf_op jit(solution)/shard_map/ppermute | solution.py:30
  72.5 17.6 %collective-permute-start.13 = (bf16[176,1024]{1,0:T(8,128)(2,1)S(1)}, bf16[176,1024]{1,0:T(8,128)(2,1)S(1)}, u32[]{:S(2)}, u32[]{:S(2)}) collective-permute-start(bf16[176,1024]{1,0:T(8,128)(2,1)S(1)} %get-tuple-element.36), channel_id=1, source_target_pairs={{0,4},{1,5},{2,6},{3,7},{4,0},{5,1},{6,2},{7,3},{8,12},{9,13},{10,... | collective-permute-start | bytes 1081352 | tf_op jit(solution)/shard_map/ppermute | solution.py:30
  73.0 20.7 %collective-permute-start.11 = (bf16[128,1024]{1,0:T(8,128)(2,1)S(1)}, bf16[128,1024]{1,0:T(8,128)(2,1)S(1)}, u32[]{:S(2)}, u32[]{:S(2)}) collective-permute-start(bf16[128,1024]{1,0:T(8,128)(2,1)S(1)} %slice.24), channel_id=1, source_target_pairs={{0,4},{1,5},{2,6},{3,7},{4,0},{5,1},{6,2},{7,3},{8,12},{9,13},{10,... | collective-permute-start | bytes 786440 | tf_op jit(solution)/shard_map/ppermute | solution.py:30
  74.6 19.9 %collective-permute-start.10 = (bf16[32,1024]{1,0:T(8,128)(2,1)S(1)}, bf16[32,1024]{1,0:T(8,128)(2,1)S(1)}, u32[]{:S(2)}, u32[]{:S(2)}) collective-permute-start(bf16[32,1024]{1,0:T(8,128)(2,1)S(1)} %slice.22), channel_id=1, source_target_pairs={{0,4},{1,5},{2,6},{3,7},{4,0},{5,1},{6,2},{7,3},{8,12},{9,13},{10,... | collective-permute-start | bytes 196616 | tf_op jit(solution)/shard_map/ppermute | solution.py:30
  83.2 2.2 %copy-start.3 = (bf16[2,256,4096]{2,1,0:T(8,128)(2,1)S(1)}, bf16[2,256,4096]{2,1,0:T(8,128)(2,1)}, u32[]{:S(2)}) copy-start(bf16[2,256,4096]{2,1,0:T(8,128)(2,1)} %get-tuple-element.32.refs_2_) | copy-start | bytes 12582916
  90.0 1.2 %copy-start = (bf16[512,1024]{1,0:T(8,128)(2,1)S(1)}, bf16[512,1024]{1,0:T(8,128)(2,1)}, u32[]{:S(2)}) copy-start(bf16[512,1024]{1,0:T(8,128)(2,1)} %shard_map.105.refs_3_) | copy-start | bytes 3145732
